TPU v7x, 32 devices: a whole 2x2x4 slice. The times are simulated.
32 devices in a mesh: ep: 16 (over z, x, core), tp: 2 (over y).
Axes of the slice: x: 2, y: 2, z: 4, core: 2. Of those that a mesh axis runs over, the one named last changes fastest.
Arguments:
- attn_out: bfloat16 [2048, 2048], P('ep', 'tp'), may hold values from -6 to 6
- resid: bfloat16 [2048, 2048], P(('ep', 'tp')), may hold values from -6 to 6
- norm_gain: float32 [2048], replicated, may hold values from 0.1 to 1.9
- expert_ids: int32 [2048, 6], P('ep'), may hold values from 0 to 15, all different within a row; in each aligned block of 128 rows (0 to 127, 128 to 255, ...) at most 64 rows name the same one
- gate_vals: float32 [2048, 6], P('ep'), may hold values from 0.1 to 1
- w_gate: bfloat16 [16, 1408, 2048], P('ep', 'tp'), may hold values from -0.125 to 0.125
- w_up: bfloat16 [16, 1408, 2048], P('ep', 'tp'), may hold values from -0.125 to 0.125
- w_down: bfloat16 [16, 1408, 2048], P('ep', 'tp'), may hold values from -0.15625 to 0.15625
Outputs:
- layer_out: bfloat16 [2048, 2048], P(('ep', 'tp'))
Inputs may be any that keep to these rules, and one draw needn't show every extreme that they name: `expert_ids`: among the tokens of one index of ep (aligned blocks of 128 rows), no expert is chosen by more than 64 tokens; some expert reaches 64 in some blocks. The experts of one token differ.
All inputs are finite; a program needn't handle non-finite values.
Results may differ from a plain program's by a relative error of at most 0.0095.
Values may be sent and summed in bfloat16 or wider, within the bound.
No kernel may reach another device: no remote copies, remote signals or barrier semaphores. Data moves between devices by JAX's collectives and lax.ppermute only.
A program may use at most 64 MiB of HBM per device.

v0:
```python
import jax
import jax.numpy as jnp
from jax import lax
from jax.sharding import PartitionSpec as P


def by_feature(rows, weight):
    return lax.dot_general(
        rows, weight, (((1,), (1,)), ((), ())), preferred_element_type=jnp.float32
    )


def group_total(partial_rows):
    summed = lax.psum_scatter(
        partial_rows.astype(jnp.float32).astype(jnp.bfloat16), "tp", scatter_dimension=1, tiled=True
    )
    return summed


def all_shares(share_rows):
    return lax.all_gather(share_rows, "tp", axis=1, tiled=True)


def per_device(attn_out, resid, norm_gain, expert_ids, gate_vals, w_gate, w_up, w_down):
    tp_count = lax.axis_size("tp")
    ep_count = lax.axis_size("ep")
    seq_rows = lax.all_to_all(attn_out, "tp", split_axis=0, concat_axis=1, tiled=True)
    hidden_state = (resid.astype(jnp.float32) + seq_rows.astype(jnp.float32)).astype(jnp.bfloat16)
    hidden_f32 = hidden_state.astype(jnp.float32)
    mean_sq = jnp.mean(hidden_f32 * hidden_f32, axis=-1, keepdims=True)
    normed = (hidden_f32 * lax.rsqrt(mean_sq + 1e-05) * norm_gain).astype(jnp.bfloat16)
    normed_all = lax.all_gather(normed, "tp", axis=0, tiled=True)
    tok_block = normed_all.shape[0]
    width = normed_all.shape[1]
    choose_count = expert_ids.shape[1]
    capacity = 4 * tok_block * choose_count // (3 * ep_count)
    flat_ids = expert_ids.reshape(-1)
    onehot = (flat_ids[:, None] == jnp.arange(ep_count, dtype=jnp.int32)[None, :]).astype(jnp.int32)
    rank_in = jnp.sum(onehot * (jnp.cumsum(onehot, axis=0) - onehot), axis=1)
    slot_index = (flat_ids * capacity + rank_in).reshape(tok_block, choose_count)
    slot_range = jnp.arange(ep_count * capacity, dtype=jnp.int32)
    placing = jnp.any(slot_index[None, :, :] == slot_range[:, None, None], axis=-1).astype(
        jnp.bfloat16
    )
    send_rows = jnp.dot(placing, normed_all, preferred_element_type=jnp.float32).astype(
        jnp.bfloat16
    )
    send_rows = send_rows.reshape(ep_count, capacity, width)
    received = lax.all_to_all(send_rows, "ep", split_axis=0, concat_axis=0, tiled=True)
    flat_rows = received.reshape(-1, width)
    gate_pre = by_feature(flat_rows, w_gate[0])
    up_pre = by_feature(flat_rows, w_up[0])
    act = (jax.nn.silu(gate_pre) * up_pre).astype(jnp.bfloat16)
    out_rows = jnp.dot(act, w_down[0], preferred_element_type=jnp.float32).astype(jnp.bfloat16)
    expert_rows = out_rows.reshape(received.shape[0], received.shape[1], width)
    back_rows = lax.all_to_all(expert_rows, "ep", split_axis=0, concat_axis=0, tiled=True)
    slot_rows = all_shares(group_total(back_rows))
    my_rows = tok_block // tp_count
    my_slots = lax.dynamic_slice_in_dim(slot_index, lax.axis_index("tp") * my_rows, my_rows, 0)
    my_gates = lax.dynamic_slice_in_dim(gate_vals, lax.axis_index("tp") * my_rows, my_rows, 0)
    picked = slot_rows.reshape(ep_count * capacity, width)[my_slots]
    moe_rows = jnp.sum(my_gates[:, :, None] * picked.astype(jnp.float32), axis=1)
    return (hidden_f32 + moe_rows).astype(jnp.bfloat16)


def solution(mesh):
    in_specs = (
        P("ep", "tp"),
        P(("ep", "tp"), None),
        P(),
        P("ep", None),
        P("ep", None),
        P("ep", "tp", None),
        P("ep", "tp", None),
        P("ep", "tp", None),
    )
    out_specs = P(("ep", "tp"), None)
    return jax.shard_map(
        per_device, mesh=mesh, in_specs=in_specs, out_specs=out_specs, check_vma=False
    )
```

profile of v0, /device:TPU:0, one launch (start us, length us, event | category | flops | bytes accessed | tf_op | source)
XLA Modules:
  0.0 377.5 jit_solution(18192333451482127063)
XLA Ops:
  6.5 0.0 copy-start
  6.5 0.0 copy-start.2
  6.5 0.0 copy-start.3
  6.5 4.5 %all-to-all-start = ((bf16[2,64,1024]{2,1,0:T(8,128)(2,1)}), bf16[2,64,1024]{2,1,0:T(8,128)(2,1)S(1)}, u32[]{:S(2)}, u32[]{:S(2)}) async-start(bf16[2,64,1024]{2,1,0:T(8,128)(2,1)} %bitcast.52), calls=%async_computation | async-start | bytes 524288 | tf_op jit(solution)/shard_map/all_to_all | solution.py:27
  11.0 0.0 reduce-scatter.2.cloned.1.call-start
  11.0 0.8 copy.42
  11.8 0.1 eq.42
  12.0 0.1 eq.38
  12.1 1.7 reduce-window.6
  13.8 0.3 slice_reduce_fusion
  14.1 0.1 fusion.16
  14.2 0.1 reduce_sum.30
  14.4 0.1 copy.45
  14.4 0.7 multiply_add_fusion
  15.1 0.5 fusion
  15.6 1.3 all-to-all-done
  17.0 0.0 copy-done.2
  17.0 0.2 fusion.10
  17.2 0.0 copy-done.3
  17.2 0.1 fusion.12
  17.3 8.2 %all_gather.6 = bf16[128,2048]{1,0:T(8,128)(2,1)S(1)} all-gather(bf16[64,2048]{1,0:T(8,128)(2,1)S(1)} %fusion.12), channel_id=1, replica_groups=mesh['ep'=16,'tp'=2] {'tp'}, dimensions={0}, use_global_device_ids=true | all-gather | bytes 786432 | tf_op jit(solution)/shard_map/all_gather | solution.py:32
  25.5 1.2 convolution_convert_fusion.1
  26.8 0.0 copy-start.5
  26.8 98.2 %all_to_all.23 = bf16[16,64,2048]{2,1,0:T(8,128)(2,1)S(1)} all-to-all(bf16[16,64,2048]{2,1,0:T(8,128)(2,1)S(1)} %bitcast.47), channel_id=1, replica_groups=mesh['ep'=16,'tp'=2] {'ep'}, dimensions={0} | all-to-all | bytes 8388608 | tf_op jit(solution)/shard_map/all_to_all | solution.py:49
  125.0 0.0 copy-start.1
  125.0 2.0 copy-done.1
  127.0 0.0 copy-done.5
  127.0 4.8 %fusion.2 = f32[1024,704]{0,1:T(8,128)} fusion(bf16[1024,2048]{1,0:T(8,128)(2,1)S(1)} %bitcast.48, bf16[1,704,2048]{2,1,0:T(8,128)(2,1)S(1)} %copy-done.5), kind=kOutput, calls=%fused_computation.7 | convolution fusion | flops 2952790016 | bytes 9961472 | tf_op jit(solution)/shard_map/dot_general | solution.py:8
  131.8 0.0 copy-done
  131.8 11.3 %convolution_convert_fusion = bf16[1024,2048]{1,0:T(8,128)(2,1)} fusion(bf16[1,704,2048]{2,1,0:T(8,128)(2,1)S(1)} %copy-done, f32[1024,704]{0,1:T(8,128)} %fusion.2, bf16[1024,2048]{1,0:T(8,128)(2,1)} %bitcast.49, bf16[1,704,2048]{2,1,0:T(8,128)(2,1)} %param.13), kind=kOutput, calls=%fused_computation.2 | convolution fusion | flops 5912002560 | bytes 17039360 | tf_op jit(solution)/shard_map/dot_general | solution.py:54
  143.1 97.7 %all_to_all.24 = bf16[16,64,2048]{2,1,0:T(8,128)(2,1)} all-to-all(bf16[16,64,2048]{2,1,0:T(8,128)(2,1)} %bitcast.50), channel_id=1, replica_groups=mesh['ep'=16,'tp'=2] {'ep'}, dimensions={0} | all-to-all | bytes 8388608 | tf_op jit(solution)/shard_map/all_to_all | solution.py:56
  240.8 0.0 copy-start.4
  240.8 0.0 reduce-scatter.2.cloned.1.call-update
  240.8 0.2 all-gather.2.cloned.1.call-start
  241.0 55.0 %reduce-scatter.2.cloned.1.call-done = bf16[16,32,2048]{2,1,0:T(8,128)(2,1)} async-done(((bf16[16,64,2048]{2,1,0:T(8,128)(2,1)}), bf16[16,32,2048]{2,1,0:T(8,128)(2,1)}) %reduce-scatter.2.cloned.1.call-update) | async-done | bytes 2097168 | tf_op jit(solution)/shard_map/reduce_scatter | solution.py:14
  296.0 0.0 all-gather.2.cloned.1.call-update
  296.1 0.1 compare_select_fusion
  296.1 0.1 copy.46
  296.2 0.1 reshape.61
  296.4 0.0 copy-done.4
  296.4 0.1 constant_dynamic-slice_fusion
  296.5 0.1 copy.41
  296.6 57.9 %all-gather.2.cloned.1.call-done = bf16[16,64,2048]{2,1,0:T(8,128)(2,1)} async-done(((bf16[16,32,2048]{2,1,0:T(8,128)(2,1)}), bf16[16,64,2048]{2,1,0:T(8,128)(2,1)}) %all-gather.2.cloned.1.call-update) | async-done | bytes 4194320 | tf_op jit(solution)/shard_map/all_gather | solution.py:21
  354.4 7.8 %gather_fusion = bf16[384,2048]{1,0:T(8,128)(2,1)} fusion(bf16[1024,2048]{1,0:T(8,128)(2,1)} %bitcast.46, s32[1024]{0:T(1024)S(1)} %pad_clamp_fusion), kind=kCustom, calls=%fused_computation | custom fusion | bytes 3147264 | tf_op jit(solution)/shard_map/gather | solution.py:61
  362.2 3.9 %reshape.69 = f32[64,6,2048]{2,1,0:T(8,128)} reshape(bf16[384,2048]{1,0:T(8,128)(2,1)} %gather_fusion) | data formatting | bytes 4718592 | tf_op jit(solution)/shard_map/convert_element_type | solution.py:62
  366.1 3.7 multiply_reduce_fusion
  369.9 0.8 fusion.13
  (6 shorter events, 0.1 us)
Async XLA Ops:
  6.5 125.3 %copy-start = (bf16[1,704,2048]{2,1,0:T(8,128)(2,1)S(1)}, bf16[1,704,2048]{2,1,0:T(8,128)(2,1)}, u32[]{:S(2)}) copy-start(bf16[1,704,2048]{2,1,0:T(8,128)(2,1)} %param.15) | copy-start | bytes 8650756
  6.5 10.5 %copy-start.2 = (bf16[64,2048]{1,0:T(8,128)(2,1)S(1)}, bf16[64,2048]{1,0:T(8,128)(2,1)}, u32[]{:S(2)}) copy-start(bf16[64,2048]{1,0:T(8,128)(2,1)} %param.9) | copy-start | bytes 786436
  6.5 10.7 %copy-start.3 = (f32[2048]{0:T(1024)S(1)}, f32[2048]{0:T(1024)}, u32[]{:S(2)}) copy-start(f32[2048]{0:T(1024)} %param.10) | copy-start | bytes 24580
  6.5 10.4 %all-to-all-start = ((bf16[2,64,1024]{2,1,0:T(8,128)(2,1)}), bf16[2,64,1024]{2,1,0:T(8,128)(2,1)S(1)}, u32[]{:S(2)}, u32[]{:S(2)}) async-start(bf16[2,64,1024]{2,1,0:T(8,128)(2,1)} %bitcast.52), calls=%async_computation | async-start | bytes 524288 | tf_op jit(solution)/shard_map/all_to_all | solution.py:27
  11.0 285.0 %reduce-scatter.2.cloned.1.call-start = ((), (), s32[]{:S(2)}) async-start(), calls=%async_computation.4 | async-start | bytes 6291456 | tf_op jit(solution)/shard_map/reduce_scatter | solution.py:14
  26.8 100.2 %copy-start.5 = (bf16[1,704,2048]{2,1,0:T(8,128)(2,1)S(1)}, bf16[1,704,2048]{2,1,0:T(8,128)(2,1)}, u32[]{:S(2)}) copy-start(bf16[1,704,2048]{2,1,0:T(8,128)(2,1)} %param.14) | copy-start | bytes 8650756
  125.0 2.0 copy-start.1
  240.8 55.6 %copy-start.4 = (f32[128,6]{0,1:T(8,128)S(1)}, f32[128,6]{0,1:T(8,128)}, u32[]{:S(2)}) copy-start(f32[128,6]{0,1:T(8,128)} %param.12) | copy-start | bytes 9220
  240.8 113.7 %all-gather.2.cloned.1.call-start = ((), (), s32[]{:S(2)}) async-start(), calls=%async_computation.5 | async-start | bytes 6291456 | tf_op jit(solution)/shard_map/all_gather | solution.py:21
Sparse Core Ops, SparseCore 0:
  240.9 55.0 reduce-scatter.1
  297.7 56.7 all-gather.1
where the time goes:
time: 378 us; the launch traced here: 377 us
  blocking collectives  204 us (54%)
  waiting for transfers between devices  114 us (30%)
  matrix products  17.3 us (5%)
  local copies, waits for them, and re-layouts  15.6 us (4%)
  between operations  13.5 us (4%)
  other arithmetic  8 us (2%)
  starting transfers between devices  4.72 us (1%)
    all_to_all x1, blocking collectives, per_device(): lax.all_to_all(send_rows, 'ep', split_axis=0, concat_axis=0, tiled=True)  98.2 us
    all_to_all x1, blocking collectives, per_device(): lax.all_to_all(expert_rows, 'ep', split_axis=0, concat_axis=0, tiled=True)  97.7 us
    all_gather x1, waiting for transfers between devices, all_shares(): return lax.all_gather(share_rows, 'tp', axis=1, tiled=True)  57.9 us
    reduce_scatter x1, waiting for transfers between devices, group_total(): lax.psum_scatter(partial_rows.astype(jnp.float32).astype(jnp.bfloat16), '...  55 us
    dot_general x1, matrix products, per_device(): jnp.dot(act, w_down[0], preferred_element_type=jnp.float32)  11.3 us
    all_gather x1, blocking collectives, per_device(): normed_all = lax.all_gather(normed, 'tp', axis=0, tiled=True)  8.17 us
    gather x1, local copies, waits for them, and re-layouts, per_device(): picked = slot_rows.reshape(ep_count * capacity, width)[my_slots]  7.79 us
  transfers between devices with their start and end apart: 3, of which 3 were waited for; matrix products, arithmetic and copies ran while one was open for 1% of the time, Pallas kernels for 0%

commit v1 on v0

v1 whole, which is shorter than its diff:
```python
import jax
import jax.numpy as jnp
from jax import lax
from jax.sharding import PartitionSpec as P

F32 = jnp.float32
BF16 = jnp.bfloat16
AXES = ("ep", "tp")


def by_feature(rows, weight):
    return lax.dot_general(rows, weight, (((1,), (1,)), ((), ())), preferred_element_type=F32)


def flip_if(odd, a, axis):
    return jnp.where(odd == 1, jnp.flip(a, axis), a)


def norm_rows(attn_out, resid, norm_gain):
    seq_rows = lax.all_to_all(attn_out, "tp", split_axis=0, concat_axis=1, tiled=True)
    hidden_state = (resid.astype(F32) + seq_rows.astype(F32)).astype(BF16)
    hidden_f32 = hidden_state.astype(F32)
    mean_sq = jnp.mean(hidden_f32 * hidden_f32, axis=-1, keepdims=True)
    normed = (hidden_f32 * lax.rsqrt(mean_sq + 1e-05) * norm_gain).astype(BF16)
    return hidden_f32, normed


def expert_rows(rows, w_gate, w_up, w_down):
    gate_pre = by_feature(rows, w_gate)
    up_pre = by_feature(rows, w_up)
    act = (jax.nn.silu(gate_pre) * up_pre).astype(BF16)
    return jnp.dot(act, w_down, preferred_element_type=F32)


def gathered_plan(ep_count, attn_out, resid, norm_gain, expert_ids, gate_vals, w_gate, w_up, w_down):
    planes = ep_count // 4
    me = lax.axis_index("ep")
    core, pair, plane = me % 2, (me // 2) % 2, me // 4
    half = lax.axis_index("tp")

    def routes(move):
        pairs = []
        for e in range(ep_count):
            for t in range(2):
                z, x, c, y = move(e // 4, (e // 2) % 2, e % 2, t)
                pairs.append((e * 2 + t, ((z * 2 + x) * 2 + c) * 2 + y))
        return lambda a: lax.ppermute(a, AXES, pairs)

    first = routes(lambda z, x, c, y: (z, x, c, 1 - y) if c else (z, 1 - x, c, y))
    second = routes(lambda z, x, c, y: (z, 1 - x, c, y) if c else (z, x, c, 1 - y))
    sibling = routes(lambda z, x, c, y: (z, x, 1 - c, y))
    down = routes(lambda z, x, c, y: ((z - 1) % planes, x, c, y))

    top = expert_ids.shape[1]
    table = jnp.stack([expert_ids.T.astype(F32), gate_vals.T])
    table = lax.all_gather(table, "ep", axis=0, tiled=False)
    weight = jnp.sum(jnp.where(table[:, 0] == me.astype(F32), table[:, 1], 0.0), axis=1)
    weight = weight.reshape(planes, 2, 2, 2, -1)
    weight = jnp.moveaxis(weight, 2, 1)
    weight = flip_if(core, weight, 1)
    weight = flip_if(pair, weight, 2)
    weight = flip_if(half, weight, 3)
    pair_major, half_major = weight, jnp.swapaxes(weight, 2, 3)
    own_weight = jnp.where(core == 1, pair_major[:, 0], half_major[:, 0]).reshape(planes, -1)
    sib_weight = jnp.where(core == 1, half_major[:, 1], pair_major[:, 1]).reshape(planes, -1)

    hidden_f32, normed = norm_rows(attn_out, resid, norm_gain)
    my_rows = normed.shape[0]
    slots = 2 * my_rows

    def gather_plane(piece):
        two = jnp.concatenate([piece, first(piece)], axis=0)
        own = jnp.concatenate([two, second(two)], axis=0)
        return own, sibling(own)

    def placing(row_weight):
        chosen = row_weight != 0
        counts = chosen.astype(jnp.int32)
        rank = jnp.cumsum(counts) - counts
        slot = jnp.where(chosen, rank, -1)
        return slot[None, :] == jnp.arange(slots, dtype=jnp.int32)[:, None]

    def experts(own, sib, w_own, w_sib):
        place_own, place_sib = placing(w_own), placing(w_sib)
        rows = jnp.concatenate(
            [
                jnp.dot(place_own.astype(BF16), own, preferred_element_type=F32).astype(BF16),
                jnp.dot(place_sib.astype(BF16), sib, preferred_element_type=F32).astype(BF16),
            ],
            axis=0,
        )
        scale = jnp.concatenate(
            [
                jnp.sum(jnp.where(place_own, w_own[None, :], 0.0), axis=1),
                jnp.sum(jnp.where(place_sib, w_sib[None, :], 0.0), axis=1),
            ]
        )
        out = (expert_rows(rows, w_gate[0], w_up[0], w_down[0]) * scale[:, None]).astype(BF16)

        def back(place, slot_rows):
            return lax.dot_general(
                place.astype(BF16), slot_rows, (((0,), (0,)), ((), ())), preferred_element_type=F32
            ).astype(BF16)

        return back(place_own, out[:slots]), back(place_sib, out[slots:])

    def add(a, b):
        return (a.astype(F32) + b.astype(F32)).astype(BF16)

    pieces = [normed]
    for _ in range(planes - 1):
        pieces.append(down(pieces[-1]))
    gathered = [gather_plane(piece) for piece in pieces]
    carried = None
    for step in list(range(1, planes)) + [0]:
        source = (plane + step) % planes
        w_own = lax.dynamic_index_in_dim(own_weight, source, 0, keepdims=False)
        w_sib = lax.dynamic_index_in_dim(sib_weight, source, 0, keepdims=False)
        out_own, out_sib = experts(*gathered[step], w_own, w_sib)
        total = add(out_own, sibling(out_sib))
        kept = total[:slots].astype(F32) + second(total[slots:]).astype(F32)
        if carried is not None:
            kept = kept + carried.astype(F32)
        kept = kept.astype(BF16)
        if step:
            carried = down(kept)
    moe_rows = kept[:my_rows].astype(F32) + first(kept[my_rows:]).astype(F32)
    return (hidden_f32 + moe_rows).astype(BF16)


def exchanged_plan(ep_count, attn_out, resid, norm_gain, expert_ids, gate_vals, w_gate, w_up, w_down):
    hidden_f32, normed = norm_rows(attn_out, resid, norm_gain)
    normed_all = lax.all_gather(normed, "tp", axis=0, tiled=True)
    tok_block, width = normed_all.shape
    capacity = 4 * tok_block * expert_ids.shape[1] // (3 * ep_count)
    flat_ids = expert_ids.reshape(-1)
    onehot = (flat_ids[:, None] == jnp.arange(ep_count, dtype=jnp.int32)[None, :]).astype(jnp.int32)
    rank_in = jnp.sum(onehot * (jnp.cumsum(onehot, axis=0) - onehot), axis=1)
    slot_index = (flat_ids * capacity + rank_in).reshape(tok_block, -1)
    slot_range = jnp.arange(ep_count * capacity, dtype=jnp.int32)
    hit = slot_index[None, :, :] == slot_range[:, None, None]
    placing = jnp.any(hit, axis=-1).astype(BF16)
    send_rows = jnp.dot(placing, normed_all, preferred_element_type=F32).astype(BF16)
    send_rows = send_rows.reshape(ep_count, capacity, width)
    received = lax.all_to_all(send_rows, "ep", split_axis=0, concat_axis=0, tiled=True)
    out_rows = expert_rows(received.reshape(-1, width), w_gate[0], w_up[0], w_down[0]).astype(BF16)
    back_rows = lax.all_to_all(
        out_rows.reshape(received.shape), "ep", split_axis=0, concat_axis=0, tiled=True
    )
    scale = jnp.sum(jnp.where(hit, gate_vals[None, :, :], 0.0), axis=(1, 2))
    weighted = (back_rows.reshape(-1, width).astype(F32) * scale[:, None]).astype(BF16)
    part = lax.dot_general(placing, weighted, (((0,), (0,)), ((), ())), preferred_element_type=F32)
    moe_rows = lax.psum_scatter(part, "tp", scatter_dimension=0, tiled=True)
    return (hidden_f32 + moe_rows).astype(BF16)


def solution(mesh):
    ep_count, tp_count = mesh.shape["ep"], mesh.shape["tp"]
    plan = gathered_plan if tp_count == 2 and ep_count % 4 == 0 else exchanged_plan

    def per_device(*arguments):
        return plan(ep_count, *arguments)

    in_specs = (
        P("ep", "tp"),
        P(AXES, None),
        P(),
        P("ep", None),
        P("ep", None),
        P("ep", "tp", None),
        P("ep", "tp", None),
        P("ep", "tp", None),
    )
    return jax.shard_map(
        per_device, mesh=mesh, in_specs=in_specs, out_specs=P(AXES, None), check_vma=False
    )
```

time: 378 us -> 200 us (0.53)
  blocking collectives: 204 us -> 22.7 us
  waiting for transfers between devices: 114 us -> 56.4 us
  matrix products: 17.3 us -> 62.8 us
  starting transfers between devices: 4.72 us -> 37.3 us
  between operations: 13.5 us -> 0.59 us
    all_to_all x2 -> x0, blocking collectives: 196 us -> none  [the longest x1 98.2 us: per_device(): lax.all_to_all(send_rows, 'ep', split_axis=0, concat_axis=0, tiled=True)]
    all_gather x1 -> x0, waiting for transfers between devices: 57.9 us -> none  [all_shares(): return lax.all_gather(share_rows, 'tp', axis=1, tiled=True)]
    ppermute x0 -> x27, waiting for transfers between devices: none -> 56.4 us  [routes(): return lambda a: lax.ppermute(a, AXES, pairs)]
    reduce_scatter x1 -> x0, waiting for transfers between devices: 55 us -> none  [group_total(): lax.psum_scatter(partial_rows.astype(jnp.float32).astype(jnp.bfloat16), '...]
    dot_general x2 -> x20, matrix products: 12.5 us -> 49.7 us  [the longest x4 26.6 us: expert_rows(): return jnp.dot(act, w_down, preferred_element_type=F32)]
    ppermute x0 -> x27, starting transfers between devices: none -> 32.8 us  [routes(): return lambda a: lax.ppermute(a, AXES, pairs)]
    all_gather x1, blocking collectives: 8.17 us -> 22.7 us  [gathered_plan(): table = lax.all_gather(table, 'ep', axis=0, tiled=False)]
    dot_general x1 -> x4, matrix products: 4.83 us -> 13.1 us  [by_feature(): lax.dot_general(rows, weight, (((1,), (1,)), ((), ())), preferred_element...]
  transfers between devices with their start and end apart: 3 -> 28, of which waited for: 3 -> 12; matrix products, arithmetic and copies ran while one was open for 1% -> 39% of each run, Pallas kernels for 0% -> 0%
where the time goes in v1:
time: 200 us
  matrix products  62.8 us (31%)
  waiting for transfers between devices  56.4 us (28%)
  starting transfers between devices  37.3 us (19%)
  blocking collectives  22.7 us (11%)
  local copies, waits for them, and re-layouts  12 us (6%)
  other arithmetic  8.02 us (4%)
    ppermute x27, waiting for transfers between devices, routes(): return lambda a: lax.ppermute(a, AXES, pairs)  56.4 us
    ppermute x27, starting transfers between devices, routes(): return lambda a: lax.ppermute(a, AXES, pairs)  32.8 us
    dot_general x4, matrix products, expert_rows(): return jnp.dot(act, w_down, preferred_element_type=F32)  26.6 us
    all_gather x1, blocking collectives, gathered_plan(): table = lax.all_gather(table, 'ep', axis=0, tiled=False)  22.7 us
    dot_general x4, matrix products, by_feature(): lax.dot_general(rows, weight, (((1,), (1,)), ((), ())), preferred_element...  13.1 us
    dot_general x8, matrix products, back(): lax.dot_general(place.astype(BF16), slot_rows, (((0,), (0,)), ((), ())),...  10.9 us
    unnamed x34, local copies, waits for them, and re-layouts  7.6 us
    dot_general x4, matrix products, experts(): jnp.dot(place_own.astype(BF16), own, preferred_element_type=F32)  7.3 us
  transfers between devices with their start and end apart: 28, of which 12 were waited for; matrix products, arithmetic and copies ran while one was open for 39% of the time, Pallas kernels for 0%

profile of v1, /device:TPU:0, one launch (start us, length us, event | category | flops | bytes accessed | tf_op | source)
XLA Modules:
  0.0 199.9 jit_solution(1080636234052076980)
XLA Ops:
  0.0 4.5 %all-to-all-start = ((bf16[2,64,1024]{2,1,0:T(8,128)(2,1)}), bf16[2,64,1024]{2,1,0:T(8,128)(2,1)S(1)}, u32[]{:S(2)}, u32[]{:S(2)}) async-start(bf16[2,64,1024]{2,1,0:T(8,128)(2,1)} %bitcast.129), calls=%async_computation | async-start | bytes 524288 | tf_op jit(solution)/shard_map/all_to_all | solution.py:20
  5.9 22.7 %all-gather = f32[32,6,128]{2,1,0:T(8,128)S(1)} all-gather(f32[2,6,128]{2,1,0:T(8,128)S(1)} %pad_maximum_fusion.21), channel_id=2, replica_groups=mesh['ep'=16,'tp'=2] {'ep'}, dimensions={0}, use_global_device_ids=true | all-gather | bytes 104448 | tf_op jit(solution)/shard_map/all_gather | solution.py:56
  35.3 8.3 %collective-permute-done.5 = bf16[64,2048]{1,0:T(8,128)(2,1)S(1)} collective-permute-done((bf16[64,2048]{1,0:T(8,128)(2,1)S(1)}, bf16[64,2048]{1,0:T(8,128)(2,1)S(1)}, u32[]{:S(2)}, u32[]{:S(2)}) %collective-permute-start.5) | collective-permute-done | bytes 262176 | tf_op jit(solution)/shard_map/ppermute | solution.py:47
  43.6 2.0 collective-permute-start.1
  45.6 2.1 %collective-permute-start.6 = (bf16[64,2048]{1,0:T(8,128)(2,1)S(1)}, bf16[64,2048]{1,0:T(8,128)(2,1)S(1)}, u32[]{:S(2)}, u32[]{:S(2)}) collective-permute-start(bf16[64,2048]{1,0:T(8,128)(2,1)S(1)} %collective-permute-done.5), channel_id=1, source_target_pairs={{0,24},{1,25},{2,26},{3,27},{4,28},{5,29},{6,30},{7,31},{8,0},{9,1... | collective-permute-start | bytes 786440 | tf_op jit(solution)/shard_map/ppermute | solution.py:47
  48.4 4.0 %collective-permute-done.18 = bf16[64,2048]{1,0:T(8,128)(2,1)S(1)} collective-permute-done((bf16[64,2048]{1,0:T(8,128)(2,1)S(1)}, bf16[64,2048]{1,0:T(8,128)(2,1)S(1)}, u32[]{:S(2)}, u32[]{:S(2)}) %collective-permute-start.18) | collective-permute-done | bytes 262176 | tf_op jit(solution)/shard_map/ppermute | solution.py:47
  52.5 2.3 %collective-permute-start.19 = (bf16[128,2048]{1,0:T(8,128)(2,1)S(1)}, bf16[128,2048]{1,0:T(8,128)(2,1)S(1)}, u32[]{:S(2)}, u32[]{:S(2)}) collective-permute-start(bf16[128,2048]{1,0:T(8,128)(2,1)S(1)} %pad_maximum_fusion.20), channel_id=1, source_target_pairs={{0,1},{1,0},{2,6},{3,7},{4,5},{5,4},{6,2},{7,3},{8,9},{9,8},{10,14... | collective-permute-start | bytes 1572872 | tf_op jit(solution)/shard_map/ppermute | solution.py:47
  55.6 4.2 %collective-permute-start.7 = (bf16[64,2048]{1,0:T(8,128)(2,1)S(1)}, bf16[64,2048]{1,0:T(8,128)(2,1)S(1)}, u32[]{:S(2)}, u32[]{:S(2)}) collective-permute-start(bf16[64,2048]{1,0:T(8,128)(2,1)S(1)} %collective-permute-done.6), channel_id=1, source_target_pairs={{0,24},{1,25},{2,26},{3,27},{4,28},{5,29},{6,30},{7,31},{8,0},{9,1... | collective-permute-start | bytes 786440 | tf_op jit(solution)/shard_map/ppermute | solution.py:47
  60.5 3.6 %collective-permute-done.13 = bf16[64,2048]{1,0:T(8,128)(2,1)S(1)} collective-permute-done((bf16[64,2048]{1,0:T(8,128)(2,1)S(1)}, bf16[64,2048]{1,0:T(8,128)(2,1)S(1)}, u32[]{:S(2)}, u32[]{:S(2)}) %collective-permute-start.13) | collective-permute-done | bytes 262176 | tf_op jit(solution)/shard_map/ppermute | solution.py:47
  66.4 1.0 constant_dynamic-update-slice_fusion.6
  67.4 2.0 collective-permute-start.20
  69.3 2.3 %convolution_convert_fusion.9 = bf16[128,2048]{1,0:T(8,128)(2,1)} fusion(bf16[256,2048]{1,0:T(8,128)(2,1)} %constant_dynamic-update-slice_fusion.6, s32[256]{0:T(256)S(1)} %bitcast.139), kind=kOutput, calls=%fused_computation.45 | convolution fusion | flops 134512640 | bytes 1573888 | tf_op jit(solution)/shard_map/dot_general | solution.py:87
  72.5 1.1 collective-permute-start.9
  74.3 1.8 collective-permute-done.14
  76.2 0.9 constant_dynamic-update-slice_fusion.3
  77.0 2.3 %convolution_convert_fusion.11 = bf16[128,2048]{1,0:T(8,128)(2,1)} fusion(bf16[256,2048]{1,0:T(8,128)(2,1)} %constant_dynamic-update-slice_fusion.3, s32[256]{0:T(256)S(1)} %bitcast.136), kind=kOutput, calls=%fused_computation.47 | convolution fusion | flops 134512640 | bytes 1573888 | tf_op jit(solution)/shard_map/dot_general | solution.py:87
  79.4 2.4 %collective-permute-done.9 = bf16[128,2048]{1,0:T(8,128)(2,1)S(1)} collective-permute-done((bf16[128,2048]{1,0:T(8,128)(2,1)S(1)}, bf16[128,2048]{1,0:T(8,128)(2,1)S(1)}, u32[]{:S(2)}, u32[]{:S(2)}) %collective-permute-start.9) | collective-permute-done | bytes 524320 | tf_op jit(solution)/shard_map/ppermute | solution.py:47
  81.8 0.9 constant_dynamic-update-slice_fusion
  83.2 2.3 %convolution_convert_fusion.13 = bf16[128,2048]{1,0:T(8,128)(2,1)} fusion(bf16[256,2048]{1,0:T(8,128)(2,1)} %constant_dynamic-update-slice_fusion, s32[256]{0:T(256)S(1)} %bitcast.133), kind=kOutput, calls=%fused_computation.49 | convolution fusion | flops 134512640 | bytes 1573888 | tf_op jit(solution)/shard_map/dot_general | solution.py:87
  86.6 1.8 fusion.22
  88.4 6.6 %fusion.45 = bf16[256,2048]{1,0:T(8,128)(2,1)} fusion(bf16[1,704,2048]{2,1,0:T(8,128)(2,1)S(1)} %copy-done, f32[256]{0:T(256)S(1)} %pad_maximum_fusion.22, bf16[1,704,2048]{2,1,0:T(8,128)(2,1)} %param.14, f32[256,704]{0,1:T(8,128)} %fusion.22, bf16[128,2048]{1,0:T(8,128)(2,1)} %copy-done.6, bf16[128,2048]{1,0:T(8,128)(2,1)} %copy-done.13), kind=kOutput, calls=%fused_computation.31 | convolution fusion | flops 1480622080 | bytes 8586240 | tf_op jit(solution)/shard_map/dot_general | solution.py:32
  95.1 1.5 convolution_convert_fusion.8
  96.6 0.8 copy-done.7
  97.4 3.9 %fusion.16 = f32[256,704]{0,1:T(8,128)} fusion(bf16[1,704,2048]{2,1,0:T(8,128)(2,1)} %param.13, bf16[128,2048]{1,0:T(8,128)(2,1)S(1)} %convolution_convert_fusion.8, bf16[128,2048]{1,0:T(8,128)(2,1)} %convolution_convert_fusion.9), kind=kOutput, calls=%fused_computation.16 | convolution fusion | flops 740294656 | bytes 4653056 | tf_op jit(solution)/shard_map/dot_general | solution.py:12
  101.3 6.6 %fusion.36 = bf16[256,2048]{1,0:T(8,128)(2,1)} fusion(bf16[1,704,2048]{2,1,0:T(8,128)(2,1)S(1)} %copy-done, f32[256]{0:T(256)S(1)} %pad_maximum_fusion.25, bf16[1,704,2048]{2,1,0:T(8,128)(2,1)} %param.14, f32[256,704]{0,1:T(8,128)} %fusion.16, bf16[128,2048]{1,0:T(8,128)(2,1)} %copy-done.7, bf16[128,2048]{1,0:T(8,128)(2,1)} %convolution_convert_fusion.9), kind=kOutput, calls=%fused_computation.28 | convolution fusion | flops 1480622080 | bytes 8586240 | tf_op jit(solution)/shard_map/dot_general | solution.py:32
  107.9 2.6 %convolution_convert_fusion = bf16[256,2048]{1,0:T(8,128)(2,1)} fusion(bf16[256,2048]{1,0:T(8,128)(2,1)} %fusion.36, s32[256]{0:T(256)S(1)} %bitcast.152), kind=kOutput, calls=%fused_computation.32 | convolution fusion | flops 134774784 | bytes 1573888 | tf_op jit(solution)/shard_map/dot_general | solution.py:101
  110.6 1.5 convolution_convert_fusion.10
  112.9 3.7 %fusion.18 = f32[256,704]{0,1:T(8,128)} fusion(bf16[1,704,2048]{2,1,0:T(8,128)(2,1)} %param.13, bf16[128,2048]{1,0:T(8,128)(2,1)S(1)} %convolution_convert_fusion.10, bf16[128,2048]{1,0:T(8,128)(2,1)S(1)} %copy-done.5), kind=kOutput, calls=%fused_computation.18 | convolution fusion | flops 740294656 | bytes 4653056 | tf_op jit(solution)/shard_map/dot_general | solution.py:12
  116.6 6.8 %fusion.39 = bf16[256,2048]{1,0:T(8,128)(2,1)} fusion(bf16[1,704,2048]{2,1,0:T(8,128)(2,1)S(1)} %copy-done, f32[256]{0:T(256)S(1)} %pad_maximum_fusion.24, bf16[1,704,2048]{2,1,0:T(8,128)(2,1)} %param.14, f32[256,704]{0,1:T(8,128)} %fusion.18, bf16[128,2048]{1,0:T(8,128)(2,1)} %copy-done.8, bf16[128,2048]{1,0:T(8,128)(2,1)} %convolution_convert_fusion.11), kind=kOutput, calls=%fused_computation.29 | convolution fusion | flops 1480622080 | bytes 8586240 | tf_op jit(solution)/shard_map/dot_general | solution.py:32
  123.4 2.6 %convolution_convert_fusion.2 = bf16[256,2048]{1,0:T(8,128)(2,1)} fusion(bf16[256,2048]{1,0:T(8,128)(2,1)} %fusion.39, s32[256]{0:T(256)S(1)} %bitcast.149), kind=kOutput, calls=%fused_computation.34 | convolution fusion | flops 134774784 | bytes 1573888 | tf_op jit(solution)/shard_map/dot_general | solution.py:101
  126.5 1.5 convolution_convert_fusion.12
  128.1 0.8 copy-done.9
  128.9 3.7 %fusion.20 = f32[256,704]{0,1:T(8,128)} fusion(bf16[1,704,2048]{2,1,0:T(8,128)(2,1)} %param.13, bf16[128,2048]{1,0:T(8,128)(2,1)S(1)} %convolution_convert_fusion.12, bf16[128,2048]{1,0:T(8,128)(2,1)S(1)} %copy-done.4), kind=kOutput, calls=%fused_computation.20 | convolution fusion | flops 740294656 | bytes 4653056 | tf_op jit(solution)/shard_map/dot_general | solution.py:12
  132.6 6.6 %fusion.42 = bf16[256,2048]{1,0:T(8,128)(2,1)} fusion(bf16[1,704,2048]{2,1,0:T(8,128)(2,1)S(1)} %copy-done, f32[256]{0:T(256)S(1)} %pad_maximum_fusion.23, bf16[1,704,2048]{2,1,0:T(8,128)(2,1)} %param.14, f32[256,704]{0,1:T(8,128)} %fusion.20, bf16[128,2048]{1,0:T(8,128)(2,1)} %copy-done.9, bf16[128,2048]{1,0:T(8,128)(2,1)} %convolution_convert_fusion.13), kind=kOutput, calls=%fused_computation.30 | convolution fusion | flops 1480622080 | bytes 8586240 | tf_op jit(solution)/shard_map/dot_general | solution.py:32
  139.2 2.0 %add_convert_fusion = bf16[256,2048]{1,0:T(8,128)(2,1)S(1)} fusion(bf16[256,2048]{1,0:T(8,128)(2,1)} %collective-permute-done.21, bf16[256,2048]{1,0:T(8,128)(2,1)} %fusion.36, s32[256]{0:T(256)S(1)} %bitcast.140), kind=kOutput, calls=%fused_computation.52 | convolution fusion | flops 136871936 | bytes 2622464 | tf_op jit(solution)/shard_map/dot_general | solution.py:101
  141.2 1.9 collective-permute-start.22
  143.7 1.8 add_convert_fusion.1
  145.8 4.7 %collective-permute-done.22 = bf16[128,2048]{1,0:T(8,128)(2,1)S(1)} collective-permute-done((bf16[128,2048]{1,0:T(8,128)(2,1)S(1)}, bf16[128,2048]{1,0:T(8,128)(2,1)S(1)}, u32[]{:S(2)}, u32[]{:S(2)}) %collective-permute-start.22) | collective-permute-done | bytes 524320 | tf_op jit(solution)/shard_map/ppermute | solution.py:47
  150.6 2.7 %collective-permute-start.23 = (bf16[128,2048]{1,0:T(8,128)(2,1)S(1)}, bf16[128,2048]{1,0:T(8,128)(2,1)S(1)}, u32[]{:S(2)}, u32[]{:S(2)}) collective-permute-start(bf16[128,2048]{1,0:T(8,128)(2,1)S(1)} %add_convert_fusion.7), channel_id=1, source_target_pairs={{0,24},{1,25},{2,26},{3,27},{4,28},{5,29},{6,30},{7,31},{8,0},{9,1... | collective-permute-start | bytes 1572872 | tf_op jit(solution)/shard_map/ppermute | solution.py:47
  154.4 1.3 collective-permute-start.12
  156.1 8.1 %collective-permute-done.23 = bf16[128,2048]{1,0:T(8,128)(2,1)S(1)} collective-permute-done((bf16[128,2048]{1,0:T(8,128)(2,1)S(1)}, bf16[128,2048]{1,0:T(8,128)(2,1)S(1)}, u32[]{:S(2)}, u32[]{:S(2)}) %collective-permute-start.23) | collective-permute-done | bytes 524320 | tf_op jit(solution)/shard_map/ppermute | solution.py:47
  164.4 4.3 %collective-permute-start.24 = (bf16[128,2048]{1,0:T(8,128)(2,1)S(1)}, bf16[128,2048]{1,0:T(8,128)(2,1)S(1)}, u32[]{:S(2)}, u32[]{:S(2)}) collective-permute-start(bf16[128,2048]{1,0:T(8,128)(2,1)S(1)} %add_convert_fusion.6), channel_id=1, source_target_pairs={{0,24},{1,25},{2,26},{3,27},{4,28},{5,29},{6,30},{7,31},{8,0},{9,1... | collective-permute-start | bytes 1572872 | tf_op jit(solution)/shard_map/ppermute | solution.py:47
  169.3 0.9 collective-permute-start.4
  170.2 8.5 %collective-permute-done.24 = bf16[128,2048]{1,0:T(8,128)(2,1)S(1)} collective-permute-done((bf16[128,2048]{1,0:T(8,128)(2,1)S(1)}, bf16[128,2048]{1,0:T(8,128)(2,1)S(1)}, u32[]{:S(2)}, u32[]{:S(2)}) %collective-permute-start.24) | collective-permute-done | bytes 524320 | tf_op jit(solution)/shard_map/ppermute | solution.py:47
  179.0 4.3 %collective-permute-start.25 = (bf16[128,2048]{1,0:T(8,128)(2,1)S(1)}, bf16[128,2048]{1,0:T(8,128)(2,1)S(1)}, u32[]{:S(2)}, u32[]{:S(2)}) collective-permute-start(bf16[128,2048]{1,0:T(8,128)(2,1)S(1)} %add_convert_fusion.5), channel_id=1, source_target_pairs={{0,24},{1,25},{2,26},{3,27},{4,28},{5,29},{6,30},{7,31},{8,0},{9,1... | collective-permute-start | bytes 1572872 | tf_op jit(solution)/shard_map/ppermute | solution.py:47
  183.3 9.0 %collective-permute-done.25 = bf16[128,2048]{1,0:T(8,128)(2,1)S(1)} collective-permute-done((bf16[128,2048]{1,0:T(8,128)(2,1)S(1)}, bf16[128,2048]{1,0:T(8,128)(2,1)S(1)}, u32[]{:S(2)}, u32[]{:S(2)}) %collective-permute-start.25) | collective-permute-done | bytes 524320 | tf_op jit(solution)/shard_map/ppermute | solution.py:47
  192.6 1.7 collective-permute-start.26
  194.3 4.7 %collective-permute-done.26 = bf16[64,2048]{1,0:T(8,128)(2,1)S(1)} collective-permute-done((bf16[64,2048]{1,0:T(8,128)(2,1)S(1)}, bf16[64,2048]{1,0:T(8,128)(2,1)S(1)}, u32[]{:S(2)}, u32[]{:S(2)}) %collective-permute-start.26) | collective-permute-done | bytes 262176 | tf_op jit(solution)/shard_map/ppermute | solution.py:47
  (160 shorter events, 21.4 us)
Async XLA Ops:
  0.0 88.4 %copy-start = (bf16[1,704,2048]{2,1,0:T(8,128)(2,1)S(1)}, bf16[1,704,2048]{2,1,0:T(8,128)(2,1)}, u32[]{:S(2)}) copy-start(bf16[1,704,2048]{2,1,0:T(8,128)(2,1)} %param.15) | copy-start | bytes 8650756
  0.0 34.6 %copy-start.10 = (bf16[64,2048]{1,0:T(8,128)(2,1)S(1)}, bf16[64,2048]{1,0:T(8,128)(2,1)}, u32[]{:S(2)}) copy-start(bf16[64,2048]{1,0:T(8,128)(2,1)} %param.9) | copy-start | bytes 786436
  0.0 34.5 %all-to-all-start = ((bf16[2,64,1024]{2,1,0:T(8,128)(2,1)}), bf16[2,64,1024]{2,1,0:T(8,128)(2,1)S(1)}, u32[]{:S(2)}, u32[]{:S(2)}) async-start(bf16[2,64,1024]{2,1,0:T(8,128)(2,1)} %bitcast.129), calls=%async_computation | async-start | bytes 524288 | tf_op jit(solution)/shard_map/all_to_all | solution.py:20
  4.5 30.3 %copy-start.11 = (f32[2048]{0:T(1024)S(1)}, f32[2048]{0:T(1024)}, u32[]{:S(2)}) copy-start(f32[2048]{0:T(1024)} %param.10) | copy-start | bytes 24580
  35.0 8.6 %collective-permute-start.5 = (bf16[64,2048]{1,0:T(8,128)(2,1)S(1)}, bf16[64,2048]{1,0:T(8,128)(2,1)S(1)}, u32[]{:S(2)}, u32[]{:S(2)}) collective-permute-start(bf16[64,2048]{1,0:T(8,128)(2,1)S(1)} %fusion.86), channel_id=1, source_target_pairs={{0,24},{1,25},{2,26},{3,27},{4,28},{5,29},{6,30},{7,31},{8,0},{9,1... | collective-permute-start | bytes 786440 | tf_op jit(solution)/shard_map/ppermute | solution.py:47
  35.0 8.5 %collective-permute-start = (bf16[64,2048]{1,0:T(8,128)(2,1)S(1)}, bf16[64,2048]{1,0:T(8,128)(2,1)S(1)}, u32[]{:S(2)}, u32[]{:S(2)}) collective-permute-start(bf16[64,2048]{1,0:T(8,128)(2,1)S(1)} %fusion.86), channel_id=1, source_target_pairs={{0,4},{1,5},{2,3},{3,2},{4,0},{5,1},{6,7},{7,6},{8,12},{9,13},{10,... | collective-permute-start | bytes 786440 | tf_op jit(solution)/shard_map/ppermute | solution.py:47
  43.6 8.9 %collective-permute-start.18 = (bf16[64,2048]{1,0:T(8,128)(2,1)S(1)}, bf16[64,2048]{1,0:T(8,128)(2,1)S(1)}, u32[]{:S(2)}, u32[]{:S(2)}) collective-permute-start(bf16[64,2048]{1,0:T(8,128)(2,1)S(1)} %collective-permute-done.5), channel_id=1, source_target_pairs={{0,4},{1,5},{2,3},{3,2},{4,0},{5,1},{6,7},{7,6},{8,12},{9,13},{10,... | collective-permute-start | bytes 786440 | tf_op jit(solution)/shard_map/ppermute | solution.py:47
  43.6 20.6 %collective-permute-start.1 = (bf16[128,2048]{1,0:T(8,128)(2,1)S(1)}, bf16[128,2048]{1,0:T(8,128)(2,1)S(1)}, u32[]{:S(2)}, u32[]{:S(2)}) collective-permute-start(bf16[128,2048]{1,0:T(8,128)(2,1)S(1)} %pad_maximum_fusion.17), channel_id=1, source_target_pairs={{0,1},{1,0},{2,6},{3,7},{4,5},{5,4},{6,2},{7,3},{8,9},{9,8},{10,14... | collective-permute-start | bytes 1572872 | tf_op jit(solution)/shard_map/ppermute | solution.py:47
  45.6 9.2 %collective-permute-start.6 = (bf16[64,2048]{1,0:T(8,128)(2,1)S(1)}, bf16[64,2048]{1,0:T(8,128)(2,1)S(1)}, u32[]{:S(2)}, u32[]{:S(2)}) collective-permute-start(bf16[64,2048]{1,0:T(8,128)(2,1)S(1)} %collective-permute-done.5), channel_id=1, source_target_pairs={{0,24},{1,25},{2,26},{3,27},{4,28},{5,29},{6,30},{7,31},{8,0},{9,1... | collective-permute-start | bytes 786440 | tf_op jit(solution)/shard_map/ppermute | solution.py:47
  52.5 13.9 %collective-permute-start.19 = (bf16[128,2048]{1,0:T(8,128)(2,1)S(1)}, bf16[128,2048]{1,0:T(8,128)(2,1)S(1)}, u32[]{:S(2)}, u32[]{:S(2)}) collective-permute-start(bf16[128,2048]{1,0:T(8,128)(2,1)S(1)} %pad_maximum_fusion.20), channel_id=1, source_target_pairs={{0,1},{1,0},{2,6},{3,7},{4,5},{5,4},{6,2},{7,3},{8,9},{9,8},{10,14... | collective-permute-start | bytes 1572872 | tf_op jit(solution)/shard_map/ppermute | solution.py:47
  54.8 9.2 %collective-permute-start.13 = (bf16[64,2048]{1,0:T(8,128)(2,1)S(1)}, bf16[64,2048]{1,0:T(8,128)(2,1)S(1)}, u32[]{:S(2)}, u32[]{:S(2)}) collective-permute-start(bf16[64,2048]{1,0:T(8,128)(2,1)S(1)} %collective-permute-done.6), channel_id=1, source_target_pairs={{0,4},{1,5},{2,3},{3,2},{4,0},{5,1},{6,7},{7,6},{8,12},{9,13},{10,... | collective-permute-start | bytes 786440 | tf_op jit(solution)/shard_map/ppermute | solution.py:47
  55.6 8.9 %collective-permute-start.7 = (bf16[64,2048]{1,0:T(8,128)(2,1)S(1)}, bf16[64,2048]{1,0:T(8,128)(2,1)S(1)}, u32[]{:S(2)}, u32[]{:S(2)}) collective-permute-start(bf16[64,2048]{1,0:T(8,128)(2,1)S(1)} %collective-permute-done.6), channel_id=1, source_target_pairs={{0,24},{1,25},{2,26},{3,27},{4,28},{5,29},{6,30},{7,31},{8,0},{9,1... | collective-permute-start | bytes 786440 | tf_op jit(solution)/shard_map/ppermute | solution.py:47
  64.1 12.1 %collective-permute-start.14 = (bf16[128,2048]{1,0:T(8,128)(2,1)S(1)}, bf16[128,2048]{1,0:T(8,128)(2,1)S(1)}, u32[]{:S(2)}, u32[]{:S(2)}) collective-permute-start(bf16[128,2048]{1,0:T(8,128)(2,1)S(1)} %pad_maximum_fusion.19), channel_id=1, source_target_pairs={{0,1},{1,0},{2,6},{3,7},{4,5},{5,4},{6,2},{7,3},{8,9},{9,8},{10,14... | collective-permute-start | bytes 1572872 | tf_op jit(solution)/shard_map/ppermute | solution.py:47
  64.4 21.1 %collective-permute-start.2 = (bf16[256,2048]{1,0:T(8,128)(2,1)S(1)}, bf16[256,2048]{1,0:T(8,128)(2,1)S(1)}, u32[]{:S(2)}, u32[]{:S(2)}) collective-permute-start(bf16[256,2048]{1,0:T(8,128)(2,1)S(1)} %pad_maximum_fusion), channel_id=1, source_target_pairs={{0,2},{1,3},{2,0},{3,1},{4,6},{5,7},{6,4},{7,5},{8,10},{9,11},{10,... | collective-permute-start | bytes 3145736 | tf_op jit(solution)/shard_map/ppermute | solution.py:47
  65.2 7.3 %collective-permute-start.8 = (bf16[64,2048]{1,0:T(8,128)(2,1)S(1)}, bf16[64,2048]{1,0:T(8,128)(2,1)S(1)}, u32[]{:S(2)}, u32[]{:S(2)}) collective-permute-start(bf16[64,2048]{1,0:T(8,128)(2,1)S(1)} %collective-permute-done.7), channel_id=1, source_target_pairs={{0,4},{1,5},{2,3},{3,2},{4,0},{5,1},{6,7},{7,6},{8,12},{9,13},{10,... | collective-permute-start | bytes 786440 | tf_op jit(solution)/shard_map/ppermute | solution.py:47
  66.4 19.4 %copy-start.13 = (bf16[128,2048]{1,0:T(8,128)(2,1)}, bf16[128,2048]{1,0:T(8,128)(2,1)S(1)}, u32[]{:S(2)}) copy-start(bf16[128,2048]{1,0:T(8,128)(2,1)S(1)} %convolution_convert_fusion.15) | copy-start | bytes 1572868
  67.4 27.7 %collective-permute-start.20 = (bf16[256,2048]{1,0:T(8,128)(2,1)}, bf16[256,2048]{1,0:T(8,128)(2,1)}, u32[]{:S(2)}, u32[]{:S(2)}) collective-permute-start(bf16[256,2048]{1,0:T(8,128)(2,1)} %constant_dynamic-update-slice_fusion.6), channel_id=1, source_target_pairs={{0,2},{1,3},{2,0},{3,1},{4,6},{5,7},{6,4},{7,5},{8,10},{9,11},{10,... | collective-permute-start | bytes 3145736 | tf_op jit(solution)/shard_map/ppermute | solution.py:47
  72.5 9.3 %collective-permute-start.9 = (bf16[128,2048]{1,0:T(8,128)(2,1)S(1)}, bf16[128,2048]{1,0:T(8,128)(2,1)S(1)}, u32[]{:S(2)}, u32[]{:S(2)}) collective-permute-start(bf16[128,2048]{1,0:T(8,128)(2,1)S(1)} %pad_maximum_fusion.18), channel_id=1, source_target_pairs={{0,1},{1,0},{2,6},{3,7},{4,5},{5,4},{6,2},{7,3},{8,9},{9,8},{10,14... | collective-permute-start | bytes 1572872 | tf_op jit(solution)/shard_map/ppermute | solution.py:47
  77.0 33.6 %collective-permute-start.15 = (bf16[256,2048]{1,0:T(8,128)(2,1)}, bf16[256,2048]{1,0:T(8,128)(2,1)}, u32[]{:S(2)}, u32[]{:S(2)}) collective-permute-start(bf16[256,2048]{1,0:T(8,128)(2,1)} %constant_dynamic-update-slice_fusion.3), channel_id=1, source_target_pairs={{0,2},{1,3},{2,0},{3,1},{4,6},{5,7},{6,4},{7,5},{8,10},{9,11},{10,... | collective-permute-start | bytes 3145736 | tf_op jit(solution)/shard_map/ppermute | solution.py:47
  79.4 7.2 %copy-start.12 = (bf16[1,704,2048]{2,1,0:T(8,128)(2,1)S(1)}, bf16[1,704,2048]{2,1,0:T(8,128)(2,1)}, u32[]{:S(2)}) copy-start(bf16[1,704,2048]{2,1,0:T(8,128)(2,1)} %param.13) | copy-start | bytes 8650756
  82.6 43.9 %collective-permute-start.10 = (bf16[256,2048]{1,0:T(8,128)(2,1)}, bf16[256,2048]{1,0:T(8,128)(2,1)}, u32[]{:S(2)}, u32[]{:S(2)}) collective-permute-start(bf16[256,2048]{1,0:T(8,128)(2,1)} %constant_dynamic-update-slice_fusion), channel_id=1, source_target_pairs={{0,2},{1,3},{2,0},{3,1},{4,6},{5,7},{6,4},{7,5},{8,10},{9,11},{10,... | collective-permute-start | bytes 3145736 | tf_op jit(solution)/shard_map/ppermute | solution.py:47
  85.8 0.8 copy-start.6
  96.6 0.8 copy-start.7
  107.9 5.0 %copy-start.5 = (bf16[128,2048]{1,0:T(8,128)(2,1)S(1)}, bf16[128,2048]{1,0:T(8,128)(2,1)}, u32[]{:S(2)}) copy-start(bf16[128,2048]{1,0:T(8,128)(2,1)} %convolution_convert_fusion.11) | copy-start | bytes 1572868
  110.6 28.6 %collective-permute-start.21 = (bf16[256,2048]{1,0:T(8,128)(2,1)}, bf16[256,2048]{1,0:T(8,128)(2,1)}, u32[]{:S(2)}, u32[]{:S(2)}) collective-permute-start(bf16[256,2048]{1,0:T(8,128)(2,1)} %convolution_convert_fusion), channel_id=1, source_target_pairs={{0,2},{1,3},{2,0},{3,1},{4,6},{5,7},{6,4},{7,5},{8,10},{9,11},{10,... | collective-permute-start | bytes 3145736 | tf_op jit(solution)/shard_map/ppermute | solution.py:47
  112.1 0.8 copy-start.8
  123.4 5.4 %copy-start.4 = (bf16[128,2048]{1,0:T(8,128)(2,1)S(1)}, bf16[128,2048]{1,0:T(8,128)(2,1)}, u32[]{:S(2)}) copy-start(bf16[128,2048]{1,0:T(8,128)(2,1)} %convolution_convert_fusion.13) | copy-start | bytes 1572868
  126.0 17.7 %collective-permute-start.16 = (bf16[256,2048]{1,0:T(8,128)(2,1)}, bf16[256,2048]{1,0:T(8,128)(2,1)}, u32[]{:S(2)}, u32[]{:S(2)}) collective-permute-start(bf16[256,2048]{1,0:T(8,128)(2,1)} %convolution_convert_fusion.2), channel_id=1, source_target_pairs={{0,2},{1,3},{2,0},{3,1},{4,6},{5,7},{6,4},{7,5},{8,10},{9,11},{10,... | collective-permute-start | bytes 3145736 | tf_op jit(solution)/shard_map/ppermute | solution.py:47
  128.0 0.8 copy-start.9
  139.1 4.0 %copy-start.2 = (bf16[256,2048]{1,0:T(8,128)(2,1)S(1)}, bf16[256,2048]{1,0:T(8,128)(2,1)}, u32[]{:S(2)}) copy-start(bf16[256,2048]{1,0:T(8,128)(2,1)} %fusion.42) | copy-start | bytes 3145732
  139.1 4.6 %copy-start.3 = (bf16[256,2048]{1,0:T(8,128)(2,1)S(1)}, bf16[256,2048]{1,0:T(8,128)(2,1)}, u32[]{:S(2)}) copy-start(bf16[256,2048]{1,0:T(8,128)(2,1)} %fusion.39) | copy-start | bytes 3145732
  141.2 9.2 %collective-permute-start.22 = (bf16[128,2048]{1,0:T(8,128)(2,1)S(1)}, bf16[128,2048]{1,0:T(8,128)(2,1)S(1)}, u32[]{:S(2)}, u32[]{:S(2)}) collective-permute-start(bf16[128,2048]{1,0:T(8,128)(2,1)S(1)} %slice.189), channel_id=1, source_target_pairs={{0,1},{1,0},{2,6},{3,7},{4,5},{5,4},{6,2},{7,3},{8,9},{9,8},{10,14... | collective-permute-start | bytes 1572872 | tf_op jit(solution)/shard_map/ppermute | solution.py:47
  143.6 9.7 %copy-start.1 = (bf16[256,2048]{1,0:T(8,128)(2,1)S(1)}, bf16[256,2048]{1,0:T(8,128)(2,1)}, u32[]{:S(2)}) copy-start(bf16[256,2048]{1,0:T(8,128)(2,1)} %fusion.45) | copy-start | bytes 3145732
  143.6 10.3 %collective-permute-start.11 = (bf16[256,2048]{1,0:T(8,128)(2,1)S(1)}, bf16[256,2048]{1,0:T(8,128)(2,1)S(1)}, u32[]{:S(2)}, u32[]{:S(2)}) collective-permute-start(bf16[256,2048]{1,0:T(8,128)(2,1)S(1)} %convolution_convert_fusion.4), channel_id=1, source_target_pairs={{0,2},{1,3},{2,0},{3,1},{4,6},{5,7},{6,4},{7,5},{8,10},{9,11},{10,... | collective-permute-start | bytes 3145736 | tf_op jit(solution)/shard_map/ppermute | solution.py:47
  145.6 10.5 %collective-permute-start.17 = (bf16[128,2048]{1,0:T(8,128)(2,1)S(1)}, bf16[128,2048]{1,0:T(8,128)(2,1)S(1)}, u32[]{:S(2)}, u32[]{:S(2)}) collective-permute-start(bf16[128,2048]{1,0:T(8,128)(2,1)S(1)} %slice.185), channel_id=1, source_target_pairs={{0,1},{1,0},{2,6},{3,7},{4,5},{5,4},{6,2},{7,3},{8,9},{9,8},{10,14... | collective-permute-start | bytes 1572872 | tf_op jit(solution)/shard_map/ppermute | solution.py:47
  150.6 13.6 %collective-permute-start.23 = (bf16[128,2048]{1,0:T(8,128)(2,1)S(1)}, bf16[128,2048]{1,0:T(8,128)(2,1)S(1)}, u32[]{:S(2)}, u32[]{:S(2)}) collective-permute-start(bf16[128,2048]{1,0:T(8,128)(2,1)S(1)} %add_convert_fusion.7), channel_id=1, source_target_pairs={{0,24},{1,25},{2,26},{3,27},{4,28},{5,29},{6,30},{7,31},{8,0},{9,1... | collective-permute-start | bytes 1572872 | tf_op jit(solution)/shard_map/ppermute | solution.py:47
  153.8 15.0 %collective-permute-start.3 = (bf16[256,2048]{1,0:T(8,128)(2,1)S(1)}, bf16[256,2048]{1,0:T(8,128)(2,1)S(1)}, u32[]{:S(2)}, u32[]{:S(2)}) collective-permute-start(bf16[256,2048]{1,0:T(8,128)(2,1)S(1)} %convolution_convert_fusion.6), channel_id=1, source_target_pairs={{0,2},{1,3},{2,0},{3,1},{4,6},{5,7},{6,4},{7,5},{8,10},{9,11},{10,... | collective-permute-start | bytes 3145736 | tf_op jit(solution)/shard_map/ppermute | solution.py:47
  154.4 15.8 %collective-permute-start.12 = (bf16[128,2048]{1,0:T(8,128)(2,1)S(1)}, bf16[128,2048]{1,0:T(8,128)(2,1)S(1)}, u32[]{:S(2)}, u32[]{:S(2)}) collective-permute-start(bf16[128,2048]{1,0:T(8,128)(2,1)S(1)} %slice.181), channel_id=1, source_target_pairs={{0,1},{1,0},{2,6},{3,7},{4,5},{5,4},{6,2},{7,3},{8,9},{9,8},{10,14... | collective-permute-start | bytes 1572872 | tf_op jit(solution)/shard_map/ppermute | solution.py:47
  164.4 14.3 %collective-permute-start.24 = (bf16[128,2048]{1,0:T(8,128)(2,1)S(1)}, bf16[128,2048]{1,0:T(8,128)(2,1)S(1)}, u32[]{:S(2)}, u32[]{:S(2)}) collective-permute-start(bf16[128,2048]{1,0:T(8,128)(2,1)S(1)} %add_convert_fusion.6), channel_id=1, source_target_pairs={{0,24},{1,25},{2,26},{3,27},{4,28},{5,29},{6,30},{7,31},{8,0},{9,1... | collective-permute-start | bytes 1572872 | tf_op jit(solution)/shard_map/ppermute | solution.py:47
  169.3 14.0 %collective-permute-start.4 = (bf16[128,2048]{1,0:T(8,128)(2,1)S(1)}, bf16[128,2048]{1,0:T(8,128)(2,1)S(1)}, u32[]{:S(2)}, u32[]{:S(2)}) collective-permute-start(bf16[128,2048]{1,0:T(8,128)(2,1)S(1)} %slice.177), channel_id=1, source_target_pairs={{0,1},{1,0},{2,6},{3,7},{4,5},{5,4},{6,2},{7,3},{8,9},{9,8},{10,14... | collective-permute-start | bytes 1572872 | tf_op jit(solution)/shard_map/ppermute | solution.py:47
  179.0 13.4 %collective-permute-start.25 = (bf16[128,2048]{1,0:T(8,128)(2,1)S(1)}, bf16[128,2048]{1,0:T(8,128)(2,1)S(1)}, u32[]{:S(2)}, u32[]{:S(2)}) collective-permute-start(bf16[128,2048]{1,0:T(8,128)(2,1)S(1)} %add_convert_fusion.5), channel_id=1, source_target_pairs={{0,24},{1,25},{2,26},{3,27},{4,28},{5,29},{6,30},{7,31},{8,0},{9,1... | collective-permute-start | bytes 1572872 | tf_op jit(solution)/shard_map/ppermute | solution.py:47
  192.6 6.4 %collective-permute-start.26 = (bf16[64,2048]{1,0:T(8,128)(2,1)S(1)}, bf16[64,2048]{1,0:T(8,128)(2,1)S(1)}, u32[]{:S(2)}, u32[]{:S(2)}) collective-permute-start(bf16[64,2048]{1,0:T(8,128)(2,1)S(1)} %slice.191), channel_id=1, source_target_pairs={{0,4},{1,5},{2,3},{3,2},{4,0},{5,1},{6,7},{7,6},{8,12},{9,13},{10,... | collective-permute-start | bytes 786440 | tf_op jit(solution)/shard_map/ppermute | solution.py:47

commit v2 on v1

v2 whole, which is shorter than its diff:
```python
import functools

import jax
import jax.numpy as jnp
from jax import lax
from jax.experimental import pallas as pl
from jax.experimental.pallas import tpu as pltpu
from jax.sharding import PartitionSpec as P

F32 = jnp.float32
BF16 = jnp.bfloat16
AXES = ("ep", "tp")
LANES = 128
VMEM = pl.BlockSpec(memory_space=pltpu.VMEM)
SMEM = pl.BlockSpec(memory_space=pltpu.SMEM)


def by_feature(rows, weight):
    return lax.dot_general(rows, weight, (((1,), (1,)), ((), ())), preferred_element_type=F32)


def norm_rows(attn_out, resid, norm_gain):
    seq_rows = lax.all_to_all(attn_out, "tp", split_axis=0, concat_axis=1, tiled=True)
    hidden_state = (resid.astype(F32) + seq_rows.astype(F32)).astype(BF16)
    hidden_f32 = hidden_state.astype(F32)
    mean_sq = jnp.mean(hidden_f32 * hidden_f32, axis=-1, keepdims=True)
    normed = (hidden_f32 * lax.rsqrt(mean_sq + 1e-05) * norm_gain).astype(BF16)
    return hidden_f32, normed


def expert_rows(rows, w_gate, w_up, w_down):
    gate_pre = by_feature(rows, w_gate)
    up_pre = by_feature(rows, w_up)
    act = (jax.nn.silu(gate_pre) * up_pre).astype(BF16)
    return jnp.dot(act, w_down, preferred_element_type=F32)


def tiles(extent, size):
    return [(start, min(size, extent - start)) for start in range(0, extent, size)]


def product(a, b, a_dim, b_dim):
    return lax.dot_general(a, b, (((a_dim,), (b_dim,)), ((), ())), preferred_element_type=F32)


def front_kernel(cols_ref, resid_ref, gain_ref, ids_ref, gates_ref, packed_ref, hidden_ref):
    shares, rows, columns = cols_ref.shape
    width = resid_ref.shape[1]
    attn = jnp.concatenate([cols_ref[i] for i in range(shares)], axis=1)
    hidden_state = (resid_ref[...].astype(F32) + attn.astype(F32)).astype(BF16)
    hidden_ref[...] = hidden_state
    hidden = hidden_state.astype(F32)
    mean_sq = jnp.mean(hidden * hidden, axis=1, keepdims=True)
    packed_ref[:, :width] = (hidden * lax.rsqrt(mean_sq + 1e-05) * gain_ref[...]).astype(BF16)
    lane = lax.broadcasted_iota(jnp.int32, (rows, LANES), 1)
    weight = jnp.zeros((rows, LANES), F32)
    for k in range(ids_ref.shape[1]):
        hit = lane % (LANES // 2) == ids_ref[:, k : k + 1]
        weight = weight + jnp.where(hit, gates_ref[:, k : k + 1], 0.0)
    high = weight.astype(BF16).astype(F32)
    packed_ref[:, width:] = jnp.where(lane < LANES // 2, high, weight - high).astype(BF16)


def front(cols, resid, norm_gain, ids, gates):
    rows, width = resid.shape
    return pl.pallas_call(
        front_kernel,
        out_shape=(
            jax.ShapeDtypeStruct((rows, width + LANES), BF16),
            jax.ShapeDtypeStruct((rows, width), BF16),
        ),
        in_specs=[VMEM] * 5,
        out_specs=(VMEM, VMEM),
        compiler_params=pltpu.CompilerParams(vmem_limit_bytes=8 * 2**20),
    )(cols, resid, norm_gain.reshape(1, -1), ids, gates)


def expert_kernel(me_ref, own_ref, sib_ref, gate_ref, up_ref, down_ref, own_out, sib_out, rows, act):
    count = own_ref.shape[0]
    hidden_units, width = down_ref.shape
    slots = count // 2
    me = me_ref[0]
    row = lax.broadcasted_iota(jnp.int32, (count, count), 0)
    column = lax.broadcasted_iota(jnp.int32, (count, count), 1)
    earlier = jnp.where(column < row, 1.0, 0.0).astype(BF16)
    slot = lax.broadcasted_iota(jnp.int32, (count, slots), 1).astype(F32)

    def placing(source):
        routing = source[:, width:].astype(F32)
        lane = lax.broadcasted_iota(jnp.int32, routing.shape, 1)
        weight = jnp.sum(jnp.where(lane % (LANES // 2) == me, routing, 0.0), axis=1, keepdims=True)
        chosen = jnp.broadcast_to(jnp.where(weight != 0, 1.0, 0.0), (count, slots))
        rank = product(earlier, chosen.astype(BF16), 1, 0)
        return jnp.where(rank == slot, chosen, 0.0).astype(BF16), weight

    place_own, weight_own = placing(own_ref)
    place_sib, weight_sib = placing(sib_ref)
    for start, size in tiles(width, 512):
        part = slice(start, start + size)
        rows[:slots, part] = product(place_own, own_ref[:, part], 0, 0).astype(BF16)
        rows[slots:, part] = product(place_sib, sib_ref[:, part], 0, 0).astype(BF16)
    for start, size in tiles(hidden_units, 256):
        part = slice(start, start + size)
        gate_pre = product(rows[...], gate_ref[part, :], 1, 1)
        up_pre = product(rows[...], up_ref[part, :], 1, 1)
        act[:, part] = (gate_pre / (1.0 + jnp.exp(-gate_pre)) * up_pre).astype(BF16)
    for start, size in tiles(width, 1024):
        part = slice(start, start + size)
        out = product(act[...], down_ref[:, part], 1, 0).astype(BF16)
        own_out[:, part] = (product(place_own, out[:slots], 1, 0) * weight_own).astype(BF16)
        sib_out[:, part] = (product(place_sib, out[slots:], 1, 0) * weight_sib).astype(BF16)


def experts(me, own, sib, w_gate, w_up, w_down):
    count = own.shape[0]
    hidden_units, width = w_down.shape
    result = jax.ShapeDtypeStruct((count, width), BF16)
    return pl.pallas_call(
        expert_kernel,
        out_shape=(result, result),
        in_specs=[SMEM] + [VMEM] * 5,
        out_specs=(VMEM, VMEM),
        scratch_shapes=[pltpu.VMEM((count, width), BF16), pltpu.VMEM((count, hidden_units), BF16)],
        compiler_params=pltpu.CompilerParams(vmem_limit_bytes=30 * 2**20),
        cost_estimate=pl.CostEstimate(
            flops=6 * count * width * hidden_units, bytes_accessed=8 * count * width, transcendentals=0
        ),
    )(me, own, sib, w_gate, w_up, w_down)


def gathered_plan(ep_count, attn_out, resid, norm_gain, expert_ids, gate_vals, w_gate, w_up, w_down):
    planes = ep_count // 4
    my_rows = resid.shape[0]
    half = lax.axis_index("tp")

    def routes(move):
        pairs = []
        for e in range(ep_count):
            for t in range(2):
                z, x, c, y = move(e // 4, (e // 2) % 2, e % 2, t)
                pairs.append((e * 2 + t, ((z * 2 + x) * 2 + c) * 2 + y))
        return lambda a: lax.ppermute(a, AXES, pairs)

    first = routes(lambda z, x, c, y: (z, x, c, 1 - y) if c else (z, 1 - x, c, y))
    second = routes(lambda z, x, c, y: (z, 1 - x, c, y) if c else (z, x, c, 1 - y))
    sibling = routes(lambda z, x, c, y: (z, x, 1 - c, y))
    down = routes(lambda z, x, c, y: ((z - 1) % planes, x, c, y))

    cols = attn_out.reshape(2, my_rows, -1)
    cols = lax.all_to_all(cols, "tp", split_axis=0, concat_axis=0, tiled=True)
    ids = lax.dynamic_slice_in_dim(expert_ids, half * my_rows, my_rows, 0)
    gates = lax.dynamic_slice_in_dim(gate_vals, half * my_rows, my_rows, 0)
    packed, hidden = front(cols, resid, norm_gain, ids, gates)
    me = lax.axis_index("ep").reshape(1)

    def gather_plane(piece):
        two = jnp.concatenate([piece, first(piece)], axis=0)
        own = jnp.concatenate([two, second(two)], axis=0)
        return own, sibling(own)

    def add(*terms):
        return functools.reduce(lambda a, b: a + b, [t.astype(F32) for t in terms])

    pieces = [packed]
    for _ in range(planes - 1):
        pieces.append(down(pieces[-1]))
    gathered = [gather_plane(piece) for piece in pieces]
    carried = []
    for step in list(range(1, planes)) + [0]:
        out_own, out_sib = experts(me, *gathered[step], w_gate[0], w_up[0], w_down[0])
        total = add(out_own, sibling(out_sib)).astype(BF16)
        kept = add(total[: 2 * my_rows], second(total[2 * my_rows :]), *carried).astype(BF16)
        if step:
            carried = [down(kept)]
    return add(hidden, kept[:my_rows], first(kept[my_rows:])).astype(BF16)


def exchanged_plan(ep_count, attn_out, resid, norm_gain, expert_ids, gate_vals, w_gate, w_up, w_down):
    hidden_f32, normed = norm_rows(attn_out, resid, norm_gain)
    normed_all = lax.all_gather(normed, "tp", axis=0, tiled=True)
    tok_block, width = normed_all.shape
    capacity = 4 * tok_block * expert_ids.shape[1] // (3 * ep_count)
    flat_ids = expert_ids.reshape(-1)
    onehot = (flat_ids[:, None] == jnp.arange(ep_count, dtype=jnp.int32)[None, :]).astype(jnp.int32)
    rank_in = jnp.sum(onehot * (jnp.cumsum(onehot, axis=0) - onehot), axis=1)
    slot_index = (flat_ids * capacity + rank_in).reshape(tok_block, -1)
    slot_range = jnp.arange(ep_count * capacity, dtype=jnp.int32)
    hit = slot_index[None, :, :] == slot_range[:, None, None]
    placing = jnp.any(hit, axis=-1).astype(BF16)
    send_rows = jnp.dot(placing, normed_all, preferred_element_type=F32).astype(BF16)
    send_rows = send_rows.reshape(ep_count, capacity, width)
    received = lax.all_to_all(send_rows, "ep", split_axis=0, concat_axis=0, tiled=True)
    out_rows = expert_rows(received.reshape(-1, width), w_gate[0], w_up[0], w_down[0]).astype(BF16)
    back_rows = lax.all_to_all(
        out_rows.reshape(received.shape), "ep", split_axis=0, concat_axis=0, tiled=True
    )
    scale = jnp.sum(jnp.where(hit, gate_vals[None, :, :], 0.0), axis=(1, 2))
    weighted = (back_rows.reshape(-1, width).astype(F32) * scale[:, None]).astype(BF16)
    part = lax.dot_general(placing, weighted, (((0,), (0,)), ((), ())), preferred_element_type=F32)
    moe_rows = lax.psum_scatter(part, "tp", scatter_dimension=0, tiled=True)
    return (hidden_f32 + moe_rows).astype(BF16)


def solution(mesh):
    ep_count, tp_count = mesh.shape["ep"], mesh.shape["tp"]
    paired = tp_count == 2 and ep_count % 4 == 0 and ep_count <= LANES // 2
    plan = gathered_plan if paired else exchanged_plan

    def per_device(*arguments):
        return plan(ep_count, *arguments)

    in_specs = (
        P("ep", "tp"),
        P(AXES, None),
        P(),
        P("ep", None),
        P("ep", None),
        P("ep", "tp", None),
        P("ep", "tp", None),
        P("ep", "tp", None),
    )
    return jax.shard_map(
        per_device, mesh=mesh, in_specs=in_specs, out_specs=P(AXES, None), check_vma=False
    )
```

time: 200 us -> 150 us (0.75)
  matrix products: 62.8 us -> 0 us
  blocking collectives: 22.7 us -> 0 us
  Pallas kernels: 0 us -> 22.4 us
  waiting for transfers between devices: 56.4 us -> 67.6 us
  other arithmetic: 8.02 us -> 3.36 us
  local copies, waits for them, and re-layouts: 12 us -> 15.9 us
  starting transfers between devices: 37.3 us -> 40.1 us
    dot_general x24 -> x0, matrix products: 62.8 us -> none  [the longest x4 26.6 us: expert_rows(): return jnp.dot(act, w_down, preferred_element_type=F32)]
    all_gather x1 -> x0, blocking collectives: 22.7 us -> none  [gathered_plan(): table = lax.all_gather(table, 'ep', axis=0, tiled=False)]
    pallas_call x0 -> x5, Pallas kernels: none -> 22.4 us  [the longest x4 22 us: experts(): pl.pallas_call(expert_kernel, out_shape=(result, result), in_specs=[SMEM]...]
    ppermute x27, waiting for transfers between devices: 56.4 us -> 62.8 us  [routes(): return lambda a: lax.ppermute(a, AXES, pairs)]
    all_to_all x1, waiting for transfers between devices: 0.01 us -> 4.84 us  [gathered_plan(): cols = lax.all_to_all(cols, 'tp', split_axis=0, concat_axis=0, tiled=True)]
    another operation x26 -> x0, other arithmetic: 4.71 us -> none
    unnamed x34 -> x22, local copies, waits for them, and re-layouts: 7.6 us -> 11.4 us
    ppermute x27, starting transfers between devices: 32.8 us -> 35.7 us  [routes(): return lambda a: lax.ppermute(a, AXES, pairs)]
  transfers between devices with their start and end apart: 28 -> 28, of which waited for: 12 -> 13; matrix products, arithmetic and copies ran while one was open for 39% -> 9% of each run, Pallas kernels for 0% -> 15%
where the time goes in v2:
time: 150 us
  waiting for transfers between devices  67.6 us (45%)
  starting transfers between devices  40.1 us (27%)
  Pallas kernels  22.4 us (15%)
  local copies, waits for them, and re-layouts  15.9 us (11%)
  other arithmetic  3.36 us (2%)
    ppermute x27, waiting for transfers between devices, routes(): return lambda a: lax.ppermute(a, AXES, pairs)  62.8 us
    ppermute x27, starting transfers between devices, routes(): return lambda a: lax.ppermute(a, AXES, pairs)  35.7 us
    pallas_call x4, Pallas kernels, experts(): pl.pallas_call(expert_kernel, out_shape=(result, result), in_specs=[SMEM]...  22 us
    unnamed x22, local copies, waits for them, and re-layouts  11.4 us
    all_to_all x1, waiting for transfers between devices, gathered_plan(): cols = lax.all_to_all(cols, 'tp', split_axis=0, concat_axis=0, tiled=True)  4.84 us
    all_to_all x1, starting transfers between devices, gathered_plan(): cols = lax.all_to_all(cols, 'tp', split_axis=0, concat_axis=0, tiled=True)  4.37 us
    concatenate x4, local copies, waits for them, and re-layouts, gather_plane(): own = jnp.concatenate([two, second(two)], axis=0)  3.48 us
  transfers between devices with their start and end apart: 28, of which 13 were waited for; matrix products, arithmetic and copies ran while one was open for 9% of the time, Pallas kernels for 15%

profile of v2, /device:TPU:0, one launch (start us, length us, event | category | flops | bytes accessed | tf_op | source)
XLA Modules:
  0.0 149.5 jit_solution(12504435942399759022)
XLA Ops:
  0.0 4.4 %all-to-all-start = ((bf16[2,64,1024]{2,1,0:T(8,128)(2,1)}), bf16[2,64,1024]{2,1,0:T(8,128)(2,1)S(1)}, u32[]{:S(2)}, u32[]{:S(2)}) async-start(bf16[2,64,1024]{2,1,0:T(8,128)(2,1)} %bitcast.19), calls=%async_computation | async-start | bytes 524288 | tf_op jit(solution)/shard_map/all_to_all | solution.py:150
  4.5 0.8 constant_dynamic-slice_fusion
  5.4 4.8 %all-to-all-done.cols_ref = bf16[2,64,1024]{2,1,0:T(8,128)(2,1)S(1)} async-done(((bf16[2,64,1024]{2,1,0:T(8,128)(2,1)}), bf16[2,64,1024]{2,1,0:T(8,128)(2,1)S(1)}, u32[]{:S(2)}, u32[]{:S(2)}) %all-to-all-start) | async-done | bytes 262176 | tf_op jit(solution)/shard_map/all_to_all | solution.py:150
  10.2 0.9 copy-done.4
  12.2 3.9 %collective-permute-start.5 = (bf16[64,2176]{1,0:T(8,128)(2,1)S(1)}, bf16[64,2176]{1,0:T(8,128)(2,1)S(1)}, u32[]{:S(2)}, u32[]{:S(2)}) collective-permute-start(bf16[64,2176]{1,0:T(8,128)(2,1)S(1)} %get-tuple-element.16), channel_id=1, source_target_pairs={{0,24},{1,25},{2,26},{3,27},{4,28},{5,29},{6,30},{7,31},{8,0},{9,1... | collective-permute-start | bytes 835592 | tf_op jit(solution)/shard_map/ppermute | solution.py:142
  16.1 1.5 collective-permute-start
  17.6 0.7 constant_dynamic-update-slice_fusion.2
  18.4 4.3 %collective-permute-done = bf16[64,2176]{1,0:T(8,128)(2,1)S(1)} collective-permute-done((bf16[64,2176]{1,0:T(8,128)(2,1)S(1)}, bf16[64,2176]{1,0:T(8,128)(2,1)S(1)}, u32[]{:S(2)}, u32[]{:S(2)}) %collective-permute-start) | collective-permute-done | bytes 278560 | tf_op jit(solution)/shard_map/ppermute | solution.py:142
  23.8 1.5 collective-permute-start.18
  25.3 2.4 %collective-permute-start.6 = (bf16[64,2176]{1,0:T(8,128)(2,1)S(1)}, bf16[64,2176]{1,0:T(8,128)(2,1)S(1)}, u32[]{:S(2)}, u32[]{:S(2)}) collective-permute-start(bf16[64,2176]{1,0:T(8,128)(2,1)S(1)} %collective-permute-done.5), channel_id=1, source_target_pairs={{0,24},{1,25},{2,26},{3,27},{4,28},{5,29},{6,30},{7,31},{8,0},{9,1... | collective-permute-start | bytes 835592 | tf_op jit(solution)/shard_map/ppermute | solution.py:142
  27.7 0.7 constant_dynamic-update-slice_fusion.1
  28.4 3.8 %collective-permute-done.18 = bf16[64,2176]{1,0:T(8,128)(2,1)S(1)} collective-permute-done((bf16[64,2176]{1,0:T(8,128)(2,1)S(1)}, bf16[64,2176]{1,0:T(8,128)(2,1)S(1)}, u32[]{:S(2)}, u32[]{:S(2)}) %collective-permute-start.18) | collective-permute-done | bytes 278560 | tf_op jit(solution)/shard_map/ppermute | solution.py:142
  33.6 1.7 %collective-permute-start.13 = (bf16[64,2176]{1,0:T(8,128)(2,1)S(1)}, bf16[64,2176]{1,0:T(8,128)(2,1)S(1)}, u32[]{:S(2)}, u32[]{:S(2)}) collective-permute-start(bf16[64,2176]{1,0:T(8,128)(2,1)S(1)} %collective-permute-done.6), channel_id=1, source_target_pairs={{0,4},{1,5},{2,3},{3,2},{4,0},{5,1},{6,7},{7,6},{8,12},{9,13},{10,... | collective-permute-start | bytes 835592 | tf_op jit(solution)/shard_map/ppermute | solution.py:142
  35.3 2.1 %collective-permute-start.7 = (bf16[64,2176]{1,0:T(8,128)(2,1)S(1)}, bf16[64,2176]{1,0:T(8,128)(2,1)S(1)}, u32[]{:S(2)}, u32[]{:S(2)}) collective-permute-start(bf16[64,2176]{1,0:T(8,128)(2,1)S(1)} %collective-permute-done.6), channel_id=1, source_target_pairs={{0,24},{1,25},{2,26},{3,27},{4,28},{5,29},{6,30},{7,31},{8,0},{9,1... | collective-permute-start | bytes 835592 | tf_op jit(solution)/shard_map/ppermute | solution.py:142
  38.2 4.0 %collective-permute-done.13 = bf16[64,2176]{1,0:T(8,128)(2,1)S(1)} collective-permute-done((bf16[64,2176]{1,0:T(8,128)(2,1)S(1)}, bf16[64,2176]{1,0:T(8,128)(2,1)S(1)}, u32[]{:S(2)}, u32[]{:S(2)}) %collective-permute-start.13) | collective-permute-done | bytes 278560 | tf_op jit(solution)/shard_map/ppermute | solution.py:142
  42.2 1.4 collective-permute-start.14
  43.6 0.9 constant_dynamic-update-slice_fusion.own_ref
  44.5 0.9 collective-permute-start.8
  45.4 0.8 constant_dynamic-update-slice_fusion.5
  46.2 0.7 constant_dynamic-update-slice_fusion.7
  46.9 0.9 constant_dynamic-update-slice_fusion.9.own_ref
  47.8 3.2 %collective-permute-done.8 = bf16[64,2176]{1,0:T(8,128)(2,1)S(1)} collective-permute-done((bf16[64,2176]{1,0:T(8,128)(2,1)S(1)}, bf16[64,2176]{1,0:T(8,128)(2,1)S(1)}, u32[]{:S(2)}, u32[]{:S(2)}) %collective-permute-start.8) | collective-permute-done | bytes 278560 | tf_op jit(solution)/shard_map/ppermute | solution.py:142
  51.1 0.8 collective-permute-start.9
  51.8 2.9 %collective-permute-done.14 = bf16[128,2176]{1,0:T(8,128)(2,1)S(1)} collective-permute-done((bf16[128,2176]{1,0:T(8,128)(2,1)S(1)}, bf16[128,2176]{1,0:T(8,128)(2,1)S(1)}, u32[]{:S(2)}, u32[]{:S(2)}) %collective-permute-start.14) | collective-permute-done | bytes 557088 | tf_op jit(solution)/shard_map/ppermute | solution.py:142
  54.8 0.9 constant_dynamic-update-slice_fusion.6.own_ref
  55.6 0.7 constant_dynamic-update-slice_fusion.4
  56.4 4.4 %collective-permute-done.9 = bf16[128,2176]{1,0:T(8,128)(2,1)S(1)} collective-permute-done((bf16[128,2176]{1,0:T(8,128)(2,1)S(1)}, bf16[128,2176]{1,0:T(8,128)(2,1)S(1)}, u32[]{:S(2)}, u32[]{:S(2)}) %collective-permute-start.9) | collective-permute-done | bytes 557088 | tf_op jit(solution)/shard_map/ppermute | solution.py:142
  60.7 0.8 constant_dynamic-update-slice_fusion.3.own_ref
  61.6 1.5 collective-permute-start.10
  63.1 1.8 %copy-done.2 = bf16[1,704,2048]{2,1,0:T(8,128)(2,1)S(1)} copy-done((bf16[1,704,2048]{2,1,0:T(8,128)(2,1)S(1)}, bf16[1,704,2048]{2,1,0:T(8,128)(2,1)}, u32[]{:S(2)}) %copy-start.2) | copy-done | bytes 2883608
  64.9 1.8 %copy-done.3 = bf16[1,704,2048]{2,1,0:T(8,128)(2,1)S(1)} copy-done((bf16[1,704,2048]{2,1,0:T(8,128)(2,1)S(1)}, bf16[1,704,2048]{2,1,0:T(8,128)(2,1)}, u32[]{:S(2)}) %copy-start.3) | copy-done | bytes 2883608
  66.7 5.5 %shard_map.86 = (bf16[256,2048]{1,0:T(8,128)(2,1)S(1)}, bf16[256,2048]{1,0:T(8,128)(2,1)S(1)}) custom-call(s32[1]{0:T(128)} %bitcast.2.me_ref, bf16[256,2176]{1,0:T(8,128)(2,1)} %constant_dynamic-update-slice_fusion.9.own_ref, bf16[256,2176]{1,0:T(8,128)(2,1)} %collective-permute-done.20.sib_ref, bf16[704,2048]{1,0:T(8,128)(2,1)S(1)} %bitcast.6, ...), custom_call_target="tpu_custom_call" | custom-call | flops 2214592512 | bytes 4194304 | tf_op jit(solution)/shard_map/pallas_call | solution.py:118
  72.3 5.5 %shard_map.85 = (bf16[256,2048]{1,0:T(8,128)(2,1)S(1)}, bf16[256,2048]{1,0:T(8,128)(2,1)S(1)}) custom-call(s32[1]{0:T(128)} %bitcast.2.me_ref, bf16[256,2176]{1,0:T(8,128)(2,1)} %constant_dynamic-update-slice_fusion.6.own_ref, bf16[256,2176]{1,0:T(8,128)(2,1)} %collective-permute-done.15.sib_ref, bf16[704,2048]{1,0:T(8,128)(2,1)S(1)} %bitcast.7, ...), custom_call_target="tpu_custom_call" | custom-call | flops 2214592512 | bytes 4194304 | tf_op jit(solution)/shard_map/pallas_call | solution.py:118
  78.3 5.5 %shard_map.83 = (bf16[256,2048]{1,0:T(8,128)(2,1)S(1)}, bf16[256,2048]{1,0:T(8,128)(2,1)S(1)}) custom-call(s32[1]{0:T(128)} %bitcast.2.me_ref, bf16[256,2176]{1,0:T(8,128)(2,1)} %constant_dynamic-update-slice_fusion.own_ref, bf16[256,2176]{1,0:T(8,128)(2,1)} %collective-permute-done.2.sib_ref, bf16[704,2048]{1,0:T(8,128)(2,1)S(1)} %bitcast.8, ...), custom_call_target="tpu_custom_call" | custom-call | flops 2214592512 | bytes 4194304 | tf_op jit(solution)/shard_map/pallas_call | solution.py:118
  83.9 5.7 %shard_map.84 = (bf16[256,2048]{1,0:T(8,128)(2,1)S(1)}, bf16[256,2048]{1,0:T(8,128)(2,1)S(1)}) custom-call(s32[1]{0:T(128)} %bitcast.2.me_ref, bf16[256,2176]{1,0:T(8,128)(2,1)} %constant_dynamic-update-slice_fusion.3.own_ref, bf16[256,2176]{1,0:T(8,128)(2,1)} %collective-permute-done.10.sib_ref, bf16[704,2048]{1,0:T(8,128)(2,1)S(1)} %bitcast.9, ...), custom_call_target="tpu_custom_call" | custom-call | flops 2214592512 | bytes 4194304 | tf_op jit(solution)/shard_map/pallas_call | solution.py:118
  91.7 1.4 collective-permute-start.17
  93.1 6.6 %collective-permute-done.22 = bf16[128,2048]{1,0:T(8,128)(2,1)S(1)} collective-permute-done((bf16[128,2048]{1,0:T(8,128)(2,1)S(1)}, bf16[128,2048]{1,0:T(8,128)(2,1)S(1)}, u32[]{:S(2)}, u32[]{:S(2)}) %collective-permute-start.22) | collective-permute-done | bytes 524320 | tf_op jit(solution)/shard_map/ppermute | solution.py:142
  99.9 2.8 %collective-permute-start.23 = (bf16[128,2048]{1,0:T(8,128)(2,1)S(1)}, bf16[128,2048]{1,0:T(8,128)(2,1)S(1)}, u32[]{:S(2)}, u32[]{:S(2)}) collective-permute-start(bf16[128,2048]{1,0:T(8,128)(2,1)S(1)} %add_convert_fusion.7), channel_id=1, source_target_pairs={{0,24},{1,25},{2,26},{3,27},{4,28},{5,29},{6,30},{7,31},{8,0},{9,1... | collective-permute-start | bytes 1572872 | tf_op jit(solution)/shard_map/ppermute | solution.py:142
  103.1 1.0 collective-permute-start.12
  104.1 1.3 collective-permute-done.17
  105.4 8.3 %collective-permute-done.23 = bf16[128,2048]{1,0:T(8,128)(2,1)S(1)} collective-permute-done((bf16[128,2048]{1,0:T(8,128)(2,1)S(1)}, bf16[128,2048]{1,0:T(8,128)(2,1)S(1)}, u32[]{:S(2)}, u32[]{:S(2)}) %collective-permute-start.23) | collective-permute-done | bytes 524320 | tf_op jit(solution)/shard_map/ppermute | solution.py:142
  113.9 4.3 %collective-permute-start.24 = (bf16[128,2048]{1,0:T(8,128)(2,1)S(1)}, bf16[128,2048]{1,0:T(8,128)(2,1)S(1)}, u32[]{:S(2)}, u32[]{:S(2)}) collective-permute-start(bf16[128,2048]{1,0:T(8,128)(2,1)S(1)} %add_convert_fusion.6), channel_id=1, source_target_pairs={{0,24},{1,25},{2,26},{3,27},{4,28},{5,29},{6,30},{7,31},{8,0},{9,1... | collective-permute-start | bytes 1572872 | tf_op jit(solution)/shard_map/ppermute | solution.py:142
  118.7 1.0 collective-permute-start.4
  119.7 8.6 %collective-permute-done.24 = bf16[128,2048]{1,0:T(8,128)(2,1)S(1)} collective-permute-done((bf16[128,2048]{1,0:T(8,128)(2,1)S(1)}, bf16[128,2048]{1,0:T(8,128)(2,1)S(1)}, u32[]{:S(2)}, u32[]{:S(2)}) %collective-permute-start.24) | collective-permute-done | bytes 524320 | tf_op jit(solution)/shard_map/ppermute | solution.py:142
  128.5 4.3 %collective-permute-start.25 = (bf16[128,2048]{1,0:T(8,128)(2,1)S(1)}, bf16[128,2048]{1,0:T(8,128)(2,1)S(1)}, u32[]{:S(2)}, u32[]{:S(2)}) collective-permute-start(bf16[128,2048]{1,0:T(8,128)(2,1)S(1)} %add_convert_fusion.5), channel_id=1, source_target_pairs={{0,24},{1,25},{2,26},{3,27},{4,28},{5,29},{6,30},{7,31},{8,0},{9,1... | collective-permute-start | bytes 1572872 | tf_op jit(solution)/shard_map/ppermute | solution.py:142
  132.9 9.1 %collective-permute-done.25 = bf16[128,2048]{1,0:T(8,128)(2,1)S(1)} collective-permute-done((bf16[128,2048]{1,0:T(8,128)(2,1)S(1)}, bf16[128,2048]{1,0:T(8,128)(2,1)S(1)}, u32[]{:S(2)}, u32[]{:S(2)}) %collective-permute-start.25) | collective-permute-done | bytes 524320 | tf_op jit(solution)/shard_map/ppermute | solution.py:142
  142.5 6.2 %collective-permute-done.26 = bf16[64,2048]{1,0:T(8,128)(2,1)S(1)} collective-permute-done((bf16[64,2048]{1,0:T(8,128)(2,1)S(1)}, bf16[64,2048]{1,0:T(8,128)(2,1)S(1)}, u32[]{:S(2)}, u32[]{:S(2)}) %collective-permute-start.26) | collective-permute-done | bytes 262176 | tf_op jit(solution)/shard_map/ppermute | solution.py:142
  148.7 0.8 add_convert_fusion.8
  (59 shorter events, 9.5 us)
Async XLA Ops:
  0.0 4.4 %copy-start = (s32[128,6]{0,1:T(8,128)S(1)}, s32[128,6]{0,1:T(8,128)}, u32[]{:S(2)}) copy-start(s32[128,6]{0,1:T(8,128)} %param.11) | copy-start | bytes 9220
  0.0 10.2 %all-to-all-start = ((bf16[2,64,1024]{2,1,0:T(8,128)(2,1)}), bf16[2,64,1024]{2,1,0:T(8,128)(2,1)S(1)}, u32[]{:S(2)}, u32[]{:S(2)}) async-start(bf16[2,64,1024]{2,1,0:T(8,128)(2,1)} %bitcast.19), calls=%async_computation | async-start | bytes 524288 | tf_op jit(solution)/shard_map/all_to_all | solution.py:150
  10.2 1.0 copy-start.4
  11.2 0.7 copy-start.5
  12.2 10.8 %collective-permute-start.5 = (bf16[64,2176]{1,0:T(8,128)(2,1)S(1)}, bf16[64,2176]{1,0:T(8,128)(2,1)S(1)}, u32[]{:S(2)}, u32[]{:S(2)}) collective-permute-start(bf16[64,2176]{1,0:T(8,128)(2,1)S(1)} %get-tuple-element.16), channel_id=1, source_target_pairs={{0,24},{1,25},{2,26},{3,27},{4,28},{5,29},{6,30},{7,31},{8,0},{9,1... | collective-permute-start | bytes 835592 | tf_op jit(solution)/shard_map/ppermute | solution.py:142
  16.1 6.5 %collective-permute-start = (bf16[64,2176]{1,0:T(8,128)(2,1)S(1)}, bf16[64,2176]{1,0:T(8,128)(2,1)S(1)}, u32[]{:S(2)}, u32[]{:S(2)}) collective-permute-start(bf16[64,2176]{1,0:T(8,128)(2,1)S(1)} %get-tuple-element.16), channel_id=1, source_target_pairs={{0,4},{1,5},{2,3},{3,2},{4,0},{5,1},{6,7},{7,6},{8,12},{9,13},{10,... | collective-permute-start | bytes 835592 | tf_op jit(solution)/shard_map/ppermute | solution.py:142
  22.7 20.9 %collective-permute-start.1 = (bf16[128,2176]{1,0:T(8,128)(2,1)S(1)}, bf16[128,2176]{1,0:T(8,128)(2,1)S(1)}, u32[]{:S(2)}, u32[]{:S(2)}) collective-permute-start(bf16[128,2176]{1,0:T(8,128)(2,1)S(1)} %pad_maximum_fusion), channel_id=1, source_target_pairs={{0,1},{1,0},{2,6},{3,7},{4,5},{5,4},{6,2},{7,3},{8,9},{9,8},{10,14... | collective-permute-start | bytes 1671176 | tf_op jit(solution)/shard_map/ppermute | solution.py:142
  23.8 8.4 %collective-permute-start.18 = (bf16[64,2176]{1,0:T(8,128)(2,1)S(1)}, bf16[64,2176]{1,0:T(8,128)(2,1)S(1)}, u32[]{:S(2)}, u32[]{:S(2)}) collective-permute-start(bf16[64,2176]{1,0:T(8,128)(2,1)S(1)} %collective-permute-done.5), channel_id=1, source_target_pairs={{0,4},{1,5},{2,3},{3,2},{4,0},{5,1},{6,7},{7,6},{8,12},{9,13},{10,... | collective-permute-start | bytes 835592 | tf_op jit(solution)/shard_map/ppermute | solution.py:142
  25.3 7.6 %collective-permute-start.6 = (bf16[64,2176]{1,0:T(8,128)(2,1)S(1)}, bf16[64,2176]{1,0:T(8,128)(2,1)S(1)}, u32[]{:S(2)}, u32[]{:S(2)}) collective-permute-start(bf16[64,2176]{1,0:T(8,128)(2,1)S(1)} %collective-permute-done.5), channel_id=1, source_target_pairs={{0,24},{1,25},{2,26},{3,27},{4,28},{5,29},{6,30},{7,31},{8,0},{9,1... | collective-permute-start | bytes 835592 | tf_op jit(solution)/shard_map/ppermute | solution.py:142
  32.2 14.7 %collective-permute-start.19 = (bf16[128,2176]{1,0:T(8,128)(2,1)S(1)}, bf16[128,2176]{1,0:T(8,128)(2,1)S(1)}, u32[]{:S(2)}, u32[]{:S(2)}) collective-permute-start(bf16[128,2176]{1,0:T(8,128)(2,1)S(1)} %pad_maximum_fusion.3), channel_id=1, source_target_pairs={{0,1},{1,0},{2,6},{3,7},{4,5},{5,4},{6,2},{7,3},{8,9},{9,8},{10,14... | collective-permute-start | bytes 1671176 | tf_op jit(solution)/shard_map/ppermute | solution.py:142
  33.6 8.6 %collective-permute-start.13 = (bf16[64,2176]{1,0:T(8,128)(2,1)S(1)}, bf16[64,2176]{1,0:T(8,128)(2,1)S(1)}, u32[]{:S(2)}, u32[]{:S(2)}) collective-permute-start(bf16[64,2176]{1,0:T(8,128)(2,1)S(1)} %collective-permute-done.6), channel_id=1, source_target_pairs={{0,4},{1,5},{2,3},{3,2},{4,0},{5,1},{6,7},{7,6},{8,12},{9,13},{10,... | collective-permute-start | bytes 835592 | tf_op jit(solution)/shard_map/ppermute | solution.py:142
  35.3 9.2 %collective-permute-start.7 = (bf16[64,2176]{1,0:T(8,128)(2,1)S(1)}, bf16[64,2176]{1,0:T(8,128)(2,1)S(1)}, u32[]{:S(2)}, u32[]{:S(2)}) collective-permute-start(bf16[64,2176]{1,0:T(8,128)(2,1)S(1)} %collective-permute-done.6), channel_id=1, source_target_pairs={{0,24},{1,25},{2,26},{3,27},{4,28},{5,29},{6,30},{7,31},{8,0},{9,1... | collective-permute-start | bytes 835592 | tf_op jit(solution)/shard_map/ppermute | solution.py:142
  42.2 12.6 %collective-permute-start.14 = (bf16[128,2176]{1,0:T(8,128)(2,1)S(1)}, bf16[128,2176]{1,0:T(8,128)(2,1)S(1)}, u32[]{:S(2)}, u32[]{:S(2)}) collective-permute-start(bf16[128,2176]{1,0:T(8,128)(2,1)S(1)} %pad_maximum_fusion.2), channel_id=1, source_target_pairs={{0,1},{1,0},{2,6},{3,7},{4,5},{5,4},{6,2},{7,3},{8,9},{9,8},{10,14... | collective-permute-start | bytes 1671176 | tf_op jit(solution)/shard_map/ppermute | solution.py:142
  44.5 33.8 %collective-permute-start.2 = (bf16[256,2176]{1,0:T(8,128)(2,1)}, bf16[256,2176]{1,0:T(8,128)(2,1)}, u32[]{:S(2)}, u32[]{:S(2)}) collective-permute-start(bf16[256,2176]{1,0:T(8,128)(2,1)} %constant_dynamic-update-slice_fusion.own_ref), channel_id=1, source_target_pairs={{0,2},{1,3},{2,0},{3,1},{4,6},{5,7},{6,4},{7,5},{8,10},{9,11},{10,... | collective-permute-start | bytes 3342344 | tf_op jit(solution)/shard_map/ppermute | solution.py:142
  44.5 6.5 %collective-permute-start.8 = (bf16[64,2176]{1,0:T(8,128)(2,1)S(1)}, bf16[64,2176]{1,0:T(8,128)(2,1)S(1)}, u32[]{:S(2)}, u32[]{:S(2)}) collective-permute-start(bf16[64,2176]{1,0:T(8,128)(2,1)S(1)} %collective-permute-done.7), channel_id=1, source_target_pairs={{0,4},{1,5},{2,3},{3,2},{4,0},{5,1},{6,7},{7,6},{8,12},{9,13},{10,... | collective-permute-start | bytes 835592 | tf_op jit(solution)/shard_map/ppermute | solution.py:142
  47.8 15.3 %collective-permute-start.20 = (bf16[256,2176]{1,0:T(8,128)(2,1)}, bf16[256,2176]{1,0:T(8,128)(2,1)}, u32[]{:S(2)}, u32[]{:S(2)}) collective-permute-start(bf16[256,2176]{1,0:T(8,128)(2,1)} %constant_dynamic-update-slice_fusion.9.own_ref), channel_id=1, source_target_pairs={{0,2},{1,3},{2,0},{3,1},{4,6},{5,7},{6,4},{7,5},{8,10},{9,11},{10,... | collective-permute-start | bytes 3342344 | tf_op jit(solution)/shard_map/ppermute | solution.py:142
  51.0 12.0 %copy-start.1 = (bf16[1,704,2048]{2,1,0:T(8,128)(2,1)S(1)}, bf16[1,704,2048]{2,1,0:T(8,128)(2,1)}, u32[]{:S(2)}) copy-start(bf16[1,704,2048]{2,1,0:T(8,128)(2,1)} %param.13) | copy-start | bytes 8650756
  51.1 9.7 %collective-permute-start.9 = (bf16[128,2176]{1,0:T(8,128)(2,1)S(1)}, bf16[128,2176]{1,0:T(8,128)(2,1)S(1)}, u32[]{:S(2)}, u32[]{:S(2)}) collective-permute-start(bf16[128,2176]{1,0:T(8,128)(2,1)S(1)} %pad_maximum_fusion.1), channel_id=1, source_target_pairs={{0,1},{1,0},{2,6},{3,7},{4,5},{5,4},{6,2},{7,3},{8,9},{9,8},{10,14... | collective-permute-start | bytes 1671176 | tf_op jit(solution)/shard_map/ppermute | solution.py:142
  55.6 16.6 %collective-permute-start.15 = (bf16[256,2176]{1,0:T(8,128)(2,1)}, bf16[256,2176]{1,0:T(8,128)(2,1)}, u32[]{:S(2)}, u32[]{:S(2)}) collective-permute-start(bf16[256,2176]{1,0:T(8,128)(2,1)} %constant_dynamic-update-slice_fusion.6.own_ref), channel_id=1, source_target_pairs={{0,2},{1,3},{2,0},{3,1},{4,6},{5,7},{6,4},{7,5},{8,10},{9,11},{10,... | collective-permute-start | bytes 3342344 | tf_op jit(solution)/shard_map/ppermute | solution.py:142
  61.6 22.3 %collective-permute-start.10 = (bf16[256,2176]{1,0:T(8,128)(2,1)}, bf16[256,2176]{1,0:T(8,128)(2,1)}, u32[]{:S(2)}, u32[]{:S(2)}) collective-permute-start(bf16[256,2176]{1,0:T(8,128)(2,1)} %constant_dynamic-update-slice_fusion.3.own_ref), channel_id=1, source_target_pairs={{0,2},{1,3},{2,0},{3,1},{4,6},{5,7},{6,4},{7,5},{8,10},{9,11},{10,... | collective-permute-start | bytes 3342344 | tf_op jit(solution)/shard_map/ppermute | solution.py:142
  63.1 1.8 %copy-start.2 = (bf16[1,704,2048]{2,1,0:T(8,128)(2,1)S(1)}, bf16[1,704,2048]{2,1,0:T(8,128)(2,1)}, u32[]{:S(2)}) copy-start(bf16[1,704,2048]{2,1,0:T(8,128)(2,1)} %param.14) | copy-start | bytes 8650756
  64.9 1.8 %copy-start.3 = (bf16[1,704,2048]{2,1,0:T(8,128)(2,1)S(1)}, bf16[1,704,2048]{2,1,0:T(8,128)(2,1)}, u32[]{:S(2)}) copy-start(bf16[1,704,2048]{2,1,0:T(8,128)(2,1)} %param.15) | copy-start | bytes 8650756
  72.2 17.9 %collective-permute-start.21 = (bf16[256,2048]{1,0:T(8,128)(2,1)S(1)}, bf16[256,2048]{1,0:T(8,128)(2,1)S(1)}, u32[]{:S(2)}, u32[]{:S(2)}) collective-permute-start(bf16[256,2048]{1,0:T(8,128)(2,1)S(1)} %get-tuple-element.24), channel_id=1, source_target_pairs={{0,2},{1,3},{2,0},{3,1},{4,6},{5,7},{6,4},{7,5},{8,10},{9,11},{10,... | collective-permute-start | bytes 3145736 | tf_op jit(solution)/shard_map/ppermute | solution.py:142
  77.8 13.5 %collective-permute-start.16 = (bf16[256,2048]{1,0:T(8,128)(2,1)S(1)}, bf16[256,2048]{1,0:T(8,128)(2,1)S(1)}, u32[]{:S(2)}, u32[]{:S(2)}) collective-permute-start(bf16[256,2048]{1,0:T(8,128)(2,1)S(1)} %get-tuple-element.22), channel_id=1, source_target_pairs={{0,2},{1,3},{2,0},{3,1},{4,6},{5,7},{6,4},{7,5},{8,10},{9,11},{10,... | collective-permute-start | bytes 3145736 | tf_op jit(solution)/shard_map/ppermute | solution.py:142
  83.8 34.5 %collective-permute-start.3 = (bf16[256,2048]{1,0:T(8,128)(2,1)S(1)}, bf16[256,2048]{1,0:T(8,128)(2,1)S(1)}, u32[]{:S(2)}, u32[]{:S(2)}) collective-permute-start(bf16[256,2048]{1,0:T(8,128)(2,1)S(1)} %get-tuple-element.18), channel_id=1, source_target_pairs={{0,2},{1,3},{2,0},{3,1},{4,6},{5,7},{6,4},{7,5},{8,10},{9,11},{10,... | collective-permute-start | bytes 3145736 | tf_op jit(solution)/shard_map/ppermute | solution.py:142
  89.5 13.2 %collective-permute-start.11 = (bf16[256,2048]{1,0:T(8,128)(2,1)S(1)}, bf16[256,2048]{1,0:T(8,128)(2,1)S(1)}, u32[]{:S(2)}, u32[]{:S(2)}) collective-permute-start(bf16[256,2048]{1,0:T(8,128)(2,1)S(1)} %get-tuple-element.20), channel_id=1, source_target_pairs={{0,2},{1,3},{2,0},{3,1},{4,6},{5,7},{6,4},{7,5},{8,10},{9,11},{10,... | collective-permute-start | bytes 3145736 | tf_op jit(solution)/shard_map/ppermute | solution.py:142
  90.5 9.2 %collective-permute-start.22 = (bf16[128,2048]{1,0:T(8,128)(2,1)S(1)}, bf16[128,2048]{1,0:T(8,128)(2,1)S(1)}, u32[]{:S(2)}, u32[]{:S(2)}) collective-permute-start(bf16[128,2048]{1,0:T(8,128)(2,1)S(1)} %slice.47), channel_id=1, source_target_pairs={{0,1},{1,0},{2,6},{3,7},{4,5},{5,4},{6,2},{7,3},{8,9},{9,8},{10,14... | collective-permute-start | bytes 1572872 | tf_op jit(solution)/shard_map/ppermute | solution.py:142
  91.7 13.7 %collective-permute-start.17 = (bf16[128,2048]{1,0:T(8,128)(2,1)S(1)}, bf16[128,2048]{1,0:T(8,128)(2,1)S(1)}, u32[]{:S(2)}, u32[]{:S(2)}) collective-permute-start(bf16[128,2048]{1,0:T(8,128)(2,1)S(1)} %slice.45), channel_id=1, source_target_pairs={{0,1},{1,0},{2,6},{3,7},{4,5},{5,4},{6,2},{7,3},{8,9},{9,8},{10,14... | collective-permute-start | bytes 1572872 | tf_op jit(solution)/shard_map/ppermute | solution.py:142
  99.9 13.7 %collective-permute-start.23 = (bf16[128,2048]{1,0:T(8,128)(2,1)S(1)}, bf16[128,2048]{1,0:T(8,128)(2,1)S(1)}, u32[]{:S(2)}, u32[]{:S(2)}) collective-permute-start(bf16[128,2048]{1,0:T(8,128)(2,1)S(1)} %add_convert_fusion.7), channel_id=1, source_target_pairs={{0,24},{1,25},{2,26},{3,27},{4,28},{5,29},{6,30},{7,31},{8,0},{9,1... | collective-permute-start | bytes 1572872 | tf_op jit(solution)/shard_map/ppermute | solution.py:142
  103.1 16.5 %collective-permute-start.12 = (bf16[128,2048]{1,0:T(8,128)(2,1)S(1)}, bf16[128,2048]{1,0:T(8,128)(2,1)S(1)}, u32[]{:S(2)}, u32[]{:S(2)}) collective-permute-start(bf16[128,2048]{1,0:T(8,128)(2,1)S(1)} %slice.43), channel_id=1, source_target_pairs={{0,1},{1,0},{2,6},{3,7},{4,5},{5,4},{6,2},{7,3},{8,9},{9,8},{10,14... | collective-permute-start | bytes 1572872 | tf_op jit(solution)/shard_map/ppermute | solution.py:142
  113.9 14.4 %collective-permute-start.24 = (bf16[128,2048]{1,0:T(8,128)(2,1)S(1)}, bf16[128,2048]{1,0:T(8,128)(2,1)S(1)}, u32[]{:S(2)}, u32[]{:S(2)}) collective-permute-start(bf16[128,2048]{1,0:T(8,128)(2,1)S(1)} %add_convert_fusion.6), channel_id=1, source_target_pairs={{0,24},{1,25},{2,26},{3,27},{4,28},{5,29},{6,30},{7,31},{8,0},{9,1... | collective-permute-start | bytes 1572872 | tf_op jit(solution)/shard_map/ppermute | solution.py:142
  118.7 14.2 %collective-permute-start.4 = (bf16[128,2048]{1,0:T(8,128)(2,1)S(1)}, bf16[128,2048]{1,0:T(8,128)(2,1)S(1)}, u32[]{:S(2)}, u32[]{:S(2)}) collective-permute-start(bf16[128,2048]{1,0:T(8,128)(2,1)S(1)} %slice.41), channel_id=1, source_target_pairs={{0,1},{1,0},{2,6},{3,7},{4,5},{5,4},{6,2},{7,3},{8,9},{9,8},{10,14... | collective-permute-start | bytes 1572872 | tf_op jit(solution)/shard_map/ppermute | solution.py:142
  128.5 13.5 %collective-permute-start.25 = (bf16[128,2048]{1,0:T(8,128)(2,1)S(1)}, bf16[128,2048]{1,0:T(8,128)(2,1)S(1)}, u32[]{:S(2)}, u32[]{:S(2)}) collective-permute-start(bf16[128,2048]{1,0:T(8,128)(2,1)S(1)} %add_convert_fusion.5), channel_id=1, source_target_pairs={{0,24},{1,25},{2,26},{3,27},{4,28},{5,29},{6,30},{7,31},{8,0},{9,1... | collective-permute-start | bytes 1572872 | tf_op jit(solution)/shard_map/ppermute | solution.py:142
  142.3 6.4 %collective-permute-start.26 = (bf16[64,2048]{1,0:T(8,128)(2,1)S(1)}, bf16[64,2048]{1,0:T(8,128)(2,1)S(1)}, u32[]{:S(2)}, u32[]{:S(2)}) collective-permute-start(bf16[64,2048]{1,0:T(8,128)(2,1)S(1)} %slice.49), channel_id=1, source_target_pairs={{0,4},{1,5},{2,3},{3,2},{4,0},{5,1},{6,7},{7,6},{8,12},{9,13},{10,... | collective-permute-start | bytes 786440 | tf_op jit(solution)/shard_map/ppermute | solution.py:142

commit v3 on v2

--- a/solution.py
+++ b/solution.py
@@ -43,25 +43,28 @@
     return lax.dot_general(a, b, (((a_dim,), (b_dim,)), ((), ())), preferred_element_type=F32)
 
 
-def front_kernel(cols_ref, resid_ref, gain_ref, ids_ref, gates_ref, packed_ref, hidden_ref):
-    shares, rows, columns = cols_ref.shape
-    width = resid_ref.shape[1]
-    attn = jnp.concatenate([cols_ref[i] for i in range(shares)], axis=1)
+def front_kernel(half_ref, attn_ref, came_ref, resid_ref, gain_ref, ids_ref, gates_ref, packed_ref, hidden_ref):
+    rows, width = resid_ref.shape
+    half = half_ref[0]
+    mine = pl.ds(pl.multiple_of(half * rows, rows), rows)
+    kept, came = attn_ref[mine, :], came_ref[...]
+    attn = jnp.concatenate([jnp.where(half == 0, kept, came), jnp.where(half == 0, came, kept)], axis=1)
     hidden_state = (resid_ref[...].astype(F32) + attn.astype(F32)).astype(BF16)
     hidden_ref[...] = hidden_state
     hidden = hidden_state.astype(F32)
     mean_sq = jnp.mean(hidden * hidden, axis=1, keepdims=True)
     packed_ref[:, :width] = (hidden * lax.rsqrt(mean_sq + 1e-05) * gain_ref[...]).astype(BF16)
     lane = lax.broadcasted_iota(jnp.int32, (rows, LANES), 1)
+    ids, gates = ids_ref[mine, :], gates_ref[mine, :]
     weight = jnp.zeros((rows, LANES), F32)
-    for k in range(ids_ref.shape[1]):
-        hit = lane % (LANES // 2) == ids_ref[:, k : k + 1]
-        weight = weight + jnp.where(hit, gates_ref[:, k : k + 1], 0.0)
+    for k in range(ids.shape[1]):
+        hit = lane % (LANES // 2) == ids[:, k : k + 1]
+        weight = weight + jnp.where(hit, gates[:, k : k + 1], 0.0)
     high = weight.astype(BF16).astype(F32)
     packed_ref[:, width:] = jnp.where(lane < LANES // 2, high, weight - high).astype(BF16)
 
 
-def front(cols, resid, norm_gain, ids, gates):
+def front(half, attn_out, came, resid, norm_gain, ids, gates):
     rows, width = resid.shape
     return pl.pallas_call(
         front_kernel,
@@ -69,14 +72,14 @@
             jax.ShapeDtypeStruct((rows, width + LANES), BF16),
             jax.ShapeDtypeStruct((rows, width), BF16),
         ),
-        in_specs=[VMEM] * 5,
+        in_specs=[SMEM] + [VMEM] * 6,
         out_specs=(VMEM, VMEM),
         compiler_params=pltpu.CompilerParams(vmem_limit_bytes=8 * 2**20),
-    )(cols, resid, norm_gain.reshape(1, -1), ids, gates)
-
-
-def expert_kernel(me_ref, own_ref, sib_ref, gate_ref, up_ref, down_ref, own_out, sib_out, rows, act):
-    count = own_ref.shape[0]
+    )(half.reshape(1), attn_out, came, resid, norm_gain.reshape(1, -1), ids, gates)
+
+
+def expert_kernel(me_ref, own_a, own_b, sib_a, sib_b, gate_ref, up_ref, down_ref, own_out, sib_out, rows, act):
+    count = 2 * own_a.shape[0]
     hidden_units, width = down_ref.shape
     slots = count // 2
     me = me_ref[0]
@@ -85,20 +88,21 @@
     earlier = jnp.where(column < row, 1.0, 0.0).astype(BF16)
     slot = lax.broadcasted_iota(jnp.int32, (count, slots), 1).astype(F32)
 
-    def placing(source):
-        routing = source[:, width:].astype(F32)
+    def placing(*halves):
+        routing = jnp.concatenate([h[:, width:] for h in halves], axis=0).astype(F32)
         lane = lax.broadcasted_iota(jnp.int32, routing.shape, 1)
         weight = jnp.sum(jnp.where(lane % (LANES // 2) == me, routing, 0.0), axis=1, keepdims=True)
         chosen = jnp.broadcast_to(jnp.where(weight != 0, 1.0, 0.0), (count, slots))
         rank = product(earlier, chosen.astype(BF16), 1, 0)
         return jnp.where(rank == slot, chosen, 0.0).astype(BF16), weight
 
-    place_own, weight_own = placing(own_ref)
-    place_sib, weight_sib = placing(sib_ref)
+    place_own, weight_own = placing(own_a, own_b)
+    place_sib, weight_sib = placing(sib_a, sib_b)
     for start, size in tiles(width, 512):
         part = slice(start, start + size)
-        rows[:slots, part] = product(place_own, own_ref[:, part], 0, 0).astype(BF16)
-        rows[slots:, part] = product(place_sib, sib_ref[:, part], 0, 0).astype(BF16)
+        for place, a, b, into in ((place_own, own_a, own_b, 0), (place_sib, sib_a, sib_b, slots)):
+            both = jnp.concatenate([a[:, part], b[:, part]], axis=0)
+            rows[into : into + slots, part] = product(place, both, 0, 0).astype(BF16)
     for start, size in tiles(hidden_units, 256):
         part = slice(start, start + size)
         gate_pre = product(rows[...], gate_ref[part, :], 1, 1)
@@ -112,26 +116,27 @@
 
 
 def experts(me, own, sib, w_gate, w_up, w_down):
-    count = own.shape[0]
+    count = 2 * own[0].shape[0]
     hidden_units, width = w_down.shape
     result = jax.ShapeDtypeStruct((count, width), BF16)
     return pl.pallas_call(
         expert_kernel,
         out_shape=(result, result),
-        in_specs=[SMEM] + [VMEM] * 5,
+        in_specs=[SMEM] + [VMEM] * 7,
         out_specs=(VMEM, VMEM),
         scratch_shapes=[pltpu.VMEM((count, width), BF16), pltpu.VMEM((count, hidden_units), BF16)],
-        compiler_params=pltpu.CompilerParams(vmem_limit_bytes=30 * 2**20),
+        compiler_params=pltpu.CompilerParams(vmem_limit_bytes=16 * 2**20),
         cost_estimate=pl.CostEstimate(
             flops=6 * count * width * hidden_units, bytes_accessed=8 * count * width, transcendentals=0
         ),
-    )(me, own, sib, w_gate, w_up, w_down)
+    )(me, *own, *sib, w_gate, w_up, w_down)
 
 
 def gathered_plan(ep_count, attn_out, resid, norm_gain, expert_ids, gate_vals, w_gate, w_up, w_down):
     planes = ep_count // 4
     my_rows = resid.shape[0]
     half = lax.axis_index("tp")
+    me = lax.axis_index("ep").reshape(1)
 
     def routes(move):
         pairs = []
@@ -144,35 +149,89 @@
     first = routes(lambda z, x, c, y: (z, x, c, 1 - y) if c else (z, 1 - x, c, y))
     second = routes(lambda z, x, c, y: (z, 1 - x, c, y) if c else (z, x, c, 1 - y))
     sibling = routes(lambda z, x, c, y: (z, x, 1 - c, y))
-    down = routes(lambda z, x, c, y: ((z - 1) % planes, x, c, y))
-
-    cols = attn_out.reshape(2, my_rows, -1)
-    cols = lax.all_to_all(cols, "tp", split_axis=0, concat_axis=0, tiled=True)
-    ids = lax.dynamic_slice_in_dim(expert_ids, half * my_rows, my_rows, 0)
-    gates = lax.dynamic_slice_in_dim(gate_vals, half * my_rows, my_rows, 0)
-    packed, hidden = front(cols, resid, norm_gain, ids, gates)
-    me = lax.axis_index("ep").reshape(1)
-
-    def gather_plane(piece):
-        two = jnp.concatenate([piece, first(piece)], axis=0)
-        own = jnp.concatenate([two, second(two)], axis=0)
-        return own, sibling(own)
+    partner = routes(lambda z, x, c, y: (z, x, c, 1 - y))
+    ring = list(range(0, planes, 2)) + list(range(1, planes, 2))[::-1]
+    after = {z: ring[i - 1] for i, z in enumerate(ring)}
+    down = routes(lambda z, x, c, y: (after[z], x, c, y))
 
     def add(*terms):
         return functools.reduce(lambda a, b: a + b, [t.astype(F32) for t in terms])
 
-    pieces = [packed]
-    for _ in range(planes - 1):
-        pieces.append(down(pieces[-1]))
-    gathered = [gather_plane(piece) for piece in pieces]
-    carried = []
-    for step in list(range(1, planes)) + [0]:
-        out_own, out_sib = experts(me, *gathered[step], w_gate[0], w_up[0], w_down[0])
-        total = add(out_own, sibling(out_sib)).astype(BF16)
-        kept = add(total[: 2 * my_rows], second(total[2 * my_rows :]), *carried).astype(BF16)
+    last = []
+
+    def in_turn(value):
+        if last:
+            value, _ = lax.optimization_barrier((value, last[0]))
+        last[:] = [value]
+        return value
+
+    theirs = lax.dynamic_slice_in_dim(attn_out, (1 - half) * my_rows, my_rows, 0)
+    packed, hidden = front(half, attn_out, partner(theirs), resid, norm_gain, expert_ids, gate_vals)
+
+    piece, two, one, other, came, out, total, kept, home = ({} for _ in range(9))
+
+    def spread(step):
         if step:
-            carried = [down(kept)]
-    return add(hidden, kept[:my_rows], first(kept[my_rows:])).astype(BF16)
+            piece[step] = down(piece[step - 1])
+        else:
+            piece[0] = packed
+        piece[step] = in_turn(piece[step])
+        one[step] = first(piece[step])
+
+    def widen(step):
+        two[step] = in_turn(jnp.concatenate([piece[step], one[step]], axis=0))
+        other[step] = second(two[step])
+        came[step] = [sibling(two[step])]
+
+    def share(step):
+        other[step], came[step][0] = in_turn((other[step], came[step][0]))
+        came[step].append(sibling(other[step]))
+
+    def run(step):
+        own, sib = in_turn(([two[step], other[step]], came[step]))
+        out[step] = in_turn(experts(me, own, sib, w_gate[0], w_up[0], w_down[0]))
+        came[step] = sibling(out[step][1])
+
+    def merge_cores(step):
+        total[step] = in_turn(add(out[step][0], came[step]).astype(BF16))
+        other[step] = second(total[step][2 * my_rows :])
+
+    def merge_second(step):
+        kept[step] = in_turn(add(total[step][: 2 * my_rows], other[step]).astype(BF16))
+        one[step] = first(kept[step][my_rows:])
+
+    def merge_first(step):
+        terms = [kept[step][:my_rows], one[step]] + ([home[step - 1]] if step > 1 else [])
+        home[step] = down(in_turn(add(*terms).astype(BF16)))
+
+    spread(0)
+    spread(1)
+    widen(0)
+    widen(1)
+    spread(2)
+    share(0)
+    widen(2)
+    spread(3)
+    share(1)
+    run(1)
+    widen(3)
+    share(2)
+    run(2)
+    share(3)
+    merge_cores(1)
+    run(3)
+    merge_cores(2)
+    merge_second(1)
+    run(0)
+    merge_cores(3)
+    merge_second(2)
+    merge_first(1)
+    merge_cores(0)
+    merge_second(3)
+    merge_first(2)
+    merge_second(0)
+    merge_first(3)
+    return add(hidden, kept[0][:my_rows], one[0], home[planes - 1]).astype(BF16)
 
 
 def exchanged_plan(ep_count, attn_out, resid, norm_gain, expert_ids, gate_vals, w_gate, w_up, w_down):

time: 150 us -> 128 us (0.85)
  starting transfers between devices: 40.1 us -> 31.6 us
  waiting for transfers between devices: 67.6 us -> 59.8 us
  Pallas kernels: 22.4 us -> 17.4 us
  local copies, waits for them, and re-layouts: 15.9 us -> 13.5 us
  other arithmetic: 3.36 us -> 5.19 us
    pallas_call x4, Pallas kernels: 22 us -> 17.1 us  [experts(): pl.pallas_call(expert_kernel, out_shape=(result, result), in_specs=[SMEM]...]
    all_to_all x1 -> x0, waiting for transfers between devices: 4.84 us -> none  [gathered_plan(): cols = lax.all_to_all(cols, 'tp', split_axis=0, concat_axis=0, tiled=True)]
    all_to_all x1 -> x0, starting transfers between devices: 4.37 us -> none  [gathered_plan(): cols = lax.all_to_all(cols, 'tp', split_axis=0, concat_axis=0, tiled=True)]
    ppermute x27 -> x35, starting transfers between devices: 35.7 us -> 31.6 us  [routes(): return lambda a: lax.ppermute(a, AXES, pairs)]
    concatenate x4 -> x0, local copies, waits for them, and re-layouts: 3.48 us -> none  [gather_plane(): own = jnp.concatenate([two, second(two)], axis=0)]
    ppermute x27 -> x35, waiting for transfers between devices: 62.8 us -> 59.8 us  [routes(): return lambda a: lax.ppermute(a, AXES, pairs)]
    concatenate x4, other arithmetic: 0.16 us -> 2.01 us  [widen(): two[step] = in_turn(jnp.concatenate([piece[step], one[step]], axis=0))]
    unnamed x22 -> x38, local copies, waits for them, and re-layouts: 11.4 us -> 12.4 us
  transfers between devices with their start and end apart: 28 -> 35, of which waited for: 13 -> 19; matrix products, arithmetic and copies ran while one was open for 9% -> 5% of each run, Pallas kernels for 15% -> 13%
where the time goes in v3:
time: 128 us
  waiting for transfers between devices  59.8 us (47%)
  starting transfers between devices  31.6 us (25%)
  Pallas kernels  17.4 us (14%)
  local copies, waits for them, and re-layouts  13.5 us (11%)
  other arithmetic  5.19 us (4%)
    ppermute x35, waiting for transfers between devices, routes(): return lambda a: lax.ppermute(a, AXES, pairs)  59.8 us
    ppermute x35, starting transfers between devices, routes(): return lambda a: lax.ppermute(a, AXES, pairs)  31.6 us
    pallas_call x4, Pallas kernels, experts(): pl.pallas_call(expert_kernel, out_shape=(result, result), in_specs=[SMEM]...  17.1 us
    unnamed x38, local copies, waits for them, and re-layouts  12.4 us
  transfers between devices with their start and end apart: 35, of which 19 were waited for; matrix products, arithmetic and copies ran while one was open for 5% of the time, Pallas kernels for 13%

profile of v3, /device:TPU:0, one launch (start us, length us, event | category | flops | bytes accessed | tf_op | source)
XLA Modules:
  0.0 127.8 jit_solution(11228811972429721785)
XLA Ops:
  0.0 0.9 constant_dynamic-slice_fusion
  0.9 3.0 %collective-permute-start = (bf16[64,1024]{1,0:T(8,128)(2,1)S(1)}, bf16[64,1024]{1,0:T(8,128)(2,1)S(1)}, u32[]{:S(2)}, u32[]{:S(2)}) collective-permute-start(bf16[64,1024]{1,0:T(8,128)(2,1)S(1)} %constant_dynamic-slice_fusion), channel_id=1, source_target_pairs={{0,1},{1,0},{2,3},{3,2},{4,5},{5,4},{6,7},{7,6},{8,9},{9,8},{10,11... | collective-permute-start | bytes 393224 | tf_op jit(solution)/shard_map/ppermute | solution.py:147
  4.7 0.9 copy.10.gates_ref
  5.7 1.8 %collective-permute-done.came_ref = bf16[64,1024]{1,0:T(8,128)(2,1)S(1)} collective-permute-done((bf16[64,1024]{1,0:T(8,128)(2,1)S(1)}, bf16[64,1024]{1,0:T(8,128)(2,1)S(1)}, u32[]{:S(2)}, u32[]{:S(2)}) %collective-permute-start) | collective-permute-done | bytes 131104 | tf_op jit(solution)/shard_map/ppermute | solution.py:147
  7.4 0.9 copy-done.7
  8.4 0.9 copy-done.16
  11.1 1.8 %collective-permute-start.2 = (bf16[64,2176]{1,0:T(8,128)(2,1)S(1)}, bf16[64,2176]{1,0:T(8,128)(2,1)S(1)}, u32[]{:S(2)}, u32[]{:S(2)}) collective-permute-start(bf16[64,2176]{1,0:T(8,128)(2,1)S(1)} %get-tuple-element.66), channel_id=1, source_target_pairs={{0,8},{1,9},{2,10},{3,11},{4,12},{5,13},{6,14},{7,15},{8,24},{9,25... | collective-permute-start | bytes 835592 | tf_op jit(solution)/shard_map/ppermute | solution.py:147
  12.9 1.5 %collective-permute-start.1 = (bf16[64,2176]{1,0:T(8,128)(2,1)S(1)}, bf16[64,2176]{1,0:T(8,128)(2,1)S(1)}, u32[]{:S(2)}, u32[]{:S(2)}) collective-permute-start(bf16[64,2176]{1,0:T(8,128)(2,1)S(1)} %get-tuple-element.66), channel_id=1, source_target_pairs={{0,4},{1,5},{2,3},{3,2},{4,0},{5,1},{6,7},{7,6},{8,12},{9,13},{10,... | collective-permute-start | bytes 835592 | tf_op jit(solution)/shard_map/ppermute | solution.py:147
  14.4 5.5 %collective-permute-done.2 = bf16[64,2176]{1,0:T(8,128)(2,1)S(1)} collective-permute-done((bf16[64,2176]{1,0:T(8,128)(2,1)S(1)}, bf16[64,2176]{1,0:T(8,128)(2,1)S(1)}, u32[]{:S(2)}, u32[]{:S(2)}) %collective-permute-start.2) | collective-permute-done | bytes 278560 | tf_op jit(solution)/shard_map/ppermute | solution.py:147
  19.9 1.4 %collective-permute-start.6 = (bf16[64,2176]{1,0:T(8,128)(2,1)S(1)}, bf16[64,2176]{1,0:T(8,128)(2,1)S(1)}, u32[]{:S(2)}, u32[]{:S(2)}) collective-permute-start(bf16[64,2176]{1,0:T(8,128)(2,1)S(1)} %collective-permute-done.2), channel_id=1, source_target_pairs={{0,4},{1,5},{2,3},{3,2},{4,0},{5,1},{6,7},{7,6},{8,12},{9,13},{10,... | collective-permute-start | bytes 835592 | tf_op jit(solution)/shard_map/ppermute | solution.py:147
  22.1 1.6 %collective-permute-start.3 = (bf16[128,2176]{1,0:T(8,128)(2,1)S(1)}, bf16[128,2176]{1,0:T(8,128)(2,1)S(1)}, u32[]{:S(2)}, u32[]{:S(2)}) collective-permute-start(bf16[128,2176]{1,0:T(8,128)(2,1)S(1)} %pad_maximum_fusion.own_a), channel_id=1, source_target_pairs={{0,1},{1,0},{2,6},{3,7},{4,5},{5,4},{6,2},{7,3},{8,9},{9,8},{10,14... | collective-permute-start | bytes 1671176 | tf_op jit(solution)/shard_map/ppermute | solution.py:147
  23.7 5.7 %collective-permute-done.6 = bf16[64,2176]{1,0:T(8,128)(2,1)S(1)} collective-permute-done((bf16[64,2176]{1,0:T(8,128)(2,1)S(1)}, bf16[64,2176]{1,0:T(8,128)(2,1)S(1)}, u32[]{:S(2)}, u32[]{:S(2)}) %collective-permute-start.6) | collective-permute-done | bytes 278560 | tf_op jit(solution)/shard_map/ppermute | solution.py:147
  29.5 1.4 %collective-permute-start.11 = (bf16[64,2176]{1,0:T(8,128)(2,1)S(1)}, bf16[64,2176]{1,0:T(8,128)(2,1)S(1)}, u32[]{:S(2)}, u32[]{:S(2)}) collective-permute-start(bf16[64,2176]{1,0:T(8,128)(2,1)S(1)} %collective-permute-done.5), channel_id=1, source_target_pairs={{0,4},{1,5},{2,3},{3,2},{4,0},{5,1},{6,7},{7,6},{8,12},{9,13},{10,... | collective-permute-start | bytes 835592 | tf_op jit(solution)/shard_map/ppermute | solution.py:147
  30.9 1.6 %collective-permute-start.8 = (bf16[128,2176]{1,0:T(8,128)(2,1)S(1)}, bf16[128,2176]{1,0:T(8,128)(2,1)}, u32[]{:S(2)}, u32[]{:S(2)}) collective-permute-start(bf16[128,2176]{1,0:T(8,128)(2,1)S(1)} %pad_maximum_fusion.1.own_a), channel_id=1, source_target_pairs={{0,1},{1,0},{2,6},{3,7},{4,5},{5,4},{6,2},{7,3},{8,9},{9,8},{10,14... | collective-permute-start | bytes 1671176 | tf_op jit(solution)/shard_map/ppermute | solution.py:147
  33.3 1.4 %collective-permute-done.3.own_b = bf16[128,2176]{1,0:T(8,128)(2,1)S(1)} collective-permute-done((bf16[128,2176]{1,0:T(8,128)(2,1)S(1)}, bf16[128,2176]{1,0:T(8,128)(2,1)S(1)}, u32[]{:S(2)}, u32[]{:S(2)}) %collective-permute-start.3) | collective-permute-done | bytes 557088 | tf_op jit(solution)/shard_map/ppermute | solution.py:147
  34.7 3.4 %collective-permute-start.10 = (bf16[64,2176]{1,0:T(8,128)(2,1)S(1)}, bf16[64,2176]{1,0:T(8,128)(2,1)}, u32[]{:S(2)}, u32[]{:S(2)}) collective-permute-start(bf16[64,2176]{1,0:T(8,128)(2,1)S(1)} %collective-permute-done.5), channel_id=1, source_target_pairs={{0,8},{1,9},{2,10},{3,11},{4,12},{5,13},{6,14},{7,15},{8,24},{9,25... | collective-permute-start | bytes 835592 | tf_op jit(solution)/shard_map/ppermute | solution.py:147
  38.1 1.1 collective-permute-done.11
  39.1 0.9 pad_maximum_fusion.2.own_a
  40.0 3.4 %collective-permute-done.10 = bf16[64,2176]{1,0:T(8,128)(2,1)} collective-permute-done((bf16[64,2176]{1,0:T(8,128)(2,1)S(1)}, bf16[64,2176]{1,0:T(8,128)(2,1)}, u32[]{:S(2)}, u32[]{:S(2)}) %collective-permute-start.10) | collective-permute-done | bytes 278560 | tf_op jit(solution)/shard_map/ppermute | solution.py:147
  43.4 0.8 copy-done.12
  45.3 1.2 collective-permute-done.12.sib_b
  46.5 1.8 %copy-done.1 = bf16[1,704,2048]{2,1,0:T(8,128)(2,1)S(1)} copy-done((bf16[1,704,2048]{2,1,0:T(8,128)(2,1)S(1)}, bf16[1,704,2048]{2,1,0:T(8,128)(2,1)}, u32[]{:S(2)}) %copy-start.1) | copy-done | bytes 2883608
  48.3 1.8 %copy-done.3 = bf16[1,704,2048]{2,1,0:T(8,128)(2,1)S(1)} copy-done((bf16[1,704,2048]{2,1,0:T(8,128)(2,1)S(1)}, bf16[1,704,2048]{2,1,0:T(8,128)(2,1)}, u32[]{:S(2)}) %copy-start.3) | copy-done | bytes 2883608
  50.1 1.1 copy-done.6
  51.2 1.1 copy-done.13
  52.2 5.2 %shard_map.83 = (bf16[256,2048]{1,0:T(8,128)(2,1)S(1)}, bf16[256,2048]{1,0:T(8,128)(2,1)S(1)}) custom-call(s32[1]{0:T(128)} %bitcast.2.me_ref, bf16[128,2176]{1,0:T(8,128)(2,1)S(1)} %copy-done.6, bf16[128,2176]{1,0:T(8,128)(2,1)} %collective-permute-done.8.own_b, bf16[128,2176]{1,0:T(8,128)(2,1)S(1)} %copy-done.13, ...), custom_call_target="tpu_custom_call" | custom-call | flops 2214592512 | bytes 4194304 | tf_op jit(solution)/shard_map/pallas_call | solution.py:122
  57.6 1.1 pad_maximum_fusion.3.own_a
  59.6 1.3 %collective-permute-done.19.sib_b = bf16[128,2176]{1,0:T(8,128)(2,1)S(1)} collective-permute-done((bf16[128,2176]{1,0:T(8,128)(2,1)S(1)}, bf16[128,2176]{1,0:T(8,128)(2,1)S(1)}, u32[]{:S(2)}, u32[]{:S(2)}) %collective-permute-start.19) | collective-permute-done | bytes 557088 | tf_op jit(solution)/shard_map/ppermute | solution.py:147
  61.0 3.9 %shard_map.84 = (bf16[256,2048]{1,0:T(8,128)(2,1)S(1)}, bf16[256,2048]{1,0:T(8,128)(2,1)S(1)}) custom-call(s32[1]{0:T(128)} %bitcast.2.me_ref, bf16[128,2176]{1,0:T(8,128)(2,1)S(1)} %copy-done.4, bf16[128,2176]{1,0:T(8,128)(2,1)S(1)} %collective-permute-done.17.own_b, bf16[128,2176]{1,0:T(8,128)(2,1)S(1)} %collective-permute-done.18.sib_a, ...), custom_call_target="tpu_custom_call" | custom-call | flops 2214592512 | bytes 4194304 | tf_op jit(solution)/shard_map/pallas_call | solution.py:122
  65.1 3.6 %collective-permute-done.15.own_b = bf16[128,2176]{1,0:T(8,128)(2,1)S(1)} collective-permute-done((bf16[128,2176]{1,0:T(8,128)(2,1)S(1)}, bf16[128,2176]{1,0:T(8,128)(2,1)S(1)}, u32[]{:S(2)}, u32[]{:S(2)}) %collective-permute-start.15) | collective-permute-done | bytes 557088 | tf_op jit(solution)/shard_map/ppermute | solution.py:147
  70.7 3.9 %shard_map.85 = (bf16[256,2048]{1,0:T(8,128)(2,1)S(1)}, bf16[256,2048]{1,0:T(8,128)(2,1)S(1)}) custom-call(s32[1]{0:T(128)} %bitcast.2.me_ref, bf16[128,2176]{1,0:T(8,128)(2,1)S(1)} %pad_maximum_fusion.3.own_a, bf16[128,2176]{1,0:T(8,128)(2,1)S(1)} %collective-permute-done.15.own_b, bf16[128,2176]{1,0:T(8,128)(2,1)S(1)} %collective-permute-done.16.sib_a, ...), custom_call_target="tpu_custom_call" | custom-call | flops 2214592512 | bytes 4194304 | tf_op jit(solution)/shard_map/pallas_call | solution.py:122
  74.6 3.8 %collective-permute-done.20 = bf16[128,2048]{1,0:T(8,128)(2,1)S(1)} collective-permute-done((bf16[128,2048]{1,0:T(8,128)(2,1)S(1)}, bf16[128,2048]{1,0:T(8,128)(2,1)S(1)}, u32[]{:S(2)}, u32[]{:S(2)}) %collective-permute-start.20) | collective-permute-done | bytes 524320 | tf_op jit(solution)/shard_map/ppermute | solution.py:147
  79.6 1.4 %collective-permute-start.25 = (bf16[128,2048]{1,0:T(8,128)(2,1)S(1)}, bf16[128,2048]{1,0:T(8,128)(2,1)S(1)}, u32[]{:S(2)}, u32[]{:S(2)}) collective-permute-start(bf16[128,2048]{1,0:T(8,128)(2,1)S(1)} %slice.53), channel_id=1, source_target_pairs={{0,1},{1,0},{2,6},{3,7},{4,5},{5,4},{6,2},{7,3},{8,9},{9,8},{10,14... | collective-permute-start | bytes 1572872 | tf_op jit(solution)/shard_map/ppermute | solution.py:147
  81.0 4.1 %shard_map.86 = (bf16[256,2048]{1,0:T(8,128)(2,1)S(1)}, bf16[256,2048]{1,0:T(8,128)(2,1)S(1)}) custom-call(s32[1]{0:T(128)} %bitcast.2.me_ref, bf16[128,2176]{1,0:T(8,128)(2,1)S(1)} %pad_maximum_fusion.own_a, bf16[128,2176]{1,0:T(8,128)(2,1)S(1)} %copy-done.9, bf16[128,2176]{1,0:T(8,128)(2,1)S(1)} %copy-done.11, ...), custom_call_target="tpu_custom_call" | custom-call | flops 2214592512 | bytes 4194304 | tf_op jit(solution)/shard_map/pallas_call | solution.py:122
  85.6 2.5 %collective-permute-done.24 = bf16[64,2048]{1,0:T(8,128)(2,1)S(1)} collective-permute-done((bf16[64,2048]{1,0:T(8,128)(2,1)S(1)}, bf16[64,2048]{1,0:T(8,128)(2,1)S(1)}, u32[]{:S(2)}, u32[]{:S(2)}) %collective-permute-start.24) | collective-permute-done | bytes 262176 | tf_op jit(solution)/shard_map/ppermute | solution.py:147
  88.2 1.6 %collective-permute-done.25 = bf16[128,2048]{1,0:T(8,128)(2,1)S(1)} collective-permute-done((bf16[128,2048]{1,0:T(8,128)(2,1)S(1)}, bf16[128,2048]{1,0:T(8,128)(2,1)S(1)}, u32[]{:S(2)}, u32[]{:S(2)}) %collective-permute-start.25) | collective-permute-done | bytes 524320 | tf_op jit(solution)/shard_map/ppermute | solution.py:147
  90.3 1.4 %collective-permute-start.29 = (bf16[64,2048]{1,0:T(8,128)(2,1)S(1)}, bf16[64,2048]{1,0:T(8,128)(2,1)S(1)}, u32[]{:S(2)}, u32[]{:S(2)}) collective-permute-start(bf16[64,2048]{1,0:T(8,128)(2,1)S(1)} %add_convert_fusion.11), channel_id=1, source_target_pairs={{0,8},{1,9},{2,10},{3,11},{4,12},{5,13},{6,14},{7,15},{8,24},{9,25... | collective-permute-start | bytes 786440 | tf_op jit(solution)/shard_map/ppermute | solution.py:147
  91.7 1.3 %collective-permute-start.28 = (bf16[64,2048]{1,0:T(8,128)(2,1)S(1)}, bf16[64,2048]{1,0:T(8,128)(2,1)S(1)}, u32[]{:S(2)}, u32[]{:S(2)}) collective-permute-start(bf16[64,2048]{1,0:T(8,128)(2,1)S(1)} %slice.57), channel_id=1, source_target_pairs={{0,4},{1,5},{2,3},{3,2},{4,0},{5,1},{6,7},{7,6},{8,12},{9,13},{10,... | collective-permute-start | bytes 786440 | tf_op jit(solution)/shard_map/ppermute | solution.py:147
  93.1 0.9 collective-permute-start.30
  94.0 6.3 %collective-permute-done.29 = bf16[64,2048]{1,0:T(8,128)(2,1)S(1)} collective-permute-done((bf16[64,2048]{1,0:T(8,128)(2,1)S(1)}, bf16[64,2048]{1,0:T(8,128)(2,1)S(1)}, u32[]{:S(2)}, u32[]{:S(2)}) %collective-permute-start.29) | collective-permute-done | bytes 262176 | tf_op jit(solution)/shard_map/ppermute | solution.py:147
  100.8 2.8 %collective-permute-done.30 = bf16[128,2048]{1,0:T(8,128)(2,1)S(1)} collective-permute-done((bf16[128,2048]{1,0:T(8,128)(2,1)S(1)}, bf16[128,2048]{1,0:T(8,128)(2,1)S(1)}, u32[]{:S(2)}, u32[]{:S(2)}) %collective-permute-start.30) | collective-permute-done | bytes 524320 | tf_op jit(solution)/shard_map/ppermute | solution.py:147
  103.7 2.9 %collective-permute-start.33 = (bf16[64,2048]{1,0:T(8,128)(2,1)S(1)}, bf16[64,2048]{1,0:T(8,128)(2,1)S(1)}, u32[]{:S(2)}, u32[]{:S(2)}) collective-permute-start(bf16[64,2048]{1,0:T(8,128)(2,1)S(1)} %add_convert_fusion.10), channel_id=1, source_target_pairs={{0,8},{1,9},{2,10},{3,11},{4,12},{5,13},{6,14},{7,15},{8,24},{9,25... | collective-permute-start | bytes 786440 | tf_op jit(solution)/shard_map/ppermute | solution.py:147
  107.2 1.4 %collective-permute-start.27 = (bf16[128,2048]{1,0:T(8,128)(2,1)S(1)}, bf16[128,2048]{1,0:T(8,128)(2,1)S(1)}, u32[]{:S(2)}, u32[]{:S(2)}) collective-permute-start(bf16[128,2048]{1,0:T(8,128)(2,1)S(1)} %slice.55), channel_id=1, source_target_pairs={{0,1},{1,0},{2,6},{3,7},{4,5},{5,4},{6,2},{7,3},{8,9},{9,8},{10,14... | collective-permute-start | bytes 1572872 | tf_op jit(solution)/shard_map/ppermute | solution.py:147
  108.6 4.4 %collective-permute-done.33 = bf16[64,2048]{1,0:T(8,128)(2,1)S(1)} collective-permute-done((bf16[64,2048]{1,0:T(8,128)(2,1)S(1)}, bf16[64,2048]{1,0:T(8,128)(2,1)S(1)}, u32[]{:S(2)}, u32[]{:S(2)}) %collective-permute-start.33) | collective-permute-done | bytes 262176 | tf_op jit(solution)/shard_map/ppermute | solution.py:147
  113.0 2.8 %collective-permute-done.32 = bf16[64,2048]{1,0:T(8,128)(2,1)S(1)} collective-permute-done((bf16[64,2048]{1,0:T(8,128)(2,1)S(1)}, bf16[64,2048]{1,0:T(8,128)(2,1)S(1)}, u32[]{:S(2)}, u32[]{:S(2)}) %collective-permute-start.32) | collective-permute-done | bytes 262176 | tf_op jit(solution)/shard_map/ppermute | solution.py:147
  115.9 1.6 %collective-permute-done.27 = bf16[128,2048]{1,0:T(8,128)(2,1)S(1)} collective-permute-done((bf16[128,2048]{1,0:T(8,128)(2,1)S(1)}, bf16[128,2048]{1,0:T(8,128)(2,1)S(1)}, u32[]{:S(2)}, u32[]{:S(2)}) %collective-permute-start.27) | collective-permute-done | bytes 524320 | tf_op jit(solution)/shard_map/ppermute | solution.py:147
  118.6 8.4 %collective-permute-done.34 = bf16[64,2048]{1,0:T(8,128)(2,1)S(1)} collective-permute-done((bf16[64,2048]{1,0:T(8,128)(2,1)S(1)}, bf16[64,2048]{1,0:T(8,128)(2,1)S(1)}, u32[]{:S(2)}, u32[]{:S(2)}) %collective-permute-start.34) | collective-permute-done | bytes 262176 | tf_op jit(solution)/shard_map/ppermute | solution.py:147
  127.0 0.8 add_convert_fusion.8
  (90 shorter events, 13.3 us)
Async XLA Ops:
  0.9 6.5 %collective-permute-start = (bf16[64,1024]{1,0:T(8,128)(2,1)S(1)}, bf16[64,1024]{1,0:T(8,128)(2,1)S(1)}, u32[]{:S(2)}, u32[]{:S(2)}) collective-permute-start(bf16[64,1024]{1,0:T(8,128)(2,1)S(1)} %constant_dynamic-slice_fusion), channel_id=1, source_target_pairs={{0,1},{1,0},{2,3},{3,2},{4,5},{5,4},{6,7},{7,6},{8,9},{9,8},{10,11... | collective-permute-start | bytes 393224 | tf_op jit(solution)/shard_map/ppermute | solution.py:147
  4.7 41.8 %copy-start = (bf16[1,704,2048]{2,1,0:T(8,128)(2,1)S(1)}, bf16[1,704,2048]{2,1,0:T(8,128)(2,1)}, u32[]{:S(2)}) copy-start(bf16[1,704,2048]{2,1,0:T(8,128)(2,1)} %param.13) | copy-start | bytes 8650756
  7.4 1.0 copy-start.7
  11.1 8.7 %collective-permute-start.2 = (bf16[64,2176]{1,0:T(8,128)(2,1)S(1)}, bf16[64,2176]{1,0:T(8,128)(2,1)S(1)}, u32[]{:S(2)}, u32[]{:S(2)}) collective-permute-start(bf16[64,2176]{1,0:T(8,128)(2,1)S(1)} %get-tuple-element.66), channel_id=1, source_target_pairs={{0,8},{1,9},{2,10},{3,11},{4,12},{5,13},{6,14},{7,15},{8,24},{9,25... | collective-permute-start | bytes 835592 | tf_op jit(solution)/shard_map/ppermute | solution.py:147
  12.9 9.1 %collective-permute-start.1 = (bf16[64,2176]{1,0:T(8,128)(2,1)S(1)}, bf16[64,2176]{1,0:T(8,128)(2,1)S(1)}, u32[]{:S(2)}, u32[]{:S(2)}) collective-permute-start(bf16[64,2176]{1,0:T(8,128)(2,1)S(1)} %get-tuple-element.66), channel_id=1, source_target_pairs={{0,4},{1,5},{2,3},{3,2},{4,0},{5,1},{6,7},{7,6},{8,12},{9,13},{10,... | collective-permute-start | bytes 835592 | tf_op jit(solution)/shard_map/ppermute | solution.py:147
  19.9 9.6 %collective-permute-start.6 = (bf16[64,2176]{1,0:T(8,128)(2,1)S(1)}, bf16[64,2176]{1,0:T(8,128)(2,1)S(1)}, u32[]{:S(2)}, u32[]{:S(2)}) collective-permute-start(bf16[64,2176]{1,0:T(8,128)(2,1)S(1)} %collective-permute-done.2), channel_id=1, source_target_pairs={{0,4},{1,5},{2,3},{3,2},{4,0},{5,1},{6,7},{7,6},{8,12},{9,13},{10,... | collective-permute-start | bytes 835592 | tf_op jit(solution)/shard_map/ppermute | solution.py:147
  21.3 8.2 %collective-permute-start.5 = (bf16[64,2176]{1,0:T(8,128)(2,1)S(1)}, bf16[64,2176]{1,0:T(8,128)(2,1)S(1)}, u32[]{:S(2)}, u32[]{:S(2)}) collective-permute-start(bf16[64,2176]{1,0:T(8,128)(2,1)S(1)} %collective-permute-done.2), channel_id=1, source_target_pairs={{0,8},{1,9},{2,10},{3,11},{4,12},{5,13},{6,14},{7,15},{8,24},{9,25... | collective-permute-start | bytes 835592 | tf_op jit(solution)/shard_map/ppermute | solution.py:147
  22.1 12.6 %collective-permute-start.3 = (bf16[128,2176]{1,0:T(8,128)(2,1)S(1)}, bf16[128,2176]{1,0:T(8,128)(2,1)S(1)}, u32[]{:S(2)}, u32[]{:S(2)}) collective-permute-start(bf16[128,2176]{1,0:T(8,128)(2,1)S(1)} %pad_maximum_fusion.own_a), channel_id=1, source_target_pairs={{0,1},{1,0},{2,6},{3,7},{4,5},{5,4},{6,2},{7,3},{8,9},{9,8},{10,14... | collective-permute-start | bytes 1671176 | tf_op jit(solution)/shard_map/ppermute | solution.py:147
  23.7 14.4 %collective-permute-start.4 = (bf16[128,2176]{1,0:T(8,128)(2,1)S(1)}, bf16[128,2176]{1,0:T(8,128)(2,1)S(1)}, u32[]{:S(2)}, u32[]{:S(2)}) collective-permute-start(bf16[128,2176]{1,0:T(8,128)(2,1)S(1)} %pad_maximum_fusion.own_a), channel_id=1, source_target_pairs={{0,2},{1,3},{2,0},{3,1},{4,6},{5,7},{6,4},{7,5},{8,10},{9,11},{10,... | collective-permute-start | bytes 1671176 | tf_op jit(solution)/shard_map/ppermute | solution.py:147
  29.5 9.7 %collective-permute-start.11 = (bf16[64,2176]{1,0:T(8,128)(2,1)S(1)}, bf16[64,2176]{1,0:T(8,128)(2,1)S(1)}, u32[]{:S(2)}, u32[]{:S(2)}) collective-permute-start(bf16[64,2176]{1,0:T(8,128)(2,1)S(1)} %collective-permute-done.5), channel_id=1, source_target_pairs={{0,4},{1,5},{2,3},{3,2},{4,0},{5,1},{6,7},{7,6},{8,12},{9,13},{10,... | collective-permute-start | bytes 835592 | tf_op jit(solution)/shard_map/ppermute | solution.py:147
  30.9 12.5 %collective-permute-start.8 = (bf16[128,2176]{1,0:T(8,128)(2,1)S(1)}, bf16[128,2176]{1,0:T(8,128)(2,1)}, u32[]{:S(2)}, u32[]{:S(2)}) collective-permute-start(bf16[128,2176]{1,0:T(8,128)(2,1)S(1)} %pad_maximum_fusion.1.own_a), channel_id=1, source_target_pairs={{0,1},{1,0},{2,6},{3,7},{4,5},{5,4},{6,2},{7,3},{8,9},{9,8},{10,14... | collective-permute-start | bytes 1671176 | tf_op jit(solution)/shard_map/ppermute | solution.py:147
  32.5 10.9 %collective-permute-start.9 = (bf16[128,2176]{1,0:T(8,128)(2,1)S(1)}, bf16[128,2176]{1,0:T(8,128)(2,1)S(1)}, u32[]{:S(2)}, u32[]{:S(2)}) collective-permute-start(bf16[128,2176]{1,0:T(8,128)(2,1)S(1)} %pad_maximum_fusion.1.own_a), channel_id=1, source_target_pairs={{0,2},{1,3},{2,0},{3,1},{4,6},{5,7},{6,4},{7,5},{8,10},{9,11},{10,... | collective-permute-start | bytes 1671176 | tf_op jit(solution)/shard_map/ppermute | solution.py:147
  34.7 8.7 %copy-start.8 = (bf16[128,2176]{1,0:T(8,128)(2,1)}, bf16[128,2176]{1,0:T(8,128)(2,1)S(1)}, u32[]{:S(2)}) copy-start(bf16[128,2176]{1,0:T(8,128)(2,1)S(1)} %collective-permute-done.3.own_b) | copy-start | bytes 1671172
  34.7 8.7 %collective-permute-start.10 = (bf16[64,2176]{1,0:T(8,128)(2,1)S(1)}, bf16[64,2176]{1,0:T(8,128)(2,1)}, u32[]{:S(2)}, u32[]{:S(2)}) collective-permute-start(bf16[64,2176]{1,0:T(8,128)(2,1)S(1)} %collective-permute-done.5), channel_id=1, source_target_pairs={{0,8},{1,9},{2,10},{3,11},{4,12},{5,13},{6,14},{7,15},{8,24},{9,25... | collective-permute-start | bytes 835592 | tf_op jit(solution)/shard_map/ppermute | solution.py:147
  38.1 6.1 %copy-start.10 = (bf16[128,2176]{1,0:T(8,128)(2,1)}, bf16[128,2176]{1,0:T(8,128)(2,1)S(1)}, u32[]{:S(2)}) copy-start(bf16[128,2176]{1,0:T(8,128)(2,1)S(1)} %collective-permute-done.4.sib_a) | copy-start | bytes 1671172
  44.2 2.3 %collective-permute-start.12 = (bf16[128,2176]{1,0:T(8,128)(2,1)}, bf16[128,2176]{1,0:T(8,128)(2,1)}, u32[]{:S(2)}, u32[]{:S(2)}) collective-permute-start(bf16[128,2176]{1,0:T(8,128)(2,1)} %collective-permute-done.8.own_b), channel_id=1, source_target_pairs={{0,2},{1,3},{2,0},{3,1},{4,6},{5,7},{6,4},{7,5},{8,10},{9,11},{10,... | collective-permute-start | bytes 1671176 | tf_op jit(solution)/shard_map/ppermute | solution.py:147
  44.2 13.4 %collective-permute-start.14 = (bf16[64,2176]{1,0:T(8,128)(2,1)}, bf16[64,2176]{1,0:T(8,128)(2,1)}, u32[]{:S(2)}, u32[]{:S(2)}) collective-permute-start(bf16[64,2176]{1,0:T(8,128)(2,1)} %collective-permute-done.10), channel_id=1, source_target_pairs={{0,4},{1,5},{2,3},{3,2},{4,0},{5,1},{6,7},{7,6},{8,12},{9,13},{10,... | collective-permute-start | bytes 835592 | tf_op jit(solution)/shard_map/ppermute | solution.py:147
  44.7 14.0 %collective-permute-start.17 = (bf16[128,2176]{1,0:T(8,128)(2,1)}, bf16[128,2176]{1,0:T(8,128)(2,1)S(1)}, u32[]{:S(2)}, u32[]{:S(2)}) collective-permute-start(bf16[128,2176]{1,0:T(8,128)(2,1)} %pad_maximum_fusion.2.own_a), channel_id=1, source_target_pairs={{0,1},{1,0},{2,6},{3,7},{4,5},{5,4},{6,2},{7,3},{8,9},{9,8},{10,14... | collective-permute-start | bytes 1671176 | tf_op jit(solution)/shard_map/ppermute | solution.py:147
  45.3 13.4 %collective-permute-start.18 = (bf16[128,2176]{1,0:T(8,128)(2,1)}, bf16[128,2176]{1,0:T(8,128)(2,1)S(1)}, u32[]{:S(2)}, u32[]{:S(2)}) collective-permute-start(bf16[128,2176]{1,0:T(8,128)(2,1)} %pad_maximum_fusion.2.own_a), channel_id=1, source_target_pairs={{0,2},{1,3},{2,0},{3,1},{4,6},{5,7},{6,4},{7,5},{8,10},{9,11},{10,... | collective-permute-start | bytes 1671176 | tf_op jit(solution)/shard_map/ppermute | solution.py:147
  46.5 1.8 %copy-start.1 = (bf16[1,704,2048]{2,1,0:T(8,128)(2,1)S(1)}, bf16[1,704,2048]{2,1,0:T(8,128)(2,1)}, u32[]{:S(2)}) copy-start(bf16[1,704,2048]{2,1,0:T(8,128)(2,1)} %param.14) | copy-start | bytes 8650756
  48.3 1.8 %copy-start.3 = (bf16[1,704,2048]{2,1,0:T(8,128)(2,1)S(1)}, bf16[1,704,2048]{2,1,0:T(8,128)(2,1)}, u32[]{:S(2)}) copy-start(bf16[1,704,2048]{2,1,0:T(8,128)(2,1)} %param.15) | copy-start | bytes 8650756
  50.1 1.1 copy-start.6
  51.2 1.1 copy-start.13
  52.2 8.7 %copy-start.4 = (bf16[128,2176]{1,0:T(8,128)(2,1)S(1)}, bf16[128,2176]{1,0:T(8,128)(2,1)}, u32[]{:S(2)}) copy-start(bf16[128,2176]{1,0:T(8,128)(2,1)} %pad_maximum_fusion.2.own_a) | copy-start | bytes 1671172
  57.4 11.3 %collective-permute-start.13 = (bf16[256,2048]{1,0:T(8,128)(2,1)S(1)}, bf16[256,2048]{1,0:T(8,128)(2,1)S(1)}, u32[]{:S(2)}, u32[]{:S(2)}) collective-permute-start(bf16[256,2048]{1,0:T(8,128)(2,1)S(1)} %get-tuple-element.84), channel_id=1, source_target_pairs={{0,2},{1,3},{2,0},{3,1},{4,6},{5,7},{6,4},{7,5},{8,10},{9,11},{10,... | collective-permute-start | bytes 3145736 | tf_op jit(solution)/shard_map/ppermute | solution.py:147
  58.7 2.2 %collective-permute-start.19 = (bf16[128,2176]{1,0:T(8,128)(2,1)S(1)}, bf16[128,2176]{1,0:T(8,128)(2,1)S(1)}, u32[]{:S(2)}, u32[]{:S(2)}) collective-permute-start(bf16[128,2176]{1,0:T(8,128)(2,1)S(1)} %collective-permute-done.17.own_b), channel_id=1, source_target_pairs={{0,2},{1,3},{2,0},{3,1},{4,6},{5,7},{6,4},{7,5},{8,10},{9,11},{10,... | collective-permute-start | bytes 1671176 | tf_op jit(solution)/shard_map/ppermute | solution.py:147
  59.2 9.5 %collective-permute-start.15 = (bf16[128,2176]{1,0:T(8,128)(2,1)S(1)}, bf16[128,2176]{1,0:T(8,128)(2,1)S(1)}, u32[]{:S(2)}, u32[]{:S(2)}) collective-permute-start(bf16[128,2176]{1,0:T(8,128)(2,1)S(1)} %pad_maximum_fusion.3.own_a), channel_id=1, source_target_pairs={{0,1},{1,0},{2,6},{3,7},{4,5},{5,4},{6,2},{7,3},{8,9},{9,8},{10,14... | collective-permute-start | bytes 1671176 | tf_op jit(solution)/shard_map/ppermute | solution.py:147
  59.6 9.1 %collective-permute-start.16 = (bf16[128,2176]{1,0:T(8,128)(2,1)S(1)}, bf16[128,2176]{1,0:T(8,128)(2,1)S(1)}, u32[]{:S(2)}, u32[]{:S(2)}) collective-permute-start(bf16[128,2176]{1,0:T(8,128)(2,1)S(1)} %pad_maximum_fusion.3.own_a), channel_id=1, source_target_pairs={{0,2},{1,3},{2,0},{3,1},{4,6},{5,7},{6,4},{7,5},{8,10},{9,11},{10,... | collective-permute-start | bytes 1671176 | tf_op jit(solution)/shard_map/ppermute | solution.py:147
  64.9 4.8 %copy-start.9 = (bf16[128,2176]{1,0:T(8,128)(2,1)S(1)}, bf16[128,2176]{1,0:T(8,128)(2,1)}, u32[]{:S(2)}) copy-start(bf16[128,2176]{1,0:T(8,128)(2,1)} %copy-done.8) | copy-start | bytes 1671172
  64.9 5.8 %copy-start.2 = (bf16[1,704,2048]{2,1,0:T(8,128)(2,1)S(1)}, bf16[1,704,2048]{2,1,0:T(8,128)(2,1)}, u32[]{:S(2)}) copy-start(bf16[1,704,2048]{2,1,0:T(8,128)(2,1)} %param.14) | copy-start | bytes 8650756
  64.9 13.7 %collective-permute-start.21 = (bf16[256,2048]{1,0:T(8,128)(2,1)S(1)}, bf16[256,2048]{1,0:T(8,128)(2,1)S(1)}, u32[]{:S(2)}, u32[]{:S(2)}) collective-permute-start(bf16[256,2048]{1,0:T(8,128)(2,1)S(1)} %get-tuple-element.95), channel_id=1, source_target_pairs={{0,2},{1,3},{2,0},{3,1},{4,6},{5,7},{6,4},{7,5},{8,10},{9,11},{10,... | collective-permute-start | bytes 3145736 | tf_op jit(solution)/shard_map/ppermute | solution.py:147
  68.7 2.0 %collective-permute-start.22 = (bf16[128,2176]{1,0:T(8,128)(2,1)S(1)}, bf16[128,2176]{1,0:T(8,128)(2,1)S(1)}, u32[]{:S(2)}, u32[]{:S(2)}) collective-permute-start(bf16[128,2176]{1,0:T(8,128)(2,1)S(1)} %collective-permute-done.15.own_b), channel_id=1, source_target_pairs={{0,2},{1,3},{2,0},{3,1},{4,6},{5,7},{6,4},{7,5},{8,10},{9,11},{10,... | collective-permute-start | bytes 1671176 | tf_op jit(solution)/shard_map/ppermute | solution.py:147
  69.2 9.2 %collective-permute-start.20 = (bf16[128,2048]{1,0:T(8,128)(2,1)S(1)}, bf16[128,2048]{1,0:T(8,128)(2,1)S(1)}, u32[]{:S(2)}, u32[]{:S(2)}) collective-permute-start(bf16[128,2048]{1,0:T(8,128)(2,1)S(1)} %slice.49), channel_id=1, source_target_pairs={{0,1},{1,0},{2,6},{3,7},{4,5},{5,4},{6,2},{7,3},{8,9},{9,8},{10,14... | collective-permute-start | bytes 1572872 | tf_op jit(solution)/shard_map/ppermute | solution.py:147
  69.7 11.3 %collective-permute-start.7 = (bf16[128,2176]{1,0:T(8,128)(2,1)S(1)}, bf16[128,2176]{1,0:T(8,128)(2,1)S(1)}, u32[]{:S(2)}, u32[]{:S(2)}) collective-permute-start(bf16[128,2176]{1,0:T(8,128)(2,1)S(1)} %copy-done.9), channel_id=1, source_target_pairs={{0,2},{1,3},{2,0},{3,1},{4,6},{5,7},{6,4},{7,5},{8,10},{9,11},{10,... | collective-permute-start | bytes 1671176 | tf_op jit(solution)/shard_map/ppermute | solution.py:147
  78.6 2.5 %copy-start.11 = (bf16[128,2176]{1,0:T(8,128)(2,1)S(1)}, bf16[128,2176]{1,0:T(8,128)(2,1)}, u32[]{:S(2)}) copy-start(bf16[128,2176]{1,0:T(8,128)(2,1)} %copy-done.10) | copy-start | bytes 1671172
  79.0 9.1 %collective-permute-start.24 = (bf16[64,2048]{1,0:T(8,128)(2,1)S(1)}, bf16[64,2048]{1,0:T(8,128)(2,1)S(1)}, u32[]{:S(2)}, u32[]{:S(2)}) collective-permute-start(bf16[64,2048]{1,0:T(8,128)(2,1)S(1)} %slice.51), channel_id=1, source_target_pairs={{0,4},{1,5},{2,3},{3,2},{4,0},{5,1},{6,7},{7,6},{8,12},{9,13},{10,... | collective-permute-start | bytes 786440 | tf_op jit(solution)/shard_map/ppermute | solution.py:147
  79.6 10.3 %collective-permute-start.26 = (bf16[256,2048]{1,0:T(8,128)(2,1)S(1)}, bf16[256,2048]{1,0:T(8,128)(2,1)S(1)}, u32[]{:S(2)}, u32[]{:S(2)}) collective-permute-start(bf16[256,2048]{1,0:T(8,128)(2,1)S(1)} %get-tuple-element.106), channel_id=1, source_target_pairs={{0,2},{1,3},{2,0},{3,1},{4,6},{5,7},{6,4},{7,5},{8,10},{9,11},{10,... | collective-permute-start | bytes 3145736 | tf_op jit(solution)/shard_map/ppermute | solution.py:147
  79.6 10.1 %collective-permute-start.25 = (bf16[128,2048]{1,0:T(8,128)(2,1)S(1)}, bf16[128,2048]{1,0:T(8,128)(2,1)S(1)}, u32[]{:S(2)}, u32[]{:S(2)}) collective-permute-start(bf16[128,2048]{1,0:T(8,128)(2,1)S(1)} %slice.53), channel_id=1, source_target_pairs={{0,1},{1,0},{2,6},{3,7},{4,5},{5,4},{6,2},{7,3},{8,9},{9,8},{10,14... | collective-permute-start | bytes 1572872 | tf_op jit(solution)/shard_map/ppermute | solution.py:147
  85.1 15.2 %collective-permute-start.23 = (bf16[256,2048]{1,0:T(8,128)(2,1)S(1)}, bf16[256,2048]{1,0:T(8,128)(2,1)S(1)}, u32[]{:S(2)}, u32[]{:S(2)}) collective-permute-start(bf16[256,2048]{1,0:T(8,128)(2,1)S(1)} %get-tuple-element.116), channel_id=1, source_target_pairs={{0,2},{1,3},{2,0},{3,1},{4,6},{5,7},{6,4},{7,5},{8,10},{9,11},{10,... | collective-permute-start | bytes 3145736 | tf_op jit(solution)/shard_map/ppermute | solution.py:147
  90.3 10.0 %collective-permute-start.29 = (bf16[64,2048]{1,0:T(8,128)(2,1)S(1)}, bf16[64,2048]{1,0:T(8,128)(2,1)S(1)}, u32[]{:S(2)}, u32[]{:S(2)}) collective-permute-start(bf16[64,2048]{1,0:T(8,128)(2,1)S(1)} %add_convert_fusion.11), channel_id=1, source_target_pairs={{0,8},{1,9},{2,10},{3,11},{4,12},{5,13},{6,14},{7,15},{8,24},{9,25... | collective-permute-start | bytes 786440 | tf_op jit(solution)/shard_map/ppermute | solution.py:147
  91.7 8.6 %collective-permute-start.28 = (bf16[64,2048]{1,0:T(8,128)(2,1)S(1)}, bf16[64,2048]{1,0:T(8,128)(2,1)S(1)}, u32[]{:S(2)}, u32[]{:S(2)}) collective-permute-start(bf16[64,2048]{1,0:T(8,128)(2,1)S(1)} %slice.57), channel_id=1, source_target_pairs={{0,4},{1,5},{2,3},{3,2},{4,0},{5,1},{6,7},{7,6},{8,12},{9,13},{10,... | collective-permute-start | bytes 786440 | tf_op jit(solution)/shard_map/ppermute | solution.py:147
  93.1 10.5 %collective-permute-start.30 = (bf16[128,2048]{1,0:T(8,128)(2,1)S(1)}, bf16[128,2048]{1,0:T(8,128)(2,1)S(1)}, u32[]{:S(2)}, u32[]{:S(2)}) collective-permute-start(bf16[128,2048]{1,0:T(8,128)(2,1)S(1)} %slice.59), channel_id=1, source_target_pairs={{0,1},{1,0},{2,6},{3,7},{4,5},{5,4},{6,2},{7,3},{8,9},{9,8},{10,14... | collective-permute-start | bytes 1572872 | tf_op jit(solution)/shard_map/ppermute | solution.py:147
  103.7 23.2 %copy-start.15 = (bf16[64,2048]{1,0:T(8,128)(2,1)S(1)}, bf16[64,2048]{1,0:T(8,128)(2,1)}, u32[]{:S(2)}) copy-start(bf16[64,2048]{1,0:T(8,128)(2,1)} %copy-done.14) | copy-start | bytes 786436
  103.7 9.3 %collective-permute-start.33 = (bf16[64,2048]{1,0:T(8,128)(2,1)S(1)}, bf16[64,2048]{1,0:T(8,128)(2,1)S(1)}, u32[]{:S(2)}, u32[]{:S(2)}) collective-permute-start(bf16[64,2048]{1,0:T(8,128)(2,1)S(1)} %add_convert_fusion.10), channel_id=1, source_target_pairs={{0,8},{1,9},{2,10},{3,11},{4,12},{5,13},{6,14},{7,15},{8,24},{9,25... | collective-permute-start | bytes 786440 | tf_op jit(solution)/shard_map/ppermute | solution.py:147
  106.6 9.1 %collective-permute-start.32 = (bf16[64,2048]{1,0:T(8,128)(2,1)S(1)}, bf16[64,2048]{1,0:T(8,128)(2,1)S(1)}, u32[]{:S(2)}, u32[]{:S(2)}) collective-permute-start(bf16[64,2048]{1,0:T(8,128)(2,1)S(1)} %slice.63), channel_id=1, source_target_pairs={{0,4},{1,5},{2,3},{3,2},{4,0},{5,1},{6,7},{7,6},{8,12},{9,13},{10,... | collective-permute-start | bytes 786440 | tf_op jit(solution)/shard_map/ppermute | solution.py:147
  107.2 10.3 %collective-permute-start.27 = (bf16[128,2048]{1,0:T(8,128)(2,1)S(1)}, bf16[128,2048]{1,0:T(8,128)(2,1)S(1)}, u32[]{:S(2)}, u32[]{:S(2)}) collective-permute-start(bf16[128,2048]{1,0:T(8,128)(2,1)S(1)} %slice.55), channel_id=1, source_target_pairs={{0,1},{1,0},{2,6},{3,7},{4,5},{5,4},{6,2},{7,3},{8,9},{9,8},{10,14... | collective-permute-start | bytes 1572872 | tf_op jit(solution)/shard_map/ppermute | solution.py:147
  117.6 9.3 %collective-permute-start.34 = (bf16[64,2048]{1,0:T(8,128)(2,1)S(1)}, bf16[64,2048]{1,0:T(8,128)(2,1)S(1)}, u32[]{:S(2)}, u32[]{:S(2)}) collective-permute-start(bf16[64,2048]{1,0:T(8,128)(2,1)S(1)} %add_convert_fusion.9), channel_id=1, source_target_pairs={{0,8},{1,9},{2,10},{3,11},{4,12},{5,13},{6,14},{7,15},{8,24},{9,25... | collective-permute-start | bytes 786440 | tf_op jit(solution)/shard_map/ppermute | solution.py:147
  118.1 8.9 %collective-permute-start.31 = (bf16[64,2048]{1,0:T(8,128)(2,1)S(1)}, bf16[64,2048]{1,0:T(8,128)(2,1)S(1)}, u32[]{:S(2)}, u32[]{:S(2)}) collective-permute-start(bf16[64,2048]{1,0:T(8,128)(2,1)S(1)} %slice.61), channel_id=1, source_target_pairs={{0,4},{1,5},{2,3},{3,2},{4,0},{5,1},{6,7},{7,6},{8,12},{9,13},{10,... | collective-permute-start | bytes 786440 | tf_op jit(solution)/shard_map/ppermute | solution.py:147
  (5 other events, 4.0 us)

commit v4 on v3

--- a/solution.py
+++ b/solution.py
@@ -64,45 +64,57 @@
     packed_ref[:, width:] = jnp.where(lane < LANES // 2, high, weight - high).astype(BF16)
 
 
-def front(half, attn_out, came, resid, norm_gain, ids, gates):
-    rows, width = resid.shape
+def whole(a):
+    return pl.BlockSpec(a.shape, lambda i: (0,) * len(a.shape))
+
+
+def front(half, *arrays):
+    rows, width = arrays[2].shape
+    results = (
+        jax.ShapeDtypeStruct((rows, width + LANES), BF16),
+        jax.ShapeDtypeStruct((rows, width), BF16),
+    )
     return pl.pallas_call(
         front_kernel,
-        out_shape=(
-            jax.ShapeDtypeStruct((rows, width + LANES), BF16),
-            jax.ShapeDtypeStruct((rows, width), BF16),
-        ),
-        in_specs=[SMEM] + [VMEM] * 6,
-        out_specs=(VMEM, VMEM),
-        compiler_params=pltpu.CompilerParams(vmem_limit_bytes=8 * 2**20),
-    )(half.reshape(1), attn_out, came, resid, norm_gain.reshape(1, -1), ids, gates)
-
-
-def expert_kernel(me_ref, own_a, own_b, sib_a, sib_b, gate_ref, up_ref, down_ref, own_out, sib_out, rows, act):
+        grid=(1,),
+        out_shape=results,
+        in_specs=[SMEM] + [whole(a) for a in arrays],
+        out_specs=tuple(whole(r) for r in results),
+        compiler_params=pltpu.CompilerParams(vmem_limit_bytes=60 * 2**20),
+    )(half.reshape(1), *arrays)
+
+
+def expert_kernel(me_ref, own_a, own_b, sib_a, sib_b, gate_ref, up_ref, down_ref, own_out, sib_out, came, rows, act, arrived):
     count = 2 * own_a.shape[0]
     hidden_units, width = down_ref.shape
     slots = count // 2
     me = me_ref[0]
+    loads = []
+    for i, source in enumerate((own_a, own_b, sib_a, sib_b)):
+        into = came.at[i // 2, pl.ds(i % 2 * slots, slots)]
+        loads.append(pltpu.make_async_copy(source, into, arrived.at[i]))
+        loads[-1].start()
     row = lax.broadcasted_iota(jnp.int32, (count, count), 0)
     column = lax.broadcasted_iota(jnp.int32, (count, count), 1)
     earlier = jnp.where(column < row, 1.0, 0.0).astype(BF16)
     slot = lax.broadcasted_iota(jnp.int32, (count, slots), 1).astype(F32)
 
-    def placing(*halves):
-        routing = jnp.concatenate([h[:, width:] for h in halves], axis=0).astype(F32)
+    def placing(n):
+        routing = came[n, :, width:].astype(F32)
         lane = lax.broadcasted_iota(jnp.int32, routing.shape, 1)
         weight = jnp.sum(jnp.where(lane % (LANES // 2) == me, routing, 0.0), axis=1, keepdims=True)
         chosen = jnp.broadcast_to(jnp.where(weight != 0, 1.0, 0.0), (count, slots))
         rank = product(earlier, chosen.astype(BF16), 1, 0)
         return jnp.where(rank == slot, chosen, 0.0).astype(BF16), weight
 
-    place_own, weight_own = placing(own_a, own_b)
-    place_sib, weight_sib = placing(sib_a, sib_b)
+    for load in loads:
+        load.wait()
+    place_own, weight_own = placing(0)
+    place_sib, weight_sib = placing(1)
     for start, size in tiles(width, 512):
         part = slice(start, start + size)
-        for place, a, b, into in ((place_own, own_a, own_b, 0), (place_sib, sib_a, sib_b, slots)):
-            both = jnp.concatenate([a[:, part], b[:, part]], axis=0)
-            rows[into : into + slots, part] = product(place, both, 0, 0).astype(BF16)
+        rows[:slots, part] = product(place_own, came[0, :, part], 0, 0).astype(BF16)
+        rows[slots:, part] = product(place_sib, came[1, :, part], 0, 0).astype(BF16)
     for start, size in tiles(hidden_units, 256):
         part = slice(start, start + size)
         gate_pre = product(rows[...], gate_ref[part, :], 1, 1)
@@ -122,9 +134,14 @@
     return pl.pallas_call(
         expert_kernel,
         out_shape=(result, result),
-        in_specs=[SMEM] + [VMEM] * 7,
+        in_specs=[SMEM] + [pl.BlockSpec(memory_space=pl.ANY)] * 4 + [VMEM] * 3,
         out_specs=(VMEM, VMEM),
-        scratch_shapes=[pltpu.VMEM((count, width), BF16), pltpu.VMEM((count, hidden_units), BF16)],
+        scratch_shapes=[
+            pltpu.VMEM((2, count, own[0].shape[1]), BF16),
+            pltpu.VMEM((count, width), BF16),
+            pltpu.VMEM((count, hidden_units), BF16),
+            pltpu.SemaphoreType.DMA((4,)),
+        ],
         compiler_params=pltpu.CompilerParams(vmem_limit_bytes=16 * 2**20),
         cost_estimate=pl.CostEstimate(
             flops=6 * count * width * hidden_units, bytes_accessed=8 * count * width, transcendentals=0
@@ -153,6 +170,10 @@
     ring = list(range(0, planes, 2)) + list(range(1, planes, 2))[::-1]
     after = {z: ring[i - 1] for i, z in enumerate(ring)}
     down = routes(lambda z, x, c, y: (after[z], x, c, y))
+    place = {z: i for i, z in enumerate(ring)}
+    returns = [
+        routes(lambda z, x, c, y, step=step: (ring[(place[z] + step) % planes], x, c, y)) for step in range(planes)
+    ]
 
     def add(*terms):
         return functools.reduce(lambda a, b: a + b, [t.astype(F32) for t in terms])
@@ -166,7 +187,7 @@
         return value
 
     theirs = lax.dynamic_slice_in_dim(attn_out, (1 - half) * my_rows, my_rows, 0)
-    packed, hidden = front(half, attn_out, partner(theirs), resid, norm_gain, expert_ids, gate_vals)
+    packed, hidden = front(half, attn_out, partner(theirs), resid, norm_gain.reshape(1, -1), expert_ids, gate_vals)
 
     piece, two, one, other, came, out, total, kept, home = ({} for _ in range(9))
 
@@ -193,45 +214,45 @@
         came[step] = sibling(out[step][1])
 
     def merge_cores(step):
-        total[step] = in_turn(add(out[step][0], came[step]).astype(BF16))
+        total[step] = (add(out[step][0], came[step]).astype(BF16))
         other[step] = second(total[step][2 * my_rows :])
 
     def merge_second(step):
-        kept[step] = in_turn(add(total[step][: 2 * my_rows], other[step]).astype(BF16))
+        kept[step] = (add(total[step][: 2 * my_rows], other[step]).astype(BF16))
         one[step] = first(kept[step][my_rows:])
 
     def merge_first(step):
-        terms = [kept[step][:my_rows], one[step]] + ([home[step - 1]] if step > 1 else [])
-        home[step] = down(in_turn(add(*terms).astype(BF16)))
+        value = (add(kept[step][:my_rows], one[step]).astype(BF16))
+        home[step] = returns[step](value)
 
     spread(0)
     spread(1)
     widen(0)
+    spread(2)
     widen(1)
-    spread(2)
     share(0)
+    spread(3)
     widen(2)
-    spread(3)
     share(1)
     run(1)
     widen(3)
     share(2)
     run(2)
     share(3)
+    run(3)
+    run(0)
     merge_cores(1)
-    run(3)
     merge_cores(2)
+    merge_cores(3)
+    merge_cores(0)
     merge_second(1)
-    run(0)
-    merge_cores(3)
     merge_second(2)
+    merge_second(3)
+    merge_second(0)
     merge_first(1)
-    merge_cores(0)
-    merge_second(3)
     merge_first(2)
-    merge_second(0)
     merge_first(3)
-    return add(hidden, kept[0][:my_rows], one[0], home[planes - 1]).astype(BF16)
+    return add(hidden, kept[0][:my_rows], one[0], *(home[step] for step in range(1, planes))).astype(BF16)
 
 
 def exchanged_plan(ep_count, attn_out, resid, norm_gain, expert_ids, gate_vals, w_gate, w_up, w_down):

time: 128 us -> 119 us (0.930)
  waiting for transfers between devices: 59.8 us -> 42.5 us
  starting transfers between devices: 31.6 us -> 36.3 us
  Pallas kernels: 17.4 us -> 20.5 us
    ppermute x35, waiting for transfers between devices: 59.8 us -> 42.5 us  [routes(): return lambda a: lax.ppermute(a, AXES, pairs)]
    ppermute x35, starting transfers between devices: 31.6 us -> 36.3 us  [routes(): return lambda a: lax.ppermute(a, AXES, pairs)]
    pallas_call x1, Pallas kernels: 0.36 us -> 2.19 us  [front(): pl.pallas_call(front_kernel, grid=(1,), out_shape=results, in_specs=[SMEM...]
    unnamed x38 -> x32, local copies, waits for them, and re-layouts: 12.4 us -> 11.8 us
  transfers between devices with their start and end apart: 35 -> 35, of which waited for: 19 -> 16; matrix products, arithmetic and copies ran while one was open for 5% -> 7% of each run, Pallas kernels for 13% -> 15%
where the time goes in v4:
time: 119 us
  waiting for transfers between devices  42.5 us (36%)
  starting transfers between devices  36.3 us (31%)
  Pallas kernels  20.5 us (17%)
  local copies, waits for them, and re-layouts  13 us (11%)
  other arithmetic  6.17 us (5%)
    ppermute x35, waiting for transfers between devices, routes(): return lambda a: lax.ppermute(a, AXES, pairs)  42.5 us
    ppermute x35, starting transfers between devices, routes(): return lambda a: lax.ppermute(a, AXES, pairs)  36.3 us
    pallas_call x4, Pallas kernels, experts(): pl.pallas_call(expert_kernel, out_shape=(result, result), in_specs=[SMEM]...  18.3 us
    unnamed x32, local copies, waits for them, and re-layouts  11.8 us
    concatenate x4, other arithmetic, widen(): two[step] = in_turn(jnp.concatenate([piece[step], one[step]], axis=0))  2.98 us
  transfers between devices with their start and end apart: 35, of which 16 were waited for; matrix products, arithmetic and copies ran while one was open for 7% of the time, Pallas kernels for 15%

profile of v4, /device:TPU:0, one launch (start us, length us, event | category | flops | bytes accessed | tf_op | source)
XLA Modules:
  0.0 118.8 jit_solution(12215015479890709258)
XLA Ops:
  0.0 0.9 constant_dynamic-slice_fusion
  0.9 3.0 %collective-permute-start = (bf16[64,1024]{1,0:T(8,128)(2,1)S(1)}, bf16[64,1024]{1,0:T(8,128)(2,1)S(1)}, u32[]{:S(2)}, u32[]{:S(2)}) collective-permute-start(bf16[64,1024]{1,0:T(8,128)(2,1)S(1)} %constant_dynamic-slice_fusion), channel_id=1, source_target_pairs={{0,1},{1,0},{2,3},{3,2},{4,5},{5,4},{6,7},{7,6},{8,9},{9,8},{10,11... | collective-permute-start | bytes 393224 | tf_op jit(solution)/shard_map/ppermute | solution.py:164
  3.9 1.4 %copy.9.ids_ref = s32[128,6]{1,0:T(8,128)} copy(s32[128,6]{0,1:T(8,128)} %param.11) | data formatting | bytes 6144 | tf_op args[3]
  5.4 1.6 %copy.10.gates_ref = f32[128,6]{1,0:T(8,128)} copy(f32[128,6]{0,1:T(8,128)} %param.12) | data formatting | bytes 6144 | tf_op args[4]
  8.1 2.2 %shard_map.82 = (bf16[64,2176]{1,0:T(8,128)(2,1)}, bf16[64,2048]{1,0:T(8,128)(2,1)}) custom-call(s32[1]{0:T(128)} %bitcast.half_ref, bf16[128,1024]{1,0:T(8,128)(2,1)} %attn_ref.1, bf16[64,1024]{1,0:T(8,128)(2,1)} %copy-done.14, bf16[64,2048]{1,0:T(8,128)(2,1)} %resid_ref.1, f32[1,2048]{1,0:T(1,128)} %bitcast.18, s32[128,6]{1,0:T(8,128)} %copy.9.ids_ref, ...), custom_call_target="tpu_custom_call" | custom-call | tf_op jit(solution)/shard_map/pallas_call | solution.py:77
  10.3 1.8 %collective-permute-start.2 = (bf16[64,2176]{1,0:T(8,128)(2,1)}, bf16[64,2176]{1,0:T(8,128)(2,1)S(1)}, u32[]{:S(2)}, u32[]{:S(2)}) collective-permute-start(bf16[64,2176]{1,0:T(8,128)(2,1)} %get-tuple-element.55), channel_id=1, source_target_pairs={{0,8},{1,9},{2,10},{3,11},{4,12},{5,13},{6,14},{7,15},{8,24},{9,25... | collective-permute-start | bytes 835592 | tf_op jit(solution)/shard_map/ppermute | solution.py:164
  12.1 1.5 %collective-permute-start.1 = (bf16[64,2176]{1,0:T(8,128)(2,1)}, bf16[64,2176]{1,0:T(8,128)(2,1)S(1)}, u32[]{:S(2)}, u32[]{:S(2)}) collective-permute-start(bf16[64,2176]{1,0:T(8,128)(2,1)} %get-tuple-element.55), channel_id=1, source_target_pairs={{0,4},{1,5},{2,3},{3,2},{4,0},{5,1},{6,7},{7,6},{8,12},{9,13},{10,... | collective-permute-start | bytes 835592 | tf_op jit(solution)/shard_map/ppermute | solution.py:164
  13.6 5.7 %collective-permute-done.2 = bf16[64,2176]{1,0:T(8,128)(2,1)S(1)} collective-permute-done((bf16[64,2176]{1,0:T(8,128)(2,1)}, bf16[64,2176]{1,0:T(8,128)(2,1)S(1)}, u32[]{:S(2)}, u32[]{:S(2)}) %collective-permute-start.2) | collective-permute-done | bytes 278560 | tf_op jit(solution)/shard_map/ppermute | solution.py:164
  19.2 0.8 collective-permute-start.6
  20.0 1.5 %collective-permute-start.5 = (bf16[64,2176]{1,0:T(8,128)(2,1)S(1)}, bf16[64,2176]{1,0:T(8,128)(2,1)S(1)}, u32[]{:S(2)}, u32[]{:S(2)}) collective-permute-start(bf16[64,2176]{1,0:T(8,128)(2,1)S(1)} %collective-permute-done.2), channel_id=1, source_target_pairs={{0,4},{1,5},{2,3},{3,2},{4,0},{5,1},{6,7},{7,6},{8,12},{9,13},{10,... | collective-permute-start | bytes 835592 | tf_op jit(solution)/shard_map/ppermute | solution.py:164
  21.5 1.0 pad_maximum_fusion.own_a
  22.6 1.6 %collective-permute-start.3 = (bf16[128,2176]{1,0:T(8,128)(2,1)S(1)}, bf16[128,2176]{1,0:T(8,128)(2,1)S(1)}, u32[]{:S(2)}, u32[]{:S(2)}) collective-permute-start(bf16[128,2176]{1,0:T(8,128)(2,1)S(1)} %pad_maximum_fusion.own_a), channel_id=1, source_target_pairs={{0,1},{1,0},{2,6},{3,7},{4,5},{5,4},{6,2},{7,3},{8,9},{9,8},{10,14... | collective-permute-start | bytes 1671176 | tf_op jit(solution)/shard_map/ppermute | solution.py:164
  24.2 2.9 %collective-permute-done.6 = bf16[64,2176]{1,0:T(8,128)(2,1)S(1)} collective-permute-done((bf16[64,2176]{1,0:T(8,128)(2,1)S(1)}, bf16[64,2176]{1,0:T(8,128)(2,1)S(1)}, u32[]{:S(2)}, u32[]{:S(2)}) %collective-permute-start.6) | collective-permute-done | bytes 278560 | tf_op jit(solution)/shard_map/ppermute | solution.py:164
  27.1 1.1 collective-permute-start.12
  29.1 0.8 copy-done.7
  29.9 1.5 %collective-permute-start.10 = (bf16[128,2176]{1,0:T(8,128)(2,1)S(1)}, bf16[128,2176]{1,0:T(8,128)(2,1)}, u32[]{:S(2)}, u32[]{:S(2)}) collective-permute-start(bf16[128,2176]{1,0:T(8,128)(2,1)S(1)} %pad_maximum_fusion.1.own_a), channel_id=1, source_target_pairs={{0,1},{1,0},{2,6},{3,7},{4,5},{5,4},{6,2},{7,3},{8,9},{9,8},{10,14... | collective-permute-start | bytes 1671176 | tf_op jit(solution)/shard_map/ppermute | solution.py:164
  31.4 0.8 copy-done.5
  32.2 3.0 %collective-permute-done.3.own_b = bf16[128,2176]{1,0:T(8,128)(2,1)S(1)} collective-permute-done((bf16[128,2176]{1,0:T(8,128)(2,1)S(1)}, bf16[128,2176]{1,0:T(8,128)(2,1)S(1)}, u32[]{:S(2)}, u32[]{:S(2)}) %collective-permute-start.3) | collective-permute-done | bytes 557088 | tf_op jit(solution)/shard_map/ppermute | solution.py:164
  35.7 1.0 collective-permute-done.12
  36.7 0.9 pad_maximum_fusion.3.own_a
  37.5 0.8 copy-done.11
  38.4 2.9 %collective-permute-done.10.own_b = bf16[128,2176]{1,0:T(8,128)(2,1)} collective-permute-done((bf16[128,2176]{1,0:T(8,128)(2,1)S(1)}, bf16[128,2176]{1,0:T(8,128)(2,1)}, u32[]{:S(2)}, u32[]{:S(2)}) %collective-permute-start.10) | collective-permute-done | bytes 557088 | tf_op jit(solution)/shard_map/ppermute | solution.py:164
  41.4 1.5 %collective-permute-start.9 = (bf16[64,2176]{1,0:T(8,128)(2,1)}, bf16[64,2176]{1,0:T(8,128)(2,1)}, u32[]{:S(2)}, u32[]{:S(2)}) collective-permute-start(bf16[64,2176]{1,0:T(8,128)(2,1)} %collective-permute-done.8), channel_id=1, source_target_pairs={{0,4},{1,5},{2,3},{3,2},{4,0},{5,1},{6,7},{7,6},{8,12},{9,13},{10,... | collective-permute-start | bytes 835592 | tf_op jit(solution)/shard_map/ppermute | solution.py:164
  42.9 1.5 %collective-permute-start.16 = (bf16[128,2176]{1,0:T(8,128)(2,1)}, bf16[128,2176]{1,0:T(8,128)(2,1)S(1)}, u32[]{:S(2)}, u32[]{:S(2)}) collective-permute-start(bf16[128,2176]{1,0:T(8,128)(2,1)} %pad_maximum_fusion.3.own_a), channel_id=1, source_target_pairs={{0,1},{1,0},{2,6},{3,7},{4,5},{5,4},{6,2},{7,3},{8,9},{9,8},{10,14... | collective-permute-start | bytes 1671176 | tf_op jit(solution)/shard_map/ppermute | solution.py:164
  44.5 1.8 %copy-done.1 = bf16[1,704,2048]{2,1,0:T(8,128)(2,1)S(1)} copy-done((bf16[1,704,2048]{2,1,0:T(8,128)(2,1)S(1)}, bf16[1,704,2048]{2,1,0:T(8,128)(2,1)}, u32[]{:S(2)}) %copy-start.1) | copy-done | bytes 2883608
  46.3 1.8 %copy-done.3 = bf16[1,704,2048]{2,1,0:T(8,128)(2,1)S(1)} copy-done((bf16[1,704,2048]{2,1,0:T(8,128)(2,1)S(1)}, bf16[1,704,2048]{2,1,0:T(8,128)(2,1)}, u32[]{:S(2)}) %copy-start.3) | copy-done | bytes 2883608
  48.1 1.1 copy-done.6
  49.1 1.1 copy-done.12
  50.2 5.3 %shard_map.83 = (bf16[256,2048]{1,0:T(8,128)(2,1)S(1)}, bf16[256,2048]{1,0:T(8,128)(2,1)S(1)}) custom-call(s32[1]{0:T(128)} %bitcast.2.me_ref, bf16[128,2176]{1,0:T(8,128)(2,1)S(1)} %copy-done.6, bf16[128,2176]{1,0:T(8,128)(2,1)} %collective-permute-done.10.own_b, bf16[128,2176]{1,0:T(8,128)(2,1)S(1)} %copy-done.12, ...), custom_call_target="tpu_custom_call" | custom-call | flops 2214592512 | bytes 4194304 | tf_op jit(solution)/shard_map/pallas_call | solution.py:134
  55.6 1.1 pad_maximum_fusion.2.own_a
  58.1 1.0 collective-permute-done.18.sib_b
  59.0 4.3 %shard_map.84 = (bf16[256,2048]{1,0:T(8,128)(2,1)S(1)}, bf16[256,2048]{1,0:T(8,128)(2,1)S(1)}) custom-call(s32[1]{0:T(128)} %bitcast.2.me_ref, bf16[128,2176]{1,0:T(8,128)(2,1)S(1)} %copy-done.4, bf16[128,2176]{1,0:T(8,128)(2,1)S(1)} %collective-permute-done.16.own_b, bf16[128,2176]{1,0:T(8,128)(2,1)S(1)} %collective-permute-done.17.sib_a, ...), custom_call_target="tpu_custom_call" | custom-call | flops 2214592512 | bytes 4194304 | tf_op jit(solution)/shard_map/pallas_call | solution.py:134
  63.6 3.3 %collective-permute-done.14.own_b = bf16[128,2176]{1,0:T(8,128)(2,1)S(1)} collective-permute-done((bf16[128,2176]{1,0:T(8,128)(2,1)S(1)}, bf16[128,2176]{1,0:T(8,128)(2,1)S(1)}, u32[]{:S(2)}, u32[]{:S(2)}) %collective-permute-start.14) | collective-permute-done | bytes 557088 | tf_op jit(solution)/shard_map/ppermute | solution.py:164
  68.8 4.3 %shard_map.85 = (bf16[256,2048]{1,0:T(8,128)(2,1)S(1)}, bf16[256,2048]{1,0:T(8,128)(2,1)S(1)}) custom-call(s32[1]{0:T(128)} %bitcast.2.me_ref, bf16[128,2176]{1,0:T(8,128)(2,1)S(1)} %pad_maximum_fusion.2.own_a, bf16[128,2176]{1,0:T(8,128)(2,1)S(1)} %collective-permute-done.14.own_b, bf16[128,2176]{1,0:T(8,128)(2,1)S(1)} %collective-permute-done.15.sib_a, ...), custom_call_target="tpu_custom_call" | custom-call | flops 2214592512 | bytes 4194304 | tf_op jit(solution)/shard_map/pallas_call | solution.py:134
  73.3 3.3 %collective-permute-done.24 = bf16[128,2048]{1,0:T(8,128)(2,1)S(1)} collective-permute-done((bf16[128,2048]{1,0:T(8,128)(2,1)S(1)}, bf16[128,2048]{1,0:T(8,128)(2,1)S(1)}, u32[]{:S(2)}, u32[]{:S(2)}) %collective-permute-start.24) | collective-permute-done | bytes 524320 | tf_op jit(solution)/shard_map/ppermute | solution.py:164
  77.9 1.6 %collective-permute-start.28 = (bf16[128,2048]{1,0:T(8,128)(2,1)S(1)}, bf16[128,2048]{1,0:T(8,128)(2,1)S(1)}, u32[]{:S(2)}, u32[]{:S(2)}) collective-permute-start(bf16[128,2048]{1,0:T(8,128)(2,1)S(1)} %slice.73), channel_id=1, source_target_pairs={{0,1},{1,0},{2,6},{3,7},{4,5},{5,4},{6,2},{7,3},{8,9},{9,8},{10,14... | collective-permute-start | bytes 1572872 | tf_op jit(solution)/shard_map/ppermute | solution.py:164
  79.6 4.4 %shard_map.86 = (bf16[256,2048]{1,0:T(8,128)(2,1)S(1)}, bf16[256,2048]{1,0:T(8,128)(2,1)S(1)}) custom-call(s32[1]{0:T(128)} %bitcast.2.me_ref, bf16[128,2176]{1,0:T(8,128)(2,1)S(1)} %pad_maximum_fusion.own_a, bf16[128,2176]{1,0:T(8,128)(2,1)S(1)} %copy-done.10, bf16[128,2176]{1,0:T(8,128)(2,1)S(1)} %copy-done.8, ...), custom_call_target="tpu_custom_call" | custom-call | flops 2214592512 | bytes 4194304 | tf_op jit(solution)/shard_map/pallas_call | solution.py:134
  84.1 1.8 %collective-permute-done.25 = bf16[64,2048]{1,0:T(8,128)(2,1)S(1)} collective-permute-done((bf16[64,2048]{1,0:T(8,128)(2,1)S(1)}, bf16[64,2048]{1,0:T(8,128)(2,1)S(1)}, u32[]{:S(2)}, u32[]{:S(2)}) %collective-permute-start.25) | collective-permute-done | bytes 262176 | tf_op jit(solution)/shard_map/ppermute | solution.py:164
  86.0 2.1 %collective-permute-start.26 = (bf16[64,2048]{1,0:T(8,128)(2,1)S(1)}, bf16[64,2048]{1,0:T(8,128)(2,1)S(1)}, u32[]{:S(2)}, u32[]{:S(2)}) collective-permute-start(bf16[64,2048]{1,0:T(8,128)(2,1)S(1)} %add_convert_fusion.11), channel_id=1, source_target_pairs={{0,16},{1,17},{2,18},{3,19},{4,20},{5,21},{6,22},{7,23},{8,0},{9,1... | collective-permute-start | bytes 786440 | tf_op jit(solution)/shard_map/ppermute | solution.py:164
  89.2 1.8 %collective-permute-start.32 = (bf16[128,2048]{1,0:T(8,128)(2,1)S(1)}, bf16[128,2048]{1,0:T(8,128)(2,1)S(1)}, u32[]{:S(2)}, u32[]{:S(2)}) collective-permute-start(bf16[128,2048]{1,0:T(8,128)(2,1)S(1)} %slice.77), channel_id=1, source_target_pairs={{0,1},{1,0},{2,6},{3,7},{4,5},{5,4},{6,2},{7,3},{8,9},{9,8},{10,14... | collective-permute-start | bytes 1572872 | tf_op jit(solution)/shard_map/ppermute | solution.py:164
  91.8 5.2 %collective-permute-done.29 = bf16[64,2048]{1,0:T(8,128)(2,1)S(1)} collective-permute-done((bf16[64,2048]{1,0:T(8,128)(2,1)S(1)}, bf16[64,2048]{1,0:T(8,128)(2,1)S(1)}, u32[]{:S(2)}, u32[]{:S(2)}) %collective-permute-start.29) | collective-permute-done | bytes 262176 | tf_op jit(solution)/shard_map/ppermute | solution.py:164
  97.1 4.1 %collective-permute-start.30 = (bf16[64,2048]{1,0:T(8,128)(2,1)S(1)}, bf16[64,2048]{1,0:T(8,128)(2,1)S(1)}, u32[]{:S(2)}, u32[]{:S(2)}) collective-permute-start(bf16[64,2048]{1,0:T(8,128)(2,1)S(1)} %add_convert_fusion.10), channel_id=1, source_target_pairs={{0,24},{1,25},{2,26},{3,27},{4,28},{5,29},{6,30},{7,31},{8,16},{9,... | collective-permute-start | bytes 786440 | tf_op jit(solution)/shard_map/ppermute | solution.py:164
  101.7 5.2 %collective-permute-done.21 = bf16[128,2048]{1,0:T(8,128)(2,1)S(1)} collective-permute-done((bf16[128,2048]{1,0:T(8,128)(2,1)S(1)}, bf16[128,2048]{1,0:T(8,128)(2,1)S(1)}, u32[]{:S(2)}, u32[]{:S(2)}) %collective-permute-start.21) | collective-permute-done | bytes 524320 | tf_op jit(solution)/shard_map/ppermute | solution.py:164
  107.1 1.7 %collective-permute-start.22 = (bf16[64,2048]{1,0:T(8,128)(2,1)S(1)}, bf16[64,2048]{1,0:T(8,128)(2,1)S(1)}, u32[]{:S(2)}, u32[]{:S(2)}) collective-permute-start(bf16[64,2048]{1,0:T(8,128)(2,1)S(1)} %slice.67), channel_id=1, source_target_pairs={{0,4},{1,5},{2,3},{3,2},{4,0},{5,1},{6,7},{7,6},{8,12},{9,13},{10,... | collective-permute-start | bytes 786440 | tf_op jit(solution)/shard_map/ppermute | solution.py:164
  108.9 3.4 %collective-permute-start.34 = (bf16[64,2048]{1,0:T(8,128)(2,1)S(1)}, bf16[64,2048]{1,0:T(8,128)(2,1)S(1)}, u32[]{:S(2)}, u32[]{:S(2)}) collective-permute-start(bf16[64,2048]{1,0:T(8,128)(2,1)S(1)} %add_convert_fusion.9), channel_id=1, source_target_pairs={{0,8},{1,9},{2,10},{3,11},{4,12},{5,13},{6,14},{7,15},{8,24},{9,25... | collective-permute-start | bytes 786440 | tf_op jit(solution)/shard_map/ppermute | solution.py:164
  112.2 1.3 %collective-permute-done.22 = bf16[64,2048]{1,0:T(8,128)(2,1)S(1)} collective-permute-done((bf16[64,2048]{1,0:T(8,128)(2,1)S(1)}, bf16[64,2048]{1,0:T(8,128)(2,1)S(1)}, u32[]{:S(2)}, u32[]{:S(2)}) %collective-permute-start.22) | collective-permute-done | bytes 262176 | tf_op jit(solution)/shard_map/ppermute | solution.py:164
  113.6 4.3 %collective-permute-done.34 = bf16[64,2048]{1,0:T(8,128)(2,1)S(1)} collective-permute-done((bf16[64,2048]{1,0:T(8,128)(2,1)S(1)}, bf16[64,2048]{1,0:T(8,128)(2,1)S(1)}, u32[]{:S(2)}, u32[]{:S(2)}) %collective-permute-start.34) | collective-permute-done | bytes 262176 | tf_op jit(solution)/shard_map/ppermute | solution.py:164
  117.9 0.9 add_convert_fusion.8
  (84 shorter events, 10.9 us)
Async XLA Ops:
  0.9 6.5 %collective-permute-start = (bf16[64,1024]{1,0:T(8,128)(2,1)S(1)}, bf16[64,1024]{1,0:T(8,128)(2,1)S(1)}, u32[]{:S(2)}, u32[]{:S(2)}) collective-permute-start(bf16[64,1024]{1,0:T(8,128)(2,1)S(1)} %constant_dynamic-slice_fusion), channel_id=1, source_target_pairs={{0,1},{1,0},{2,3},{3,2},{4,5},{5,4},{6,7},{7,6},{8,9},{9,8},{10,11... | collective-permute-start | bytes 393224 | tf_op jit(solution)/shard_map/ppermute | solution.py:164
  5.4 39.1 %copy-start = (bf16[1,704,2048]{2,1,0:T(8,128)(2,1)S(1)}, bf16[1,704,2048]{2,1,0:T(8,128)(2,1)}, u32[]{:S(2)}) copy-start(bf16[1,704,2048]{2,1,0:T(8,128)(2,1)} %param.13) | copy-start | bytes 8650756
  10.3 9.0 %collective-permute-start.2 = (bf16[64,2176]{1,0:T(8,128)(2,1)}, bf16[64,2176]{1,0:T(8,128)(2,1)S(1)}, u32[]{:S(2)}, u32[]{:S(2)}) collective-permute-start(bf16[64,2176]{1,0:T(8,128)(2,1)} %get-tuple-element.55), channel_id=1, source_target_pairs={{0,8},{1,9},{2,10},{3,11},{4,12},{5,13},{6,14},{7,15},{8,24},{9,25... | collective-permute-start | bytes 835592 | tf_op jit(solution)/shard_map/ppermute | solution.py:164
  12.1 9.4 %collective-permute-start.1 = (bf16[64,2176]{1,0:T(8,128)(2,1)}, bf16[64,2176]{1,0:T(8,128)(2,1)S(1)}, u32[]{:S(2)}, u32[]{:S(2)}) collective-permute-start(bf16[64,2176]{1,0:T(8,128)(2,1)} %get-tuple-element.55), channel_id=1, source_target_pairs={{0,4},{1,5},{2,3},{3,2},{4,0},{5,1},{6,7},{7,6},{8,12},{9,13},{10,... | collective-permute-start | bytes 835592 | tf_op jit(solution)/shard_map/ppermute | solution.py:164
  19.2 7.8 %collective-permute-start.6 = (bf16[64,2176]{1,0:T(8,128)(2,1)S(1)}, bf16[64,2176]{1,0:T(8,128)(2,1)S(1)}, u32[]{:S(2)}, u32[]{:S(2)}) collective-permute-start(bf16[64,2176]{1,0:T(8,128)(2,1)S(1)} %collective-permute-done.2), channel_id=1, source_target_pairs={{0,8},{1,9},{2,10},{3,11},{4,12},{5,13},{6,14},{7,15},{8,24},{9,25... | collective-permute-start | bytes 835592 | tf_op jit(solution)/shard_map/ppermute | solution.py:164
  20.0 8.9 %collective-permute-start.5 = (bf16[64,2176]{1,0:T(8,128)(2,1)S(1)}, bf16[64,2176]{1,0:T(8,128)(2,1)S(1)}, u32[]{:S(2)}, u32[]{:S(2)}) collective-permute-start(bf16[64,2176]{1,0:T(8,128)(2,1)S(1)} %collective-permute-done.2), channel_id=1, source_target_pairs={{0,4},{1,5},{2,3},{3,2},{4,0},{5,1},{6,7},{7,6},{8,12},{9,13},{10,... | collective-permute-start | bytes 835592 | tf_op jit(solution)/shard_map/ppermute | solution.py:164
  22.5 6.5 %collective-permute-start.4 = (bf16[128,2176]{1,0:T(8,128)(2,1)S(1)}, bf16[128,2176]{1,0:T(8,128)(2,1)S(1)}, u32[]{:S(2)}, u32[]{:S(2)}) collective-permute-start(bf16[128,2176]{1,0:T(8,128)(2,1)S(1)} %pad_maximum_fusion.own_a), channel_id=1, source_target_pairs={{0,2},{1,3},{2,0},{3,1},{4,6},{5,7},{6,4},{7,5},{8,10},{9,11},{10,... | collective-permute-start | bytes 1671176 | tf_op jit(solution)/shard_map/ppermute | solution.py:164
  22.6 12.6 %collective-permute-start.3 = (bf16[128,2176]{1,0:T(8,128)(2,1)S(1)}, bf16[128,2176]{1,0:T(8,128)(2,1)S(1)}, u32[]{:S(2)}, u32[]{:S(2)}) collective-permute-start(bf16[128,2176]{1,0:T(8,128)(2,1)S(1)} %pad_maximum_fusion.own_a), channel_id=1, source_target_pairs={{0,1},{1,0},{2,6},{3,7},{4,5},{5,4},{6,2},{7,3},{8,9},{9,8},{10,14... | collective-permute-start | bytes 1671176 | tf_op jit(solution)/shard_map/ppermute | solution.py:164
  27.1 9.6 %collective-permute-start.12 = (bf16[64,2176]{1,0:T(8,128)(2,1)S(1)}, bf16[64,2176]{1,0:T(8,128)(2,1)S(1)}, u32[]{:S(2)}, u32[]{:S(2)}) collective-permute-start(bf16[64,2176]{1,0:T(8,128)(2,1)S(1)} %collective-permute-done.6), channel_id=1, source_target_pairs={{0,4},{1,5},{2,3},{3,2},{4,0},{5,1},{6,7},{7,6},{8,12},{9,13},{10,... | collective-permute-start | bytes 835592 | tf_op jit(solution)/shard_map/ppermute | solution.py:164
  28.1 7.6 %collective-permute-start.8 = (bf16[64,2176]{1,0:T(8,128)(2,1)S(1)}, bf16[64,2176]{1,0:T(8,128)(2,1)}, u32[]{:S(2)}, u32[]{:S(2)}) collective-permute-start(bf16[64,2176]{1,0:T(8,128)(2,1)S(1)} %collective-permute-done.6), channel_id=1, source_target_pairs={{0,8},{1,9},{2,10},{3,11},{4,12},{5,13},{6,14},{7,15},{8,24},{9,25... | collective-permute-start | bytes 835592 | tf_op jit(solution)/shard_map/ppermute | solution.py:164
  29.0 8.6 %collective-permute-start.11 = (bf16[128,2176]{1,0:T(8,128)(2,1)S(1)}, bf16[128,2176]{1,0:T(8,128)(2,1)S(1)}, u32[]{:S(2)}, u32[]{:S(2)}) collective-permute-start(bf16[128,2176]{1,0:T(8,128)(2,1)S(1)} %pad_maximum_fusion.1.own_a), channel_id=1, source_target_pairs={{0,2},{1,3},{2,0},{3,1},{4,6},{5,7},{6,4},{7,5},{8,10},{9,11},{10,... | collective-permute-start | bytes 1671176 | tf_op jit(solution)/shard_map/ppermute | solution.py:164
  29.1 0.8 copy-start.7
  29.9 11.4 %collective-permute-start.10 = (bf16[128,2176]{1,0:T(8,128)(2,1)S(1)}, bf16[128,2176]{1,0:T(8,128)(2,1)}, u32[]{:S(2)}, u32[]{:S(2)}) collective-permute-start(bf16[128,2176]{1,0:T(8,128)(2,1)S(1)} %pad_maximum_fusion.1.own_a), channel_id=1, source_target_pairs={{0,1},{1,0},{2,6},{3,7},{4,5},{5,4},{6,2},{7,3},{8,9},{9,8},{10,14... | collective-permute-start | bytes 1671176 | tf_op jit(solution)/shard_map/ppermute | solution.py:164
  35.2 6.1 %copy-start.9 = (bf16[128,2176]{1,0:T(8,128)(2,1)}, bf16[128,2176]{1,0:T(8,128)(2,1)S(1)}, u32[]{:S(2)}) copy-start(bf16[128,2176]{1,0:T(8,128)(2,1)S(1)} %collective-permute-done.3.own_b) | copy-start | bytes 1671172
  37.5 0.8 copy-start.11
  41.3 3.2 %collective-permute-start.13 = (bf16[128,2176]{1,0:T(8,128)(2,1)}, bf16[128,2176]{1,0:T(8,128)(2,1)}, u32[]{:S(2)}, u32[]{:S(2)}) collective-permute-start(bf16[128,2176]{1,0:T(8,128)(2,1)} %collective-permute-done.10.own_b), channel_id=1, source_target_pairs={{0,2},{1,3},{2,0},{3,1},{4,6},{5,7},{6,4},{7,5},{8,10},{9,11},{10,... | collective-permute-start | bytes 1671176 | tf_op jit(solution)/shard_map/ppermute | solution.py:164
  41.4 14.2 %collective-permute-start.9 = (bf16[64,2176]{1,0:T(8,128)(2,1)}, bf16[64,2176]{1,0:T(8,128)(2,1)}, u32[]{:S(2)}, u32[]{:S(2)}) collective-permute-start(bf16[64,2176]{1,0:T(8,128)(2,1)} %collective-permute-done.8), channel_id=1, source_target_pairs={{0,4},{1,5},{2,3},{3,2},{4,0},{5,1},{6,7},{7,6},{8,12},{9,13},{10,... | collective-permute-start | bytes 835592 | tf_op jit(solution)/shard_map/ppermute | solution.py:164
  42.9 13.8 %collective-permute-start.17 = (bf16[128,2176]{1,0:T(8,128)(2,1)}, bf16[128,2176]{1,0:T(8,128)(2,1)S(1)}, u32[]{:S(2)}, u32[]{:S(2)}) collective-permute-start(bf16[128,2176]{1,0:T(8,128)(2,1)} %pad_maximum_fusion.3.own_a), channel_id=1, source_target_pairs={{0,2},{1,3},{2,0},{3,1},{4,6},{5,7},{6,4},{7,5},{8,10},{9,11},{10,... | collective-permute-start | bytes 1671176 | tf_op jit(solution)/shard_map/ppermute | solution.py:164
  42.9 13.8 %collective-permute-start.16 = (bf16[128,2176]{1,0:T(8,128)(2,1)}, bf16[128,2176]{1,0:T(8,128)(2,1)S(1)}, u32[]{:S(2)}, u32[]{:S(2)}) collective-permute-start(bf16[128,2176]{1,0:T(8,128)(2,1)} %pad_maximum_fusion.3.own_a), channel_id=1, source_target_pairs={{0,1},{1,0},{2,6},{3,7},{4,5},{5,4},{6,2},{7,3},{8,9},{9,8},{10,14... | collective-permute-start | bytes 1671176 | tf_op jit(solution)/shard_map/ppermute | solution.py:164
  44.5 1.8 %copy-start.1 = (bf16[1,704,2048]{2,1,0:T(8,128)(2,1)S(1)}, bf16[1,704,2048]{2,1,0:T(8,128)(2,1)}, u32[]{:S(2)}) copy-start(bf16[1,704,2048]{2,1,0:T(8,128)(2,1)} %param.14) | copy-start | bytes 8650756
  46.3 1.8 %copy-start.3 = (bf16[1,704,2048]{2,1,0:T(8,128)(2,1)S(1)}, bf16[1,704,2048]{2,1,0:T(8,128)(2,1)}, u32[]{:S(2)}) copy-start(bf16[1,704,2048]{2,1,0:T(8,128)(2,1)} %param.15) | copy-start | bytes 8650756
  48.1 1.1 copy-start.6
  49.1 1.1 copy-start.12
  50.2 7.9 %copy-start.10 = (bf16[128,2176]{1,0:T(8,128)(2,1)S(1)}, bf16[128,2176]{1,0:T(8,128)(2,1)}, u32[]{:S(2)}) copy-start(bf16[128,2176]{1,0:T(8,128)(2,1)} %copy-done.9) | copy-start | bytes 1671172
  50.2 8.8 %copy-start.4 = (bf16[128,2176]{1,0:T(8,128)(2,1)S(1)}, bf16[128,2176]{1,0:T(8,128)(2,1)}, u32[]{:S(2)}) copy-start(bf16[128,2176]{1,0:T(8,128)(2,1)} %pad_maximum_fusion.3.own_a) | copy-start | bytes 1671172
  55.5 11.4 %collective-permute-start.23 = (bf16[256,2048]{1,0:T(8,128)(2,1)S(1)}, bf16[256,2048]{1,0:T(8,128)(2,1)S(1)}, u32[]{:S(2)}, u32[]{:S(2)}) collective-permute-start(bf16[256,2048]{1,0:T(8,128)(2,1)S(1)} %get-tuple-element.73), channel_id=1, source_target_pairs={{0,2},{1,3},{2,0},{3,1},{4,6},{5,7},{6,4},{7,5},{8,10},{9,11},{10,... | collective-permute-start | bytes 3145736 | tf_op jit(solution)/shard_map/ppermute | solution.py:164
  56.7 2.3 %collective-permute-start.18 = (bf16[128,2176]{1,0:T(8,128)(2,1)S(1)}, bf16[128,2176]{1,0:T(8,128)(2,1)S(1)}, u32[]{:S(2)}, u32[]{:S(2)}) collective-permute-start(bf16[128,2176]{1,0:T(8,128)(2,1)S(1)} %collective-permute-done.16.own_b), channel_id=1, source_target_pairs={{0,2},{1,3},{2,0},{3,1},{4,6},{5,7},{6,4},{7,5},{8,10},{9,11},{10,... | collective-permute-start | bytes 1671176 | tf_op jit(solution)/shard_map/ppermute | solution.py:164
  57.3 6.3 %collective-permute-start.15 = (bf16[128,2176]{1,0:T(8,128)(2,1)S(1)}, bf16[128,2176]{1,0:T(8,128)(2,1)S(1)}, u32[]{:S(2)}, u32[]{:S(2)}) collective-permute-start(bf16[128,2176]{1,0:T(8,128)(2,1)S(1)} %pad_maximum_fusion.2.own_a), channel_id=1, source_target_pairs={{0,2},{1,3},{2,0},{3,1},{4,6},{5,7},{6,4},{7,5},{8,10},{9,11},{10,... | collective-permute-start | bytes 1671176 | tf_op jit(solution)/shard_map/ppermute | solution.py:164
  57.3 9.5 %collective-permute-start.14 = (bf16[128,2176]{1,0:T(8,128)(2,1)S(1)}, bf16[128,2176]{1,0:T(8,128)(2,1)S(1)}, u32[]{:S(2)}, u32[]{:S(2)}) collective-permute-start(bf16[128,2176]{1,0:T(8,128)(2,1)S(1)} %pad_maximum_fusion.2.own_a), channel_id=1, source_target_pairs={{0,1},{1,0},{2,6},{3,7},{4,5},{5,4},{6,2},{7,3},{8,9},{9,8},{10,14... | collective-permute-start | bytes 1671176 | tf_op jit(solution)/shard_map/ppermute | solution.py:164
  58.1 15.2 %collective-permute-start.7 = (bf16[128,2176]{1,0:T(8,128)(2,1)S(1)}, bf16[128,2176]{1,0:T(8,128)(2,1)S(1)}, u32[]{:S(2)}, u32[]{:S(2)}) collective-permute-start(bf16[128,2176]{1,0:T(8,128)(2,1)S(1)} %copy-done.10), channel_id=1, source_target_pairs={{0,2},{1,3},{2,0},{3,1},{4,6},{5,7},{6,4},{7,5},{8,10},{9,11},{10,... | collective-permute-start | bytes 1671176 | tf_op jit(solution)/shard_map/ppermute | solution.py:164
  63.3 5.5 %copy-start.2 = (bf16[1,704,2048]{2,1,0:T(8,128)(2,1)S(1)}, bf16[1,704,2048]{2,1,0:T(8,128)(2,1)}, u32[]{:S(2)}) copy-start(bf16[1,704,2048]{2,1,0:T(8,128)(2,1)} %param.14) | copy-start | bytes 8650756
  63.3 14.2 %collective-permute-start.27 = (bf16[256,2048]{1,0:T(8,128)(2,1)S(1)}, bf16[256,2048]{1,0:T(8,128)(2,1)S(1)}, u32[]{:S(2)}, u32[]{:S(2)}) collective-permute-start(bf16[256,2048]{1,0:T(8,128)(2,1)S(1)} %get-tuple-element.84), channel_id=1, source_target_pairs={{0,2},{1,3},{2,0},{3,1},{4,6},{5,7},{6,4},{7,5},{8,10},{9,11},{10,... | collective-permute-start | bytes 3145736 | tf_op jit(solution)/shard_map/ppermute | solution.py:164
  66.9 2.0 %collective-permute-start.19 = (bf16[128,2176]{1,0:T(8,128)(2,1)S(1)}, bf16[128,2176]{1,0:T(8,128)(2,1)S(1)}, u32[]{:S(2)}, u32[]{:S(2)}) collective-permute-start(bf16[128,2176]{1,0:T(8,128)(2,1)S(1)} %collective-permute-done.14.own_b), channel_id=1, source_target_pairs={{0,2},{1,3},{2,0},{3,1},{4,6},{5,7},{6,4},{7,5},{8,10},{9,11},{10,... | collective-permute-start | bytes 1671176 | tf_op jit(solution)/shard_map/ppermute | solution.py:164
  67.3 9.2 %collective-permute-start.24 = (bf16[128,2048]{1,0:T(8,128)(2,1)S(1)}, bf16[128,2048]{1,0:T(8,128)(2,1)S(1)}, u32[]{:S(2)}, u32[]{:S(2)}) collective-permute-start(bf16[128,2048]{1,0:T(8,128)(2,1)S(1)} %slice.69), channel_id=1, source_target_pairs={{0,1},{1,0},{2,6},{3,7},{4,5},{5,4},{6,2},{7,3},{8,9},{9,8},{10,14... | collective-permute-start | bytes 1572872 | tf_op jit(solution)/shard_map/ppermute | solution.py:164
  73.1 15.7 %collective-permute-start.31 = (bf16[256,2048]{1,0:T(8,128)(2,1)S(1)}, bf16[256,2048]{1,0:T(8,128)(2,1)S(1)}, u32[]{:S(2)}, u32[]{:S(2)}) collective-permute-start(bf16[256,2048]{1,0:T(8,128)(2,1)S(1)} %get-tuple-element.94), channel_id=1, source_target_pairs={{0,2},{1,3},{2,0},{3,1},{4,6},{5,7},{6,4},{7,5},{8,10},{9,11},{10,... | collective-permute-start | bytes 3145736 | tf_op jit(solution)/shard_map/ppermute | solution.py:164
  76.7 2.8 %copy-start.8 = (bf16[128,2176]{1,0:T(8,128)(2,1)S(1)}, bf16[128,2176]{1,0:T(8,128)(2,1)}, u32[]{:S(2)}) copy-start(bf16[128,2176]{1,0:T(8,128)(2,1)} %copy-done.7) | copy-start | bytes 1671172
  76.7 9.2 %collective-permute-start.25 = (bf16[64,2048]{1,0:T(8,128)(2,1)S(1)}, bf16[64,2048]{1,0:T(8,128)(2,1)S(1)}, u32[]{:S(2)}, u32[]{:S(2)}) collective-permute-start(bf16[64,2048]{1,0:T(8,128)(2,1)S(1)} %slice.71), channel_id=1, source_target_pairs={{0,4},{1,5},{2,3},{3,2},{4,0},{5,1},{6,7},{7,6},{8,12},{9,13},{10,... | collective-permute-start | bytes 786440 | tf_op jit(solution)/shard_map/ppermute | solution.py:164
  77.9 10.1 %collective-permute-start.28 = (bf16[128,2048]{1,0:T(8,128)(2,1)S(1)}, bf16[128,2048]{1,0:T(8,128)(2,1)S(1)}, u32[]{:S(2)}, u32[]{:S(2)}) collective-permute-start(bf16[128,2048]{1,0:T(8,128)(2,1)S(1)} %slice.73), channel_id=1, source_target_pairs={{0,1},{1,0},{2,6},{3,7},{4,5},{5,4},{6,2},{7,3},{8,9},{9,8},{10,14... | collective-permute-start | bytes 1572872 | tf_op jit(solution)/shard_map/ppermute | solution.py:164
  84.0 7.0 %collective-permute-start.20 = (bf16[256,2048]{1,0:T(8,128)(2,1)S(1)}, bf16[256,2048]{1,0:T(8,128)(2,1)S(1)}, u32[]{:S(2)}, u32[]{:S(2)}) collective-permute-start(bf16[256,2048]{1,0:T(8,128)(2,1)S(1)} %get-tuple-element.102), channel_id=1, source_target_pairs={{0,2},{1,3},{2,0},{3,1},{4,6},{5,7},{6,4},{7,5},{8,10},{9,11},{10,... | collective-permute-start | bytes 3145736 | tf_op jit(solution)/shard_map/ppermute | solution.py:164
  86.0 26.3 %collective-permute-start.26 = (bf16[64,2048]{1,0:T(8,128)(2,1)S(1)}, bf16[64,2048]{1,0:T(8,128)(2,1)S(1)}, u32[]{:S(2)}, u32[]{:S(2)}) collective-permute-start(bf16[64,2048]{1,0:T(8,128)(2,1)S(1)} %add_convert_fusion.11), channel_id=1, source_target_pairs={{0,16},{1,17},{2,18},{3,19},{4,20},{5,21},{6,22},{7,23},{8,0},{9,1... | collective-permute-start | bytes 786440 | tf_op jit(solution)/shard_map/ppermute | solution.py:164
  88.2 8.8 %collective-permute-start.29 = (bf16[64,2048]{1,0:T(8,128)(2,1)S(1)}, bf16[64,2048]{1,0:T(8,128)(2,1)S(1)}, u32[]{:S(2)}, u32[]{:S(2)}) collective-permute-start(bf16[64,2048]{1,0:T(8,128)(2,1)S(1)} %slice.75), channel_id=1, source_target_pairs={{0,4},{1,5},{2,3},{3,2},{4,0},{5,1},{6,7},{7,6},{8,12},{9,13},{10,... | collective-permute-start | bytes 786440 | tf_op jit(solution)/shard_map/ppermute | solution.py:164
  89.2 12.0 %collective-permute-start.32 = (bf16[128,2048]{1,0:T(8,128)(2,1)S(1)}, bf16[128,2048]{1,0:T(8,128)(2,1)S(1)}, u32[]{:S(2)}, u32[]{:S(2)}) collective-permute-start(bf16[128,2048]{1,0:T(8,128)(2,1)S(1)} %slice.77), channel_id=1, source_target_pairs={{0,1},{1,0},{2,6},{3,7},{4,5},{5,4},{6,2},{7,3},{8,9},{9,8},{10,14... | collective-permute-start | bytes 1572872 | tf_op jit(solution)/shard_map/ppermute | solution.py:164
  91.5 15.5 %collective-permute-start.21 = (bf16[128,2048]{1,0:T(8,128)(2,1)S(1)}, bf16[128,2048]{1,0:T(8,128)(2,1)S(1)}, u32[]{:S(2)}, u32[]{:S(2)}) collective-permute-start(bf16[128,2048]{1,0:T(8,128)(2,1)S(1)} %slice.65), channel_id=1, source_target_pairs={{0,1},{1,0},{2,6},{3,7},{4,5},{5,4},{6,2},{7,3},{8,9},{9,8},{10,14... | collective-permute-start | bytes 1572872 | tf_op jit(solution)/shard_map/ppermute | solution.py:164
  97.1 15.2 %collective-permute-start.30 = (bf16[64,2048]{1,0:T(8,128)(2,1)S(1)}, bf16[64,2048]{1,0:T(8,128)(2,1)S(1)}, u32[]{:S(2)}, u32[]{:S(2)}) collective-permute-start(bf16[64,2048]{1,0:T(8,128)(2,1)S(1)} %add_convert_fusion.10), channel_id=1, source_target_pairs={{0,24},{1,25},{2,26},{3,27},{4,28},{5,29},{6,30},{7,31},{8,16},{9,... | collective-permute-start | bytes 786440 | tf_op jit(solution)/shard_map/ppermute | solution.py:164
  101.3 16.5 %copy-start.13 = (bf16[64,2048]{1,0:T(8,128)(2,1)S(1)}, bf16[64,2048]{1,0:T(8,128)(2,1)}, u32[]{:S(2)}) copy-start(bf16[64,2048]{1,0:T(8,128)(2,1)} %get-tuple-element.54) | copy-start | bytes 786436
  101.4 7.4 %collective-permute-start.33 = (bf16[64,2048]{1,0:T(8,128)(2,1)S(1)}, bf16[64,2048]{1,0:T(8,128)(2,1)S(1)}, u32[]{:S(2)}, u32[]{:S(2)}) collective-permute-start(bf16[64,2048]{1,0:T(8,128)(2,1)S(1)} %slice.79), channel_id=1, source_target_pairs={{0,4},{1,5},{2,3},{3,2},{4,0},{5,1},{6,7},{7,6},{8,12},{9,13},{10,... | collective-permute-start | bytes 786440 | tf_op jit(solution)/shard_map/ppermute | solution.py:164
  107.1 6.4 %collective-permute-start.22 = (bf16[64,2048]{1,0:T(8,128)(2,1)S(1)}, bf16[64,2048]{1,0:T(8,128)(2,1)S(1)}, u32[]{:S(2)}, u32[]{:S(2)}) collective-permute-start(bf16[64,2048]{1,0:T(8,128)(2,1)S(1)} %slice.67), channel_id=1, source_target_pairs={{0,4},{1,5},{2,3},{3,2},{4,0},{5,1},{6,7},{7,6},{8,12},{9,13},{10,... | collective-permute-start | bytes 786440 | tf_op jit(solution)/shard_map/ppermute | solution.py:164
  108.9 9.0 %collective-permute-start.34 = (bf16[64,2048]{1,0:T(8,128)(2,1)S(1)}, bf16[64,2048]{1,0:T(8,128)(2,1)S(1)}, u32[]{:S(2)}, u32[]{:S(2)}) collective-permute-start(bf16[64,2048]{1,0:T(8,128)(2,1)S(1)} %add_convert_fusion.9), channel_id=1, source_target_pairs={{0,8},{1,9},{2,10},{3,11},{4,12},{5,13},{6,14},{7,15},{8,24},{9,25... | collective-permute-start | bytes 786440 | tf_op jit(solution)/shard_map/ppermute | solution.py:164
  (2 other events, 1.5 us)

commit v5 on v4

--- a/solution.py
+++ b/solution.py
@@ -178,12 +178,13 @@
     def add(*terms):
         return functools.reduce(lambda a, b: a + b, [t.astype(F32) for t in terms])
 
-    last = []
+    last, tied = [], [True]
 
     def in_turn(value):
-        if last:
-            value, _ = lax.optimization_barrier((value, last[0]))
-        last[:] = [value]
+        if tied[0]:
+            if last:
+                value, _ = lax.optimization_barrier((value, last[0]))
+            last[:] = [value]
         return value
 
     theirs = lax.dynamic_slice_in_dim(attn_out, (1 - half) * my_rows, my_rows, 0)
@@ -214,44 +215,49 @@
         came[step] = sibling(out[step][1])
 
     def merge_cores(step):
-        total[step] = (add(out[step][0], came[step]).astype(BF16))
+        total[step] = in_turn(add(out[step][0], came[step]).astype(BF16))
         other[step] = second(total[step][2 * my_rows :])
 
     def merge_second(step):
-        kept[step] = (add(total[step][: 2 * my_rows], other[step]).astype(BF16))
+        kept[step] = in_turn(add(total[step][: 2 * my_rows], other[step]).astype(BF16))
         one[step] = first(kept[step][my_rows:])
 
     def merge_first(step):
-        value = (add(kept[step][:my_rows], one[step]).astype(BF16))
+        value = in_turn(add(kept[step][:my_rows], one[step]).astype(BF16))
         home[step] = returns[step](value)
 
-    spread(0)
-    spread(1)
-    widen(0)
-    spread(2)
-    widen(1)
-    share(0)
-    spread(3)
-    widen(2)
-    share(1)
-    run(1)
-    widen(3)
-    share(2)
-    run(2)
-    share(3)
-    run(3)
-    run(0)
-    merge_cores(1)
-    merge_cores(2)
-    merge_cores(3)
-    merge_cores(0)
-    merge_second(1)
-    merge_second(2)
-    merge_second(3)
-    merge_second(0)
-    merge_first(1)
-    merge_first(2)
-    merge_first(3)
+    schedule = [
+        (spread, 0, True),
+        (spread, 1, True),
+        (widen, 0, True),
+        (spread, 2, True),
+        (widen, 1, True),
+        (share, 0, True),
+        (spread, 3, True),
+        (widen, 2, True),
+        (widen, 3, False),
+        (share, 1, True),
+        (run, 1, True),
+        (share, 2, True),
+        (run, 2, True),
+        (share, 3, True),
+        (run, 3, True),
+        (run, 0, True),
+        (merge_cores, 1, False),
+        (merge_second, 1, False),
+        (merge_cores, 2, False),
+        (merge_second, 2, False),
+        (merge_first, 2, False),
+        (merge_cores, 3, False),
+        (merge_first, 1, True),
+        (merge_second, 3, False),
+        (merge_first, 3, False),
+        (merge_cores, 0, True),
+        (merge_second, 0, True),
+    ]
+    for take, step, tie in schedule:
+        tied[0] = tie
+        take(step)
     return add(hidden, kept[0][:my_rows], one[0], *(home[step] for step in range(1, planes))).astype(BF16)
 
 
@@ -283,7 +289,7 @@
 
 def solution(mesh):
     ep_count, tp_count = mesh.shape["ep"], mesh.shape["tp"]
-    paired = tp_count == 2 and ep_count % 4 == 0 and ep_count <= LANES // 2
+    paired = tp_count == 2 and divmod(ep_count, 4) == (4, 0)
     plan = gathered_plan if paired else exchanged_plan
 
     def per_device(*arguments):

time: 119 us -> 118 us (level)
    concatenate x4 -> x3, other arithmetic: 2.98 us -> 1.88 us  [widen(): two[step] = in_turn(jnp.concatenate([piece[step], one[step]], axis=0))]
    unnamed x32 -> x35, local copies, waits for them, and re-layouts: 11.8 us -> 11.9 us
  transfers between devices with their start and end apart: 35 -> 35, of which waited for: 16 -> 16; matrix products, arithmetic and copies ran while one was open for 7% -> 6% of each run, Pallas kernels for 15% -> 16%
where the time goes in v5:
time: 118 us
  waiting for transfers between devices  41.9 us (36%)
  starting transfers between devices  36 us (31%)
  Pallas kernels  21.6 us (18%)
  local copies, waits for them, and re-layouts  13.1 us (11%)
  other arithmetic  5.06 us (4%)
    ppermute x35, waiting for transfers between devices, routes(): return lambda a: lax.ppermute(a, AXES, pairs)  41.9 us
    ppermute x35, starting transfers between devices, routes(): return lambda a: lax.ppermute(a, AXES, pairs)  36 us
    pallas_call x4, Pallas kernels, experts(): pl.pallas_call(expert_kernel, out_shape=(result, result), in_specs=[SMEM]...  19.4 us
    unnamed x35, local copies, waits for them, and re-layouts  11.9 us
  transfers between devices with their start and end apart: 35, of which 16 were waited for; matrix products, arithmetic and copies ran while one was open for 6% of the time, Pallas kernels for 16%

profile of v5, /device:TPU:0, one launch (start us, length us, event | category | flops | bytes accessed | tf_op | source)
XLA Modules:
  0.0 117.9 jit_solution(11774332098327303527)
XLA Ops:
  0.0 0.9 constant_dynamic-slice_fusion
  0.9 3.0 %collective-permute-start = (bf16[64,1024]{1,0:T(8,128)(2,1)S(1)}, bf16[64,1024]{1,0:T(8,128)(2,1)S(1)}, u32[]{:S(2)}, u32[]{:S(2)}) collective-permute-start(bf16[64,1024]{1,0:T(8,128)(2,1)S(1)} %constant_dynamic-slice_fusion), channel_id=1, source_target_pairs={{0,1},{1,0},{2,3},{3,2},{4,5},{5,4},{6,7},{7,6},{8,9},{9,8},{10,11... | collective-permute-start | bytes 393224 | tf_op jit(solution)/shard_map/ppermute | solution.py:164
  3.9 1.4 %copy.9.ids_ref = s32[128,6]{1,0:T(8,128)} copy(s32[128,6]{0,1:T(8,128)} %param.11) | data formatting | bytes 6144 | tf_op args[3]
  5.4 1.6 %copy.10.gates_ref = f32[128,6]{1,0:T(8,128)} copy(f32[128,6]{0,1:T(8,128)} %param.12) | data formatting | bytes 6144 | tf_op args[4]
  8.1 2.2 %shard_map.82 = (bf16[64,2176]{1,0:T(8,128)(2,1)}, bf16[64,2048]{1,0:T(8,128)(2,1)}) custom-call(s32[1]{0:T(128)} %bitcast.half_ref, bf16[128,1024]{1,0:T(8,128)(2,1)} %attn_ref.1, bf16[64,1024]{1,0:T(8,128)(2,1)} %copy-done.15, bf16[64,2048]{1,0:T(8,128)(2,1)} %resid_ref.1, f32[1,2048]{1,0:T(1,128)} %bitcast.18, s32[128,6]{1,0:T(8,128)} %copy.9.ids_ref, ...), custom_call_target="tpu_custom_call" | custom-call | tf_op jit(solution)/shard_map/pallas_call | solution.py:77
  10.3 1.8 %collective-permute-start.2 = (bf16[64,2176]{1,0:T(8,128)(2,1)}, bf16[64,2176]{1,0:T(8,128)(2,1)S(1)}, u32[]{:S(2)}, u32[]{:S(2)}) collective-permute-start(bf16[64,2176]{1,0:T(8,128)(2,1)} %get-tuple-element.57), channel_id=1, source_target_pairs={{0,8},{1,9},{2,10},{3,11},{4,12},{5,13},{6,14},{7,15},{8,24},{9,25... | collective-permute-start | bytes 835592 | tf_op jit(solution)/shard_map/ppermute | solution.py:164
  12.1 1.5 %collective-permute-start.1 = (bf16[64,2176]{1,0:T(8,128)(2,1)}, bf16[64,2176]{1,0:T(8,128)(2,1)S(1)}, u32[]{:S(2)}, u32[]{:S(2)}) collective-permute-start(bf16[64,2176]{1,0:T(8,128)(2,1)} %get-tuple-element.57), channel_id=1, source_target_pairs={{0,4},{1,5},{2,3},{3,2},{4,0},{5,1},{6,7},{7,6},{8,12},{9,13},{10,... | collective-permute-start | bytes 835592 | tf_op jit(solution)/shard_map/ppermute | solution.py:164
  13.6 5.7 %collective-permute-done.2 = bf16[64,2176]{1,0:T(8,128)(2,1)S(1)} collective-permute-done((bf16[64,2176]{1,0:T(8,128)(2,1)}, bf16[64,2176]{1,0:T(8,128)(2,1)S(1)}, u32[]{:S(2)}, u32[]{:S(2)}) %collective-permute-start.2) | collective-permute-done | bytes 278560 | tf_op jit(solution)/shard_map/ppermute | solution.py:164
  19.3 0.8 collective-permute-start.6
  20.0 1.5 %collective-permute-start.5 = (bf16[64,2176]{1,0:T(8,128)(2,1)S(1)}, bf16[64,2176]{1,0:T(8,128)(2,1)S(1)}, u32[]{:S(2)}, u32[]{:S(2)}) collective-permute-start(bf16[64,2176]{1,0:T(8,128)(2,1)S(1)} %collective-permute-done.2), channel_id=1, source_target_pairs={{0,4},{1,5},{2,3},{3,2},{4,0},{5,1},{6,7},{7,6},{8,12},{9,13},{10,... | collective-permute-start | bytes 835592 | tf_op jit(solution)/shard_map/ppermute | solution.py:164
  21.5 1.0 pad_maximum_fusion.own_a
  22.6 1.6 %collective-permute-start.3 = (bf16[128,2176]{1,0:T(8,128)(2,1)S(1)}, bf16[128,2176]{1,0:T(8,128)(2,1)S(1)}, u32[]{:S(2)}, u32[]{:S(2)}) collective-permute-start(bf16[128,2176]{1,0:T(8,128)(2,1)S(1)} %pad_maximum_fusion.own_a), channel_id=1, source_target_pairs={{0,1},{1,0},{2,6},{3,7},{4,5},{5,4},{6,2},{7,3},{8,9},{9,8},{10,14... | collective-permute-start | bytes 1671176 | tf_op jit(solution)/shard_map/ppermute | solution.py:164
  24.2 2.9 %collective-permute-done.6 = bf16[64,2176]{1,0:T(8,128)(2,1)S(1)} collective-permute-done((bf16[64,2176]{1,0:T(8,128)(2,1)S(1)}, bf16[64,2176]{1,0:T(8,128)(2,1)S(1)}, u32[]{:S(2)}, u32[]{:S(2)}) %collective-permute-start.6) | collective-permute-done | bytes 278560 | tf_op jit(solution)/shard_map/ppermute | solution.py:164
  27.1 1.1 collective-permute-start.12
  28.2 0.8 collective-permute-start.8
  29.1 0.8 copy-done.6
  29.9 1.5 %collective-permute-start.15 = (bf16[128,2176]{1,0:T(8,128)(2,1)S(1)}, bf16[128,2176]{1,0:T(8,128)(2,1)}, u32[]{:S(2)}, u32[]{:S(2)}) collective-permute-start(bf16[128,2176]{1,0:T(8,128)(2,1)S(1)} %pad_maximum_fusion.1.own_a), channel_id=1, source_target_pairs={{0,1},{1,0},{2,6},{3,7},{4,5},{5,4},{6,2},{7,3},{8,9},{9,8},{10,14... | collective-permute-start | bytes 1671176 | tf_op jit(solution)/shard_map/ppermute | solution.py:164
  31.4 0.8 copy-done.4
  32.2 3.0 %collective-permute-done.3.own_b = bf16[128,2176]{1,0:T(8,128)(2,1)S(1)} collective-permute-done((bf16[128,2176]{1,0:T(8,128)(2,1)S(1)}, bf16[128,2176]{1,0:T(8,128)(2,1)S(1)}, u32[]{:S(2)}, u32[]{:S(2)}) %collective-permute-start.3) | collective-permute-done | bytes 557088 | tf_op jit(solution)/shard_map/ppermute | solution.py:164
  35.6 1.1 collective-permute-done.12
  36.7 0.8 pad_maximum_fusion.2.own_a
  37.5 0.8 copy-done.10
  38.4 2.9 %collective-permute-done.15.own_b = bf16[128,2176]{1,0:T(8,128)(2,1)} collective-permute-done((bf16[128,2176]{1,0:T(8,128)(2,1)S(1)}, bf16[128,2176]{1,0:T(8,128)(2,1)}, u32[]{:S(2)}, u32[]{:S(2)}) %collective-permute-start.15) | collective-permute-done | bytes 557088 | tf_op jit(solution)/shard_map/ppermute | solution.py:164
  41.8 1.4 %collective-permute-start.13 = (bf16[128,2176]{1,0:T(8,128)(2,1)}, bf16[128,2176]{1,0:T(8,128)(2,1)}, u32[]{:S(2)}, u32[]{:S(2)}) collective-permute-start(bf16[128,2176]{1,0:T(8,128)(2,1)} %pad_maximum_fusion.2.own_a), channel_id=1, source_target_pairs={{0,1},{1,0},{2,6},{3,7},{4,5},{5,4},{6,2},{7,3},{8,9},{9,8},{10,14... | collective-permute-start | bytes 1671176 | tf_op jit(solution)/shard_map/ppermute | solution.py:164
  43.2 1.4 %collective-permute-start.9 = (bf16[64,2176]{1,0:T(8,128)(2,1)}, bf16[64,2176]{1,0:T(8,128)(2,1)S(1)}, u32[]{:S(2)}, u32[]{:S(2)}) collective-permute-start(bf16[64,2176]{1,0:T(8,128)(2,1)} %copy-done.12), channel_id=1, source_target_pairs={{0,4},{1,5},{2,3},{3,2},{4,0},{5,1},{6,7},{7,6},{8,12},{9,13},{10,... | collective-permute-start | bytes 835592 | tf_op jit(solution)/shard_map/ppermute | solution.py:164
  44.5 1.8 %copy-done.1 = bf16[1,704,2048]{2,1,0:T(8,128)(2,1)S(1)} copy-done((bf16[1,704,2048]{2,1,0:T(8,128)(2,1)S(1)}, bf16[1,704,2048]{2,1,0:T(8,128)(2,1)}, u32[]{:S(2)}) %copy-start.1) | copy-done | bytes 2883608
  46.4 1.8 %copy-done.3 = bf16[1,704,2048]{2,1,0:T(8,128)(2,1)S(1)} copy-done((bf16[1,704,2048]{2,1,0:T(8,128)(2,1)S(1)}, bf16[1,704,2048]{2,1,0:T(8,128)(2,1)}, u32[]{:S(2)}) %copy-start.3) | copy-done | bytes 2883608
  48.2 1.1 copy-done.5
  49.2 1.1 copy-done.11
  50.3 5.4 %shard_map.83 = (bf16[256,2048]{1,0:T(8,128)(2,1)S(1)}, bf16[256,2048]{1,0:T(8,128)(2,1)S(1)}) custom-call(s32[1]{0:T(128)} %bitcast.2.me_ref, bf16[128,2176]{1,0:T(8,128)(2,1)S(1)} %copy-done.5, bf16[128,2176]{1,0:T(8,128)(2,1)} %collective-permute-done.15.own_b, bf16[128,2176]{1,0:T(8,128)(2,1)S(1)} %copy-done.11, ...), custom_call_target="tpu_custom_call" | custom-call | flops 2214592512 | bytes 4194304 | tf_op jit(solution)/shard_map/pallas_call | solution.py:134
  57.3 2.8 %collective-permute-done.18.sib_b = bf16[128,2176]{1,0:T(8,128)(2,1)S(1)} collective-permute-done((bf16[128,2176]{1,0:T(8,128)(2,1)}, bf16[128,2176]{1,0:T(8,128)(2,1)S(1)}, u32[]{:S(2)}, u32[]{:S(2)}) %collective-permute-start.18) | collective-permute-done | bytes 557088 | tf_op jit(solution)/shard_map/ppermute | solution.py:164
  60.1 5.3 %shard_map.84 = (bf16[256,2048]{1,0:T(8,128)(2,1)S(1)}, bf16[256,2048]{1,0:T(8,128)(2,1)S(1)}) custom-call(s32[1]{0:T(128)} %bitcast.2.me_ref, bf16[128,2176]{1,0:T(8,128)(2,1)} %pad_maximum_fusion.2.own_a, bf16[128,2176]{1,0:T(8,128)(2,1)} %collective-permute-done.13.own_b, bf16[128,2176]{1,0:T(8,128)(2,1)} %collective-permute-done.14.sib_a, ...), custom_call_target="tpu_custom_call" | custom-call | flops 2214592512 | bytes 4194304 | tf_op jit(solution)/shard_map/pallas_call | solution.py:134
  67.3 1.7 %collective-permute-done.19.sib_b = bf16[128,2176]{1,0:T(8,128)(2,1)S(1)} collective-permute-done((bf16[128,2176]{1,0:T(8,128)(2,1)S(1)}, bf16[128,2176]{1,0:T(8,128)(2,1)S(1)}, u32[]{:S(2)}, u32[]{:S(2)}) %collective-permute-start.19) | collective-permute-done | bytes 557088 | tf_op jit(solution)/shard_map/ppermute | solution.py:164
  69.0 4.3 %shard_map.85 = (bf16[256,2048]{1,0:T(8,128)(2,1)S(1)}, bf16[256,2048]{1,0:T(8,128)(2,1)S(1)}) custom-call(s32[1]{0:T(128)} %bitcast.2.me_ref, bf16[128,2176]{1,0:T(8,128)(2,1)S(1)} %constant_dynamic-update-slice_fusion.own_a, bf16[128,2176]{1,0:T(8,128)(2,1)S(1)} %collective-permute-done.10.own_b, bf16[128,2176]{1,0:T(8,128)(2,1)S(1)} %collective-permute-done.11.sib_a, ...), custom_call_target="tpu_custom_call" | custom-call | flops 2214592512 | bytes 4194304 | tf_op jit(solution)/shard_map/pallas_call | solution.py:134
  73.5 2.3 %collective-permute-done.22 = bf16[128,2048]{1,0:T(8,128)(2,1)S(1)} collective-permute-done((bf16[128,2048]{1,0:T(8,128)(2,1)S(1)}, bf16[128,2048]{1,0:T(8,128)(2,1)S(1)}, u32[]{:S(2)}, u32[]{:S(2)}) %collective-permute-start.22) | collective-permute-done | bytes 524320 | tf_op jit(solution)/shard_map/ppermute | solution.py:164
  77.2 1.5 %collective-permute-start.28 = (bf16[128,2048]{1,0:T(8,128)(2,1)S(1)}, bf16[128,2048]{1,0:T(8,128)(2,1)S(1)}, u32[]{:S(2)}, u32[]{:S(2)}) collective-permute-start(bf16[128,2048]{1,0:T(8,128)(2,1)S(1)} %slice.69), channel_id=1, source_target_pairs={{0,1},{1,0},{2,6},{3,7},{4,5},{5,4},{6,2},{7,3},{8,9},{9,8},{10,14... | collective-permute-start | bytes 1572872 | tf_op jit(solution)/shard_map/ppermute | solution.py:164
  78.7 4.4 %shard_map.86 = (bf16[256,2048]{1,0:T(8,128)(2,1)S(1)}, bf16[256,2048]{1,0:T(8,128)(2,1)S(1)}) custom-call(s32[1]{0:T(128)} %bitcast.2.me_ref, bf16[128,2176]{1,0:T(8,128)(2,1)S(1)} %pad_maximum_fusion.own_a, bf16[128,2176]{1,0:T(8,128)(2,1)S(1)} %copy-done.9, bf16[128,2176]{1,0:T(8,128)(2,1)S(1)} %copy-done.7, ...), custom_call_target="tpu_custom_call" | custom-call | flops 2214592512 | bytes 4194304 | tf_op jit(solution)/shard_map/pallas_call | solution.py:134
  83.2 1.9 %collective-permute-done.23 = bf16[64,2048]{1,0:T(8,128)(2,1)S(1)} collective-permute-done((bf16[64,2048]{1,0:T(8,128)(2,1)S(1)}, bf16[64,2048]{1,0:T(8,128)(2,1)S(1)}, u32[]{:S(2)}, u32[]{:S(2)}) %collective-permute-start.23) | collective-permute-done | bytes 262176 | tf_op jit(solution)/shard_map/ppermute | solution.py:164
  85.2 2.1 %collective-permute-start.26 = (bf16[64,2048]{1,0:T(8,128)(2,1)S(1)}, bf16[64,2048]{1,0:T(8,128)(2,1)S(1)}, u32[]{:S(2)}, u32[]{:S(2)}) collective-permute-start(bf16[64,2048]{1,0:T(8,128)(2,1)S(1)} %add_convert_fusion.11), channel_id=1, source_target_pairs={{0,16},{1,17},{2,18},{3,19},{4,20},{5,21},{6,22},{7,23},{8,0},{9,1... | collective-permute-start | bytes 786440 | tf_op jit(solution)/shard_map/ppermute | solution.py:164
  88.5 1.7 %collective-permute-start.32 = (bf16[128,2048]{1,0:T(8,128)(2,1)S(1)}, bf16[128,2048]{1,0:T(8,128)(2,1)S(1)}, u32[]{:S(2)}, u32[]{:S(2)}) collective-permute-start(bf16[128,2048]{1,0:T(8,128)(2,1)S(1)} %slice.73), channel_id=1, source_target_pairs={{0,1},{1,0},{2,6},{3,7},{4,5},{5,4},{6,2},{7,3},{8,9},{9,8},{10,14... | collective-permute-start | bytes 1572872 | tf_op jit(solution)/shard_map/ppermute | solution.py:164
  91.1 5.2 %collective-permute-done.29 = bf16[64,2048]{1,0:T(8,128)(2,1)S(1)} collective-permute-done((bf16[64,2048]{1,0:T(8,128)(2,1)S(1)}, bf16[64,2048]{1,0:T(8,128)(2,1)S(1)}, u32[]{:S(2)}, u32[]{:S(2)}) %collective-permute-start.29) | collective-permute-done | bytes 262176 | tf_op jit(solution)/shard_map/ppermute | solution.py:164
  96.3 4.0 %collective-permute-start.30 = (bf16[64,2048]{1,0:T(8,128)(2,1)S(1)}, bf16[64,2048]{1,0:T(8,128)(2,1)S(1)}, u32[]{:S(2)}, u32[]{:S(2)}) collective-permute-start(bf16[64,2048]{1,0:T(8,128)(2,1)S(1)} %add_convert_fusion.10), channel_id=1, source_target_pairs={{0,24},{1,25},{2,26},{3,27},{4,28},{5,29},{6,30},{7,31},{8,16},{9,... | collective-permute-start | bytes 786440 | tf_op jit(solution)/shard_map/ppermute | solution.py:164
  100.7 5.4 %collective-permute-done.24 = bf16[128,2048]{1,0:T(8,128)(2,1)S(1)} collective-permute-done((bf16[128,2048]{1,0:T(8,128)(2,1)S(1)}, bf16[128,2048]{1,0:T(8,128)(2,1)S(1)}, u32[]{:S(2)}, u32[]{:S(2)}) %collective-permute-start.24) | collective-permute-done | bytes 524320 | tf_op jit(solution)/shard_map/ppermute | solution.py:164
  106.2 1.8 %collective-permute-start.25 = (bf16[64,2048]{1,0:T(8,128)(2,1)S(1)}, bf16[64,2048]{1,0:T(8,128)(2,1)S(1)}, u32[]{:S(2)}, u32[]{:S(2)}) collective-permute-start(bf16[64,2048]{1,0:T(8,128)(2,1)S(1)} %slice.55), channel_id=1, source_target_pairs={{0,4},{1,5},{2,3},{3,2},{4,0},{5,1},{6,7},{7,6},{8,12},{9,13},{10,... | collective-permute-start | bytes 786440 | tf_op jit(solution)/shard_map/ppermute | solution.py:164
  108.1 3.2 %collective-permute-start.34 = (bf16[64,2048]{1,0:T(8,128)(2,1)S(1)}, bf16[64,2048]{1,0:T(8,128)(2,1)S(1)}, u32[]{:S(2)}, u32[]{:S(2)}) collective-permute-start(bf16[64,2048]{1,0:T(8,128)(2,1)S(1)} %add_convert_fusion.9), channel_id=1, source_target_pairs={{0,8},{1,9},{2,10},{3,11},{4,12},{5,13},{6,14},{7,15},{8,24},{9,25... | collective-permute-start | bytes 786440 | tf_op jit(solution)/shard_map/ppermute | solution.py:164
  111.3 1.3 %collective-permute-done.25 = bf16[64,2048]{1,0:T(8,128)(2,1)S(1)} collective-permute-done((bf16[64,2048]{1,0:T(8,128)(2,1)S(1)}, bf16[64,2048]{1,0:T(8,128)(2,1)S(1)}, u32[]{:S(2)}, u32[]{:S(2)}) %collective-permute-start.25) | collective-permute-done | bytes 262176 | tf_op jit(solution)/shard_map/ppermute | solution.py:164
  112.6 4.4 %collective-permute-done.34 = bf16[64,2048]{1,0:T(8,128)(2,1)S(1)} collective-permute-done((bf16[64,2048]{1,0:T(8,128)(2,1)S(1)}, bf16[64,2048]{1,0:T(8,128)(2,1)S(1)}, u32[]{:S(2)}, u32[]{:S(2)}) %collective-permute-start.34) | collective-permute-done | bytes 262176 | tf_op jit(solution)/shard_map/ppermute | solution.py:164
  117.0 0.9 add_convert_fusion.8
  (87 shorter events, 10.1 us)
Async XLA Ops:
  0.9 6.5 %collective-permute-start = (bf16[64,1024]{1,0:T(8,128)(2,1)S(1)}, bf16[64,1024]{1,0:T(8,128)(2,1)S(1)}, u32[]{:S(2)}, u32[]{:S(2)}) collective-permute-start(bf16[64,1024]{1,0:T(8,128)(2,1)S(1)} %constant_dynamic-slice_fusion), channel_id=1, source_target_pairs={{0,1},{1,0},{2,3},{3,2},{4,5},{5,4},{6,7},{7,6},{8,9},{9,8},{10,11... | collective-permute-start | bytes 393224 | tf_op jit(solution)/shard_map/ppermute | solution.py:164
  5.4 39.2 %copy-start = (bf16[1,704,2048]{2,1,0:T(8,128)(2,1)S(1)}, bf16[1,704,2048]{2,1,0:T(8,128)(2,1)}, u32[]{:S(2)}) copy-start(bf16[1,704,2048]{2,1,0:T(8,128)(2,1)} %param.13) | copy-start | bytes 8650756
  10.3 9.0 %collective-permute-start.2 = (bf16[64,2176]{1,0:T(8,128)(2,1)}, bf16[64,2176]{1,0:T(8,128)(2,1)S(1)}, u32[]{:S(2)}, u32[]{:S(2)}) collective-permute-start(bf16[64,2176]{1,0:T(8,128)(2,1)} %get-tuple-element.57), channel_id=1, source_target_pairs={{0,8},{1,9},{2,10},{3,11},{4,12},{5,13},{6,14},{7,15},{8,24},{9,25... | collective-permute-start | bytes 835592 | tf_op jit(solution)/shard_map/ppermute | solution.py:164
  12.1 9.4 %collective-permute-start.1 = (bf16[64,2176]{1,0:T(8,128)(2,1)}, bf16[64,2176]{1,0:T(8,128)(2,1)S(1)}, u32[]{:S(2)}, u32[]{:S(2)}) collective-permute-start(bf16[64,2176]{1,0:T(8,128)(2,1)} %get-tuple-element.57), channel_id=1, source_target_pairs={{0,4},{1,5},{2,3},{3,2},{4,0},{5,1},{6,7},{7,6},{8,12},{9,13},{10,... | collective-permute-start | bytes 835592 | tf_op jit(solution)/shard_map/ppermute | solution.py:164
  19.3 7.8 %collective-permute-start.6 = (bf16[64,2176]{1,0:T(8,128)(2,1)S(1)}, bf16[64,2176]{1,0:T(8,128)(2,1)S(1)}, u32[]{:S(2)}, u32[]{:S(2)}) collective-permute-start(bf16[64,2176]{1,0:T(8,128)(2,1)S(1)} %collective-permute-done.2), channel_id=1, source_target_pairs={{0,8},{1,9},{2,10},{3,11},{4,12},{5,13},{6,14},{7,15},{8,24},{9,25... | collective-permute-start | bytes 835592 | tf_op jit(solution)/shard_map/ppermute | solution.py:164
  20.0 8.9 %collective-permute-start.5 = (bf16[64,2176]{1,0:T(8,128)(2,1)S(1)}, bf16[64,2176]{1,0:T(8,128)(2,1)S(1)}, u32[]{:S(2)}, u32[]{:S(2)}) collective-permute-start(bf16[64,2176]{1,0:T(8,128)(2,1)S(1)} %collective-permute-done.2), channel_id=1, source_target_pairs={{0,4},{1,5},{2,3},{3,2},{4,0},{5,1},{6,7},{7,6},{8,12},{9,13},{10,... | collective-permute-start | bytes 835592 | tf_op jit(solution)/shard_map/ppermute | solution.py:164
  22.5 6.5 %collective-permute-start.4 = (bf16[128,2176]{1,0:T(8,128)(2,1)S(1)}, bf16[128,2176]{1,0:T(8,128)(2,1)S(1)}, u32[]{:S(2)}, u32[]{:S(2)}) collective-permute-start(bf16[128,2176]{1,0:T(8,128)(2,1)S(1)} %pad_maximum_fusion.own_a), channel_id=1, source_target_pairs={{0,2},{1,3},{2,0},{3,1},{4,6},{5,7},{6,4},{7,5},{8,10},{9,11},{10,... | collective-permute-start | bytes 1671176 | tf_op jit(solution)/shard_map/ppermute | solution.py:164
  22.6 12.6 %collective-permute-start.3 = (bf16[128,2176]{1,0:T(8,128)(2,1)S(1)}, bf16[128,2176]{1,0:T(8,128)(2,1)S(1)}, u32[]{:S(2)}, u32[]{:S(2)}) collective-permute-start(bf16[128,2176]{1,0:T(8,128)(2,1)S(1)} %pad_maximum_fusion.own_a), channel_id=1, source_target_pairs={{0,1},{1,0},{2,6},{3,7},{4,5},{5,4},{6,2},{7,3},{8,9},{9,8},{10,14... | collective-permute-start | bytes 1671176 | tf_op jit(solution)/shard_map/ppermute | solution.py:164
  27.1 9.6 %collective-permute-start.12 = (bf16[64,2176]{1,0:T(8,128)(2,1)S(1)}, bf16[64,2176]{1,0:T(8,128)(2,1)S(1)}, u32[]{:S(2)}, u32[]{:S(2)}) collective-permute-start(bf16[64,2176]{1,0:T(8,128)(2,1)S(1)} %collective-permute-done.6), channel_id=1, source_target_pairs={{0,4},{1,5},{2,3},{3,2},{4,0},{5,1},{6,7},{7,6},{8,12},{9,13},{10,... | collective-permute-start | bytes 835592 | tf_op jit(solution)/shard_map/ppermute | solution.py:164
  28.2 7.4 %collective-permute-start.8 = (bf16[64,2176]{1,0:T(8,128)(2,1)S(1)}, bf16[64,2176]{1,0:T(8,128)(2,1)S(1)}, u32[]{:S(2)}, u32[]{:S(2)}) collective-permute-start(bf16[64,2176]{1,0:T(8,128)(2,1)S(1)} %collective-permute-done.6), channel_id=1, source_target_pairs={{0,8},{1,9},{2,10},{3,11},{4,12},{5,13},{6,14},{7,15},{8,24},{9,25... | collective-permute-start | bytes 835592 | tf_op jit(solution)/shard_map/ppermute | solution.py:164
  29.0 8.5 %collective-permute-start.16 = (bf16[128,2176]{1,0:T(8,128)(2,1)S(1)}, bf16[128,2176]{1,0:T(8,128)(2,1)S(1)}, u32[]{:S(2)}, u32[]{:S(2)}) collective-permute-start(bf16[128,2176]{1,0:T(8,128)(2,1)S(1)} %pad_maximum_fusion.1.own_a), channel_id=1, source_target_pairs={{0,2},{1,3},{2,0},{3,1},{4,6},{5,7},{6,4},{7,5},{8,10},{9,11},{10,... | collective-permute-start | bytes 1671176 | tf_op jit(solution)/shard_map/ppermute | solution.py:164
  29.9 11.4 %collective-permute-start.15 = (bf16[128,2176]{1,0:T(8,128)(2,1)S(1)}, bf16[128,2176]{1,0:T(8,128)(2,1)}, u32[]{:S(2)}, u32[]{:S(2)}) collective-permute-start(bf16[128,2176]{1,0:T(8,128)(2,1)S(1)} %pad_maximum_fusion.1.own_a), channel_id=1, source_target_pairs={{0,1},{1,0},{2,6},{3,7},{4,5},{5,4},{6,2},{7,3},{8,9},{9,8},{10,14... | collective-permute-start | bytes 1671176 | tf_op jit(solution)/shard_map/ppermute | solution.py:164
  35.2 6.1 %copy-start.8 = (bf16[128,2176]{1,0:T(8,128)(2,1)}, bf16[128,2176]{1,0:T(8,128)(2,1)S(1)}, u32[]{:S(2)}) copy-start(bf16[128,2176]{1,0:T(8,128)(2,1)S(1)} %collective-permute-done.3.own_b) | copy-start | bytes 1671172
  35.6 5.9 %copy-start.12 = (bf16[64,2176]{1,0:T(8,128)(2,1)}, bf16[64,2176]{1,0:T(8,128)(2,1)S(1)}, u32[]{:S(2)}) copy-start(bf16[64,2176]{1,0:T(8,128)(2,1)S(1)} %collective-permute-done.8) | copy-start | bytes 835588
  37.5 0.8 copy-start.10
  41.3 3.3 %collective-permute-start.17 = (bf16[128,2176]{1,0:T(8,128)(2,1)}, bf16[128,2176]{1,0:T(8,128)(2,1)}, u32[]{:S(2)}, u32[]{:S(2)}) collective-permute-start(bf16[128,2176]{1,0:T(8,128)(2,1)} %collective-permute-done.15.own_b), channel_id=1, source_target_pairs={{0,2},{1,3},{2,0},{3,1},{4,6},{5,7},{6,4},{7,5},{8,10},{9,11},{10,... | collective-permute-start | bytes 1671176 | tf_op jit(solution)/shard_map/ppermute | solution.py:164
  41.4 14.4 %collective-permute-start.14 = (bf16[128,2176]{1,0:T(8,128)(2,1)}, bf16[128,2176]{1,0:T(8,128)(2,1)}, u32[]{:S(2)}, u32[]{:S(2)}) collective-permute-start(bf16[128,2176]{1,0:T(8,128)(2,1)} %pad_maximum_fusion.2.own_a), channel_id=1, source_target_pairs={{0,2},{1,3},{2,0},{3,1},{4,6},{5,7},{6,4},{7,5},{8,10},{9,11},{10,... | collective-permute-start | bytes 1671176 | tf_op jit(solution)/shard_map/ppermute | solution.py:164
  41.8 14.0 %collective-permute-start.13 = (bf16[128,2176]{1,0:T(8,128)(2,1)}, bf16[128,2176]{1,0:T(8,128)(2,1)}, u32[]{:S(2)}, u32[]{:S(2)}) collective-permute-start(bf16[128,2176]{1,0:T(8,128)(2,1)} %pad_maximum_fusion.2.own_a), channel_id=1, source_target_pairs={{0,1},{1,0},{2,6},{3,7},{4,5},{5,4},{6,2},{7,3},{8,9},{9,8},{10,14... | collective-permute-start | bytes 1671176 | tf_op jit(solution)/shard_map/ppermute | solution.py:164
  43.2 13.2 %collective-permute-start.9 = (bf16[64,2176]{1,0:T(8,128)(2,1)}, bf16[64,2176]{1,0:T(8,128)(2,1)S(1)}, u32[]{:S(2)}, u32[]{:S(2)}) collective-permute-start(bf16[64,2176]{1,0:T(8,128)(2,1)} %copy-done.12), channel_id=1, source_target_pairs={{0,4},{1,5},{2,3},{3,2},{4,0},{5,1},{6,7},{7,6},{8,12},{9,13},{10,... | collective-permute-start | bytes 835592 | tf_op jit(solution)/shard_map/ppermute | solution.py:164
  44.5 1.8 %copy-start.1 = (bf16[1,704,2048]{2,1,0:T(8,128)(2,1)S(1)}, bf16[1,704,2048]{2,1,0:T(8,128)(2,1)}, u32[]{:S(2)}) copy-start(bf16[1,704,2048]{2,1,0:T(8,128)(2,1)} %param.14) | copy-start | bytes 8650756
  46.4 1.8 %copy-start.3 = (bf16[1,704,2048]{2,1,0:T(8,128)(2,1)S(1)}, bf16[1,704,2048]{2,1,0:T(8,128)(2,1)}, u32[]{:S(2)}) copy-start(bf16[1,704,2048]{2,1,0:T(8,128)(2,1)} %param.15) | copy-start | bytes 8650756
  48.2 1.1 copy-start.5
  49.2 1.1 copy-start.11
  50.3 5.5 %copy-start.13 = (bf16[64,2176]{1,0:T(8,128)(2,1)S(1)}, bf16[64,2176]{1,0:T(8,128)(2,1)}, u32[]{:S(2)}) copy-start(bf16[64,2176]{1,0:T(8,128)(2,1)} %copy-done.12) | copy-start | bytes 835588
  50.3 6.9 %copy-start.9 = (bf16[128,2176]{1,0:T(8,128)(2,1)S(1)}, bf16[128,2176]{1,0:T(8,128)(2,1)}, u32[]{:S(2)}) copy-start(bf16[128,2176]{1,0:T(8,128)(2,1)} %copy-done.8) | copy-start | bytes 1671172
  55.7 10.4 %collective-permute-start.21 = (bf16[256,2048]{1,0:T(8,128)(2,1)S(1)}, bf16[256,2048]{1,0:T(8,128)(2,1)S(1)}, u32[]{:S(2)}, u32[]{:S(2)}) collective-permute-start(bf16[256,2048]{1,0:T(8,128)(2,1)S(1)} %get-tuple-element.75), channel_id=1, source_target_pairs={{0,2},{1,3},{2,0},{3,1},{4,6},{5,7},{6,4},{7,5},{8,10},{9,11},{10,... | collective-permute-start | bytes 3145736 | tf_op jit(solution)/shard_map/ppermute | solution.py:164
  55.8 4.3 %collective-permute-start.18 = (bf16[128,2176]{1,0:T(8,128)(2,1)}, bf16[128,2176]{1,0:T(8,128)(2,1)S(1)}, u32[]{:S(2)}, u32[]{:S(2)}) collective-permute-start(bf16[128,2176]{1,0:T(8,128)(2,1)} %collective-permute-done.13.own_b), channel_id=1, source_target_pairs={{0,2},{1,3},{2,0},{3,1},{4,6},{5,7},{6,4},{7,5},{8,10},{9,11},{10,... | collective-permute-start | bytes 1671176 | tf_op jit(solution)/shard_map/ppermute | solution.py:164
  56.4 9.3 %collective-permute-start.11 = (bf16[128,2176]{1,0:T(8,128)(2,1)S(1)}, bf16[128,2176]{1,0:T(8,128)(2,1)S(1)}, u32[]{:S(2)}, u32[]{:S(2)}) collective-permute-start(bf16[128,2176]{1,0:T(8,128)(2,1)S(1)} %constant_dynamic-update-slice_fusion.own_a), channel_id=1, source_target_pairs={{0,2},{1,3},{2,0},{3,1},{4,6},{5,7},{6,4},{7,5},{8,10},{9,11},{10,... | collective-permute-start | bytes 1671176 | tf_op jit(solution)/shard_map/ppermute | solution.py:164
  56.5 9.6 %collective-permute-start.10 = (bf16[128,2176]{1,0:T(8,128)(2,1)S(1)}, bf16[128,2176]{1,0:T(8,128)(2,1)S(1)}, u32[]{:S(2)}, u32[]{:S(2)}) collective-permute-start(bf16[128,2176]{1,0:T(8,128)(2,1)S(1)} %constant_dynamic-update-slice_fusion.own_a), channel_id=1, source_target_pairs={{0,1},{1,0},{2,6},{3,7},{4,5},{5,4},{6,2},{7,3},{8,9},{9,8},{10,14... | collective-permute-start | bytes 1671176 | tf_op jit(solution)/shard_map/ppermute | solution.py:164
  57.2 16.3 %collective-permute-start.7 = (bf16[128,2176]{1,0:T(8,128)(2,1)S(1)}, bf16[128,2176]{1,0:T(8,128)(2,1)S(1)}, u32[]{:S(2)}, u32[]{:S(2)}) collective-permute-start(bf16[128,2176]{1,0:T(8,128)(2,1)S(1)} %copy-done.9), channel_id=1, source_target_pairs={{0,2},{1,3},{2,0},{3,1},{4,6},{5,7},{6,4},{7,5},{8,10},{9,11},{10,... | collective-permute-start | bytes 1671176 | tf_op jit(solution)/shard_map/ppermute | solution.py:164
  65.4 3.5 %copy-start.2 = (bf16[1,704,2048]{2,1,0:T(8,128)(2,1)S(1)}, bf16[1,704,2048]{2,1,0:T(8,128)(2,1)}, u32[]{:S(2)}) copy-start(bf16[1,704,2048]{2,1,0:T(8,128)(2,1)} %param.14) | copy-start | bytes 8650756
  65.5 11.3 %collective-permute-start.27 = (bf16[256,2048]{1,0:T(8,128)(2,1)S(1)}, bf16[256,2048]{1,0:T(8,128)(2,1)S(1)}, u32[]{:S(2)}, u32[]{:S(2)}) collective-permute-start(bf16[256,2048]{1,0:T(8,128)(2,1)S(1)} %get-tuple-element.85), channel_id=1, source_target_pairs={{0,2},{1,3},{2,0},{3,1},{4,6},{5,7},{6,4},{7,5},{8,10},{9,11},{10,... | collective-permute-start | bytes 3145736 | tf_op jit(solution)/shard_map/ppermute | solution.py:164
  66.1 2.9 %collective-permute-start.19 = (bf16[128,2176]{1,0:T(8,128)(2,1)S(1)}, bf16[128,2176]{1,0:T(8,128)(2,1)S(1)}, u32[]{:S(2)}, u32[]{:S(2)}) collective-permute-start(bf16[128,2176]{1,0:T(8,128)(2,1)S(1)} %collective-permute-done.10.own_b), channel_id=1, source_target_pairs={{0,2},{1,3},{2,0},{3,1},{4,6},{5,7},{6,4},{7,5},{8,10},{9,11},{10,... | collective-permute-start | bytes 1671176 | tf_op jit(solution)/shard_map/ppermute | solution.py:164
  66.5 9.2 %collective-permute-start.22 = (bf16[128,2048]{1,0:T(8,128)(2,1)S(1)}, bf16[128,2048]{1,0:T(8,128)(2,1)S(1)}, u32[]{:S(2)}, u32[]{:S(2)}) collective-permute-start(bf16[128,2048]{1,0:T(8,128)(2,1)S(1)} %slice.65), channel_id=1, source_target_pairs={{0,1},{1,0},{2,6},{3,7},{4,5},{5,4},{6,2},{7,3},{8,9},{9,8},{10,14... | collective-permute-start | bytes 1572872 | tf_op jit(solution)/shard_map/ppermute | solution.py:164
  73.3 14.8 %collective-permute-start.31 = (bf16[256,2048]{1,0:T(8,128)(2,1)S(1)}, bf16[256,2048]{1,0:T(8,128)(2,1)S(1)}, u32[]{:S(2)}, u32[]{:S(2)}) collective-permute-start(bf16[256,2048]{1,0:T(8,128)(2,1)S(1)} %get-tuple-element.95), channel_id=1, source_target_pairs={{0,2},{1,3},{2,0},{3,1},{4,6},{5,7},{6,4},{7,5},{8,10},{9,11},{10,... | collective-permute-start | bytes 3145736 | tf_op jit(solution)/shard_map/ppermute | solution.py:164
  75.9 2.7 %copy-start.7 = (bf16[128,2176]{1,0:T(8,128)(2,1)S(1)}, bf16[128,2176]{1,0:T(8,128)(2,1)}, u32[]{:S(2)}) copy-start(bf16[128,2176]{1,0:T(8,128)(2,1)} %copy-done.6) | copy-start | bytes 1671172
  76.0 9.2 %collective-permute-start.23 = (bf16[64,2048]{1,0:T(8,128)(2,1)S(1)}, bf16[64,2048]{1,0:T(8,128)(2,1)S(1)}, u32[]{:S(2)}, u32[]{:S(2)}) collective-permute-start(bf16[64,2048]{1,0:T(8,128)(2,1)S(1)} %slice.67), channel_id=1, source_target_pairs={{0,4},{1,5},{2,3},{3,2},{4,0},{5,1},{6,7},{7,6},{8,12},{9,13},{10,... | collective-permute-start | bytes 786440 | tf_op jit(solution)/shard_map/ppermute | solution.py:164
  77.2 10.1 %collective-permute-start.28 = (bf16[128,2048]{1,0:T(8,128)(2,1)S(1)}, bf16[128,2048]{1,0:T(8,128)(2,1)S(1)}, u32[]{:S(2)}, u32[]{:S(2)}) collective-permute-start(bf16[128,2048]{1,0:T(8,128)(2,1)S(1)} %slice.69), channel_id=1, source_target_pairs={{0,1},{1,0},{2,6},{3,7},{4,5},{5,4},{6,2},{7,3},{8,9},{9,8},{10,14... | collective-permute-start | bytes 1572872 | tf_op jit(solution)/shard_map/ppermute | solution.py:164
  83.1 7.0 %collective-permute-start.20 = (bf16[256,2048]{1,0:T(8,128)(2,1)S(1)}, bf16[256,2048]{1,0:T(8,128)(2,1)S(1)}, u32[]{:S(2)}, u32[]{:S(2)}) collective-permute-start(bf16[256,2048]{1,0:T(8,128)(2,1)S(1)} %get-tuple-element.103), channel_id=1, source_target_pairs={{0,2},{1,3},{2,0},{3,1},{4,6},{5,7},{6,4},{7,5},{8,10},{9,11},{10,... | collective-permute-start | bytes 3145736 | tf_op jit(solution)/shard_map/ppermute | solution.py:164
  85.2 26.1 %collective-permute-start.26 = (bf16[64,2048]{1,0:T(8,128)(2,1)S(1)}, bf16[64,2048]{1,0:T(8,128)(2,1)S(1)}, u32[]{:S(2)}, u32[]{:S(2)}) collective-permute-start(bf16[64,2048]{1,0:T(8,128)(2,1)S(1)} %add_convert_fusion.11), channel_id=1, source_target_pairs={{0,16},{1,17},{2,18},{3,19},{4,20},{5,21},{6,22},{7,23},{8,0},{9,1... | collective-permute-start | bytes 786440 | tf_op jit(solution)/shard_map/ppermute | solution.py:164
  87.4 8.9 %collective-permute-start.29 = (bf16[64,2048]{1,0:T(8,128)(2,1)S(1)}, bf16[64,2048]{1,0:T(8,128)(2,1)S(1)}, u32[]{:S(2)}, u32[]{:S(2)}) collective-permute-start(bf16[64,2048]{1,0:T(8,128)(2,1)S(1)} %slice.71), channel_id=1, source_target_pairs={{0,4},{1,5},{2,3},{3,2},{4,0},{5,1},{6,7},{7,6},{8,12},{9,13},{10,... | collective-permute-start | bytes 786440 | tf_op jit(solution)/shard_map/ppermute | solution.py:164
  88.5 11.9 %collective-permute-start.32 = (bf16[128,2048]{1,0:T(8,128)(2,1)S(1)}, bf16[128,2048]{1,0:T(8,128)(2,1)S(1)}, u32[]{:S(2)}, u32[]{:S(2)}) collective-permute-start(bf16[128,2048]{1,0:T(8,128)(2,1)S(1)} %slice.73), channel_id=1, source_target_pairs={{0,1},{1,0},{2,6},{3,7},{4,5},{5,4},{6,2},{7,3},{8,9},{9,8},{10,14... | collective-permute-start | bytes 1572872 | tf_op jit(solution)/shard_map/ppermute | solution.py:164
  90.6 15.4 %collective-permute-start.24 = (bf16[128,2048]{1,0:T(8,128)(2,1)S(1)}, bf16[128,2048]{1,0:T(8,128)(2,1)S(1)}, u32[]{:S(2)}, u32[]{:S(2)}) collective-permute-start(bf16[128,2048]{1,0:T(8,128)(2,1)S(1)} %slice.53), channel_id=1, source_target_pairs={{0,1},{1,0},{2,6},{3,7},{4,5},{5,4},{6,2},{7,3},{8,9},{9,8},{10,14... | collective-permute-start | bytes 1572872 | tf_op jit(solution)/shard_map/ppermute | solution.py:164
  96.3 14.9 %collective-permute-start.30 = (bf16[64,2048]{1,0:T(8,128)(2,1)S(1)}, bf16[64,2048]{1,0:T(8,128)(2,1)S(1)}, u32[]{:S(2)}, u32[]{:S(2)}) collective-permute-start(bf16[64,2048]{1,0:T(8,128)(2,1)S(1)} %add_convert_fusion.10), channel_id=1, source_target_pairs={{0,24},{1,25},{2,26},{3,27},{4,28},{5,29},{6,30},{7,31},{8,16},{9,... | collective-permute-start | bytes 786440 | tf_op jit(solution)/shard_map/ppermute | solution.py:164
  100.5 16.5 %copy-start.14 = (bf16[64,2048]{1,0:T(8,128)(2,1)S(1)}, bf16[64,2048]{1,0:T(8,128)(2,1)}, u32[]{:S(2)}) copy-start(bf16[64,2048]{1,0:T(8,128)(2,1)} %get-tuple-element.56) | copy-start | bytes 786436
  100.5 7.5 %collective-permute-start.33 = (bf16[64,2048]{1,0:T(8,128)(2,1)S(1)}, bf16[64,2048]{1,0:T(8,128)(2,1)S(1)}, u32[]{:S(2)}, u32[]{:S(2)}) collective-permute-start(bf16[64,2048]{1,0:T(8,128)(2,1)S(1)} %slice.75), channel_id=1, source_target_pairs={{0,4},{1,5},{2,3},{3,2},{4,0},{5,1},{6,7},{7,6},{8,12},{9,13},{10,... | collective-permute-start | bytes 786440 | tf_op jit(solution)/shard_map/ppermute | solution.py:164
  106.2 6.4 %collective-permute-start.25 = (bf16[64,2048]{1,0:T(8,128)(2,1)S(1)}, bf16[64,2048]{1,0:T(8,128)(2,1)S(1)}, u32[]{:S(2)}, u32[]{:S(2)}) collective-permute-start(bf16[64,2048]{1,0:T(8,128)(2,1)S(1)} %slice.55), channel_id=1, source_target_pairs={{0,4},{1,5},{2,3},{3,2},{4,0},{5,1},{6,7},{7,6},{8,12},{9,13},{10,... | collective-permute-start | bytes 786440 | tf_op jit(solution)/shard_map/ppermute | solution.py:164
  108.1 8.9 %collective-permute-start.34 = (bf16[64,2048]{1,0:T(8,128)(2,1)S(1)}, bf16[64,2048]{1,0:T(8,128)(2,1)S(1)}, u32[]{:S(2)}, u32[]{:S(2)}) collective-permute-start(bf16[64,2048]{1,0:T(8,128)(2,1)S(1)} %add_convert_fusion.9), channel_id=1, source_target_pairs={{0,8},{1,9},{2,10},{3,11},{4,12},{5,13},{6,14},{7,15},{8,24},{9,25... | collective-permute-start | bytes 786440 | tf_op jit(solution)/shard_map/ppermute | solution.py:164
  (3 other events, 2.3 us)

commit v6 on v5

--- a/solution.py
+++ b/solution.py
@@ -231,7 +231,7 @@
         (spread, 1, True),
         (widen, 0, True),
         (spread, 2, True),
-        (widen, 1, True),
+        (widen, 1, False),
         (share, 0, True),
         (spread, 3, True),
         (widen, 2, True),
@@ -242,9 +242,9 @@
         (run, 2, True),
         (share, 3, True),
         (run, 3, True),
-        (run, 0, True),
         (merge_cores, 1, False),
         (merge_second, 1, False),
+        (run, 0, True),
         (merge_cores, 2, False),
         (merge_second, 2, False),
         (merge_first, 2, False),

time: 118 us -> 118 us (level)
  waiting for transfers between devices: 41.9 us -> 37.9 us
  starting transfers between devices: 36 us -> 37.6 us
  local copies, waits for them, and re-layouts: 13.1 us -> 14.6 us
    ppermute x35, waiting for transfers between devices: 41.9 us -> 37.9 us  [routes(): return lambda a: lax.ppermute(a, AXES, pairs)]
    ppermute x35, starting transfers between devices: 36 us -> 37.6 us  [routes(): return lambda a: lax.ppermute(a, AXES, pairs)]
    unnamed x35 -> x36, local copies, waits for them, and re-layouts: 11.9 us -> 13.4 us
  transfers between devices with their start and end apart: 35 -> 35, of which waited for: 16 -> 16; matrix products, arithmetic and copies ran while one was open for 6% -> 6% of each run, Pallas kernels for 16% -> 17%
where the time goes in v6:
time: 118 us; the launch traced here: 117 us
  waiting for transfers between devices  37.9 us (32%)
  starting transfers between devices  37.6 us (32%)
  Pallas kernels  21.6 us (18%)
  local copies, waits for them, and re-layouts  14.6 us (12%)
  other arithmetic  5.03 us (4%)
    ppermute x35, waiting for transfers between devices, routes(): return lambda a: lax.ppermute(a, AXES, pairs)  37.9 us
    ppermute x35, starting transfers between devices, routes(): return lambda a: lax.ppermute(a, AXES, pairs)  37.6 us
    pallas_call x4, Pallas kernels, experts(): pl.pallas_call(expert_kernel, out_shape=(result, result), in_specs=[SMEM]...  19.4 us
    unnamed x36, local copies, waits for them, and re-layouts  13.4 us
  transfers between devices with their start and end apart: 35, of which 16 were waited for; matrix products, arithmetic and copies ran while one was open for 6% of the time, Pallas kernels for 17%

profile of v6, /device:TPU:0, one launch (start us, length us, event | category | flops | bytes accessed | tf_op | source)
XLA Modules:
  0.0 117.1 jit_solution(17622547132048271542)
XLA Ops:
  0.0 0.9 constant_dynamic-slice_fusion
  0.9 3.0 %collective-permute-start = (bf16[64,1024]{1,0:T(8,128)(2,1)S(1)}, bf16[64,1024]{1,0:T(8,128)(2,1)S(1)}, u32[]{:S(2)}, u32[]{:S(2)}) collective-permute-start(bf16[64,1024]{1,0:T(8,128)(2,1)S(1)} %constant_dynamic-slice_fusion), channel_id=1, source_target_pairs={{0,1},{1,0},{2,3},{3,2},{4,5},{5,4},{6,7},{7,6},{8,9},{9,8},{10,11... | collective-permute-start | bytes 393224 | tf_op jit(solution)/shard_map/ppermute | solution.py:164
  3.9 1.4 %copy.9.ids_ref = s32[128,6]{1,0:T(8,128)} copy(s32[128,6]{0,1:T(8,128)} %param.11) | data formatting | bytes 6144 | tf_op args[3]
  5.4 1.6 %copy.10.gates_ref = f32[128,6]{1,0:T(8,128)} copy(f32[128,6]{0,1:T(8,128)} %param.12) | data formatting | bytes 6144 | tf_op args[4]
  8.1 2.2 %shard_map.82 = (bf16[64,2176]{1,0:T(8,128)(2,1)}, bf16[64,2048]{1,0:T(8,128)(2,1)}) custom-call(s32[1]{0:T(128)} %bitcast.half_ref, bf16[128,1024]{1,0:T(8,128)(2,1)} %attn_ref.1, bf16[64,1024]{1,0:T(8,128)(2,1)} %copy-done.15, bf16[64,2048]{1,0:T(8,128)(2,1)} %resid_ref.1, f32[1,2048]{1,0:T(1,128)} %bitcast.18, s32[128,6]{1,0:T(8,128)} %copy.9.ids_ref, ...), custom_call_target="tpu_custom_call" | custom-call | tf_op jit(solution)/shard_map/pallas_call | solution.py:77
  10.3 1.8 %collective-permute-start.2 = (bf16[64,2176]{1,0:T(8,128)(2,1)}, bf16[64,2176]{1,0:T(8,128)(2,1)S(1)}, u32[]{:S(2)}, u32[]{:S(2)}) collective-permute-start(bf16[64,2176]{1,0:T(8,128)(2,1)} %get-tuple-element.56), channel_id=1, source_target_pairs={{0,8},{1,9},{2,10},{3,11},{4,12},{5,13},{6,14},{7,15},{8,24},{9,25... | collective-permute-start | bytes 835592 | tf_op jit(solution)/shard_map/ppermute | solution.py:164
  12.1 1.5 %collective-permute-start.1 = (bf16[64,2176]{1,0:T(8,128)(2,1)}, bf16[64,2176]{1,0:T(8,128)(2,1)S(1)}, u32[]{:S(2)}, u32[]{:S(2)}) collective-permute-start(bf16[64,2176]{1,0:T(8,128)(2,1)} %get-tuple-element.56), channel_id=1, source_target_pairs={{0,4},{1,5},{2,3},{3,2},{4,0},{5,1},{6,7},{7,6},{8,12},{9,13},{10,... | collective-permute-start | bytes 835592 | tf_op jit(solution)/shard_map/ppermute | solution.py:164
  13.6 5.7 %collective-permute-done.2 = bf16[64,2176]{1,0:T(8,128)(2,1)S(1)} collective-permute-done((bf16[64,2176]{1,0:T(8,128)(2,1)}, bf16[64,2176]{1,0:T(8,128)(2,1)S(1)}, u32[]{:S(2)}, u32[]{:S(2)}) %collective-permute-start.2) | collective-permute-done | bytes 278560 | tf_op jit(solution)/shard_map/ppermute | solution.py:164
  19.3 1.4 %collective-permute-start.14 = (bf16[64,2176]{1,0:T(8,128)(2,1)S(1)}, bf16[64,2176]{1,0:T(8,128)(2,1)S(1)}, u32[]{:S(2)}, u32[]{:S(2)}) collective-permute-start(bf16[64,2176]{1,0:T(8,128)(2,1)S(1)} %collective-permute-done.2), channel_id=1, source_target_pairs={{0,4},{1,5},{2,3},{3,2},{4,0},{5,1},{6,7},{7,6},{8,12},{9,13},{10,... | collective-permute-start | bytes 835592 | tf_op jit(solution)/shard_map/ppermute | solution.py:164
  20.6 0.9 collective-permute-start.5
  21.5 1.0 pad_maximum_fusion.own_a
  22.6 1.6 %collective-permute-start.3 = (bf16[128,2176]{1,0:T(8,128)(2,1)S(1)}, bf16[128,2176]{1,0:T(8,128)(2,1)S(1)}, u32[]{:S(2)}, u32[]{:S(2)}) collective-permute-start(bf16[128,2176]{1,0:T(8,128)(2,1)S(1)} %pad_maximum_fusion.own_a), channel_id=1, source_target_pairs={{0,1},{1,0},{2,6},{3,7},{4,5},{5,4},{6,2},{7,3},{8,9},{9,8},{10,14... | collective-permute-start | bytes 1671176 | tf_op jit(solution)/shard_map/ppermute | solution.py:164
  24.2 3.9 %collective-permute-done.5 = bf16[64,2176]{1,0:T(8,128)(2,1)S(1)} collective-permute-done((bf16[64,2176]{1,0:T(8,128)(2,1)S(1)}, bf16[64,2176]{1,0:T(8,128)(2,1)S(1)}, u32[]{:S(2)}, u32[]{:S(2)}) %collective-permute-start.5) | collective-permute-done | bytes 278560 | tf_op jit(solution)/shard_map/ppermute | solution.py:164
  28.1 1.3 %collective-permute-start.11 = (bf16[64,2176]{1,0:T(8,128)(2,1)S(1)}, bf16[64,2176]{1,0:T(8,128)(2,1)S(1)}, u32[]{:S(2)}, u32[]{:S(2)}) collective-permute-start(bf16[64,2176]{1,0:T(8,128)(2,1)S(1)} %collective-permute-done.5), channel_id=1, source_target_pairs={{0,4},{1,5},{2,3},{3,2},{4,0},{5,1},{6,7},{7,6},{8,12},{9,13},{10,... | collective-permute-start | bytes 835592 | tf_op jit(solution)/shard_map/ppermute | solution.py:164
  31.9 0.8 copy-done.4
  32.7 2.5 %collective-permute-done.3.own_b = bf16[128,2176]{1,0:T(8,128)(2,1)S(1)} collective-permute-done((bf16[128,2176]{1,0:T(8,128)(2,1)S(1)}, bf16[128,2176]{1,0:T(8,128)(2,1)S(1)}, u32[]{:S(2)}, u32[]{:S(2)}) %collective-permute-start.3) | collective-permute-done | bytes 557088 | tf_op jit(solution)/shard_map/ppermute | solution.py:164
  35.2 0.8 copy-done.8
  36.0 0.8 collective-permute-done.7
  37.6 0.8 pad_maximum_fusion.1.own_a
  38.4 0.8 copy-done.10
  39.2 2.0 %collective-permute-done.15.own_b = bf16[128,2176]{1,0:T(8,128)(2,1)} collective-permute-done((bf16[128,2176]{1,0:T(8,128)(2,1)S(1)}, bf16[128,2176]{1,0:T(8,128)(2,1)}, u32[]{:S(2)}, u32[]{:S(2)}) %collective-permute-start.15) | collective-permute-done | bytes 557088 | tf_op jit(solution)/shard_map/ppermute | solution.py:164
  41.8 1.5 %collective-permute-start.12 = (bf16[128,2176]{1,0:T(8,128)(2,1)}, bf16[128,2176]{1,0:T(8,128)(2,1)}, u32[]{:S(2)}, u32[]{:S(2)}) collective-permute-start(bf16[128,2176]{1,0:T(8,128)(2,1)} %pad_maximum_fusion.1.own_a), channel_id=1, source_target_pairs={{0,1},{1,0},{2,6},{3,7},{4,5},{5,4},{6,2},{7,3},{8,9},{9,8},{10,14... | collective-permute-start | bytes 1671176 | tf_op jit(solution)/shard_map/ppermute | solution.py:164
  43.9 1.8 %copy-done.1 = bf16[1,704,2048]{2,1,0:T(8,128)(2,1)S(1)} copy-done((bf16[1,704,2048]{2,1,0:T(8,128)(2,1)S(1)}, bf16[1,704,2048]{2,1,0:T(8,128)(2,1)}, u32[]{:S(2)}) %copy-start.1) | copy-done | bytes 2883608
  45.7 1.8 %copy-done.3 = bf16[1,704,2048]{2,1,0:T(8,128)(2,1)S(1)} copy-done((bf16[1,704,2048]{2,1,0:T(8,128)(2,1)S(1)}, bf16[1,704,2048]{2,1,0:T(8,128)(2,1)}, u32[]{:S(2)}) %copy-start.3) | copy-done | bytes 2883608
  47.5 1.1 copy-done.5
  48.5 1.1 copy-done.11
  49.6 5.4 %shard_map.83 = (bf16[256,2048]{1,0:T(8,128)(2,1)S(1)}, bf16[256,2048]{1,0:T(8,128)(2,1)S(1)}) custom-call(s32[1]{0:T(128)} %bitcast.2.me_ref, bf16[128,2176]{1,0:T(8,128)(2,1)S(1)} %copy-done.5, bf16[128,2176]{1,0:T(8,128)(2,1)} %collective-permute-done.15.own_b, bf16[128,2176]{1,0:T(8,128)(2,1)S(1)} %copy-done.11, ...), custom_call_target="tpu_custom_call" | custom-call | flops 2214592512 | bytes 4194304 | tf_op jit(solution)/shard_map/pallas_call | solution.py:134
  55.8 1.4 %collective-permute-start.9 = (bf16[128,2176]{1,0:T(8,128)(2,1)S(1)}, bf16[128,2176]{1,0:T(8,128)(2,1)S(1)}, u32[]{:S(2)}, u32[]{:S(2)}) collective-permute-start(bf16[128,2176]{1,0:T(8,128)(2,1)S(1)} %constant_dynamic-update-slice_fusion.own_a), channel_id=1, source_target_pairs={{0,1},{1,0},{2,6},{3,7},{4,5},{5,4},{6,2},{7,3},{8,9},{9,8},{10,14... | collective-permute-start | bytes 1671176 | tf_op jit(solution)/shard_map/ppermute | solution.py:164
  57.5 1.9 %collective-permute-done.18.sib_b = bf16[128,2176]{1,0:T(8,128)(2,1)S(1)} collective-permute-done((bf16[128,2176]{1,0:T(8,128)(2,1)}, bf16[128,2176]{1,0:T(8,128)(2,1)S(1)}, u32[]{:S(2)}, u32[]{:S(2)}) %collective-permute-start.18) | collective-permute-done | bytes 557088 | tf_op jit(solution)/shard_map/ppermute | solution.py:164
  59.4 5.3 %shard_map.84 = (bf16[256,2048]{1,0:T(8,128)(2,1)S(1)}, bf16[256,2048]{1,0:T(8,128)(2,1)S(1)}) custom-call(s32[1]{0:T(128)} %bitcast.2.me_ref, bf16[128,2176]{1,0:T(8,128)(2,1)} %pad_maximum_fusion.1.own_a, bf16[128,2176]{1,0:T(8,128)(2,1)} %collective-permute-done.12.own_b, bf16[128,2176]{1,0:T(8,128)(2,1)} %collective-permute-done.13.sib_a, ...), custom_call_target="tpu_custom_call" | custom-call | flops 2214592512 | bytes 4194304 | tf_op jit(solution)/shard_map/pallas_call | solution.py:134
  65.8 1.4 %collective-permute-start.22 = (bf16[128,2048]{1,0:T(8,128)(2,1)S(1)}, bf16[128,2048]{1,0:T(8,128)(2,1)S(1)}, u32[]{:S(2)}, u32[]{:S(2)}) collective-permute-start(bf16[128,2048]{1,0:T(8,128)(2,1)S(1)} %slice.65), channel_id=1, source_target_pairs={{0,1},{1,0},{2,6},{3,7},{4,5},{5,4},{6,2},{7,3},{8,9},{9,8},{10,14... | collective-permute-start | bytes 1572872 | tf_op jit(solution)/shard_map/ppermute | solution.py:164
  67.2 1.1 collective-permute-done.19.sib_b
  68.3 4.3 %shard_map.85 = (bf16[256,2048]{1,0:T(8,128)(2,1)S(1)}, bf16[256,2048]{1,0:T(8,128)(2,1)S(1)}) custom-call(s32[1]{0:T(128)} %bitcast.2.me_ref, bf16[128,2176]{1,0:T(8,128)(2,1)S(1)} %constant_dynamic-update-slice_fusion.own_a, bf16[128,2176]{1,0:T(8,128)(2,1)S(1)} %collective-permute-done.9.own_b, bf16[128,2176]{1,0:T(8,128)(2,1)S(1)} %collective-permute-done.10.sib_a, ...), custom_call_target="tpu_custom_call" | custom-call | flops 2214592512 | bytes 4194304 | tf_op jit(solution)/shard_map/pallas_call | solution.py:134
  72.8 2.3 %collective-permute-done.22 = bf16[128,2048]{1,0:T(8,128)(2,1)S(1)} collective-permute-done((bf16[128,2048]{1,0:T(8,128)(2,1)S(1)}, bf16[128,2048]{1,0:T(8,128)(2,1)S(1)}, u32[]{:S(2)}, u32[]{:S(2)}) %collective-permute-start.22) | collective-permute-done | bytes 524320 | tf_op jit(solution)/shard_map/ppermute | solution.py:164
  75.3 1.6 %collective-permute-start.23 = (bf16[64,2048]{1,0:T(8,128)(2,1)S(1)}, bf16[64,2048]{1,0:T(8,128)(2,1)S(1)}, u32[]{:S(2)}, u32[]{:S(2)}) collective-permute-start(bf16[64,2048]{1,0:T(8,128)(2,1)S(1)} %slice.67), channel_id=1, source_target_pairs={{0,4},{1,5},{2,3},{3,2},{4,0},{5,1},{6,7},{7,6},{8,12},{9,13},{10,... | collective-permute-start | bytes 786440 | tf_op jit(solution)/shard_map/ppermute | solution.py:164
  77.8 4.4 %shard_map.86 = (bf16[256,2048]{1,0:T(8,128)(2,1)S(1)}, bf16[256,2048]{1,0:T(8,128)(2,1)S(1)}) custom-call(s32[1]{0:T(128)} %bitcast.2.me_ref, bf16[128,2176]{1,0:T(8,128)(2,1)S(1)} %pad_maximum_fusion.own_a, bf16[128,2176]{1,0:T(8,128)(2,1)S(1)} %copy-done.9, bf16[128,2176]{1,0:T(8,128)(2,1)S(1)} %copy-done.7, ...), custom_call_target="tpu_custom_call" | custom-call | flops 2214592512 | bytes 4194304 | tf_op jit(solution)/shard_map/pallas_call | solution.py:134
  82.4 1.9 %collective-permute-done.23 = bf16[64,2048]{1,0:T(8,128)(2,1)S(1)} collective-permute-done((bf16[64,2048]{1,0:T(8,128)(2,1)S(1)}, bf16[64,2048]{1,0:T(8,128)(2,1)S(1)}, u32[]{:S(2)}, u32[]{:S(2)}) %collective-permute-start.23) | collective-permute-done | bytes 262176 | tf_op jit(solution)/shard_map/ppermute | solution.py:164
  84.3 2.3 %collective-permute-start.26 = (bf16[64,2048]{1,0:T(8,128)(2,1)S(1)}, bf16[64,2048]{1,0:T(8,128)(2,1)S(1)}, u32[]{:S(2)}, u32[]{:S(2)}) collective-permute-start(bf16[64,2048]{1,0:T(8,128)(2,1)S(1)} %add_convert_fusion.11), channel_id=1, source_target_pairs={{0,16},{1,17},{2,18},{3,19},{4,20},{5,21},{6,22},{7,23},{8,0},{9,1... | collective-permute-start | bytes 786440 | tf_op jit(solution)/shard_map/ppermute | solution.py:164
  86.8 1.4 %collective-permute-start.29 = (bf16[64,2048]{1,0:T(8,128)(2,1)S(1)}, bf16[64,2048]{1,0:T(8,128)(2,1)S(1)}, u32[]{:S(2)}, u32[]{:S(2)}) collective-permute-start(bf16[64,2048]{1,0:T(8,128)(2,1)S(1)} %slice.71), channel_id=1, source_target_pairs={{0,4},{1,5},{2,3},{3,2},{4,0},{5,1},{6,7},{7,6},{8,12},{9,13},{10,... | collective-permute-start | bytes 786440 | tf_op jit(solution)/shard_map/ppermute | solution.py:164
  89.5 1.7 %collective-permute-start.24 = (bf16[128,2048]{1,0:T(8,128)(2,1)S(1)}, bf16[128,2048]{1,0:T(8,128)(2,1)S(1)}, u32[]{:S(2)}, u32[]{:S(2)}) collective-permute-start(bf16[128,2048]{1,0:T(8,128)(2,1)S(1)} %slice.53), channel_id=1, source_target_pairs={{0,1},{1,0},{2,6},{3,7},{4,5},{5,4},{6,2},{7,3},{8,9},{9,8},{10,14... | collective-permute-start | bytes 1572872 | tf_op jit(solution)/shard_map/ppermute | solution.py:164
  91.2 4.1 %collective-permute-done.29 = bf16[64,2048]{1,0:T(8,128)(2,1)S(1)} collective-permute-done((bf16[64,2048]{1,0:T(8,128)(2,1)S(1)}, bf16[64,2048]{1,0:T(8,128)(2,1)S(1)}, u32[]{:S(2)}, u32[]{:S(2)}) %collective-permute-start.29) | collective-permute-done | bytes 262176 | tf_op jit(solution)/shard_map/ppermute | solution.py:164
  95.4 4.2 %collective-permute-start.30 = (bf16[64,2048]{1,0:T(8,128)(2,1)S(1)}, bf16[64,2048]{1,0:T(8,128)(2,1)S(1)}, u32[]{:S(2)}, u32[]{:S(2)}) collective-permute-start(bf16[64,2048]{1,0:T(8,128)(2,1)S(1)} %add_convert_fusion.10), channel_id=1, source_target_pairs={{0,24},{1,25},{2,26},{3,27},{4,28},{5,29},{6,30},{7,31},{8,16},{9,... | collective-permute-start | bytes 786440 | tf_op jit(solution)/shard_map/ppermute | solution.py:164
  99.7 1.5 %collective-permute-start.33 = (bf16[64,2048]{1,0:T(8,128)(2,1)S(1)}, bf16[64,2048]{1,0:T(8,128)(2,1)S(1)}, u32[]{:S(2)}, u32[]{:S(2)}) collective-permute-start(bf16[64,2048]{1,0:T(8,128)(2,1)S(1)} %slice.75), channel_id=1, source_target_pairs={{0,4},{1,5},{2,3},{3,2},{4,0},{5,1},{6,7},{7,6},{8,12},{9,13},{10,... | collective-permute-start | bytes 786440 | tf_op jit(solution)/shard_map/ppermute | solution.py:164
  101.2 4.9 %collective-permute-done.24 = bf16[128,2048]{1,0:T(8,128)(2,1)S(1)} collective-permute-done((bf16[128,2048]{1,0:T(8,128)(2,1)S(1)}, bf16[128,2048]{1,0:T(8,128)(2,1)S(1)}, u32[]{:S(2)}, u32[]{:S(2)}) %collective-permute-start.24) | collective-permute-done | bytes 524320 | tf_op jit(solution)/shard_map/ppermute | solution.py:164
  107.3 3.3 %collective-permute-start.34 = (bf16[64,2048]{1,0:T(8,128)(2,1)S(1)}, bf16[64,2048]{1,0:T(8,128)(2,1)S(1)}, u32[]{:S(2)}, u32[]{:S(2)}) collective-permute-start(bf16[64,2048]{1,0:T(8,128)(2,1)S(1)} %add_convert_fusion.9), channel_id=1, source_target_pairs={{0,8},{1,9},{2,10},{3,11},{4,12},{5,13},{6,14},{7,15},{8,24},{9,25... | collective-permute-start | bytes 786440 | tf_op jit(solution)/shard_map/ppermute | solution.py:164
  110.7 2.1 %collective-permute-done.25 = bf16[64,2048]{1,0:T(8,128)(2,1)S(1)} collective-permute-done((bf16[64,2048]{1,0:T(8,128)(2,1)S(1)}, bf16[64,2048]{1,0:T(8,128)(2,1)S(1)}, u32[]{:S(2)}, u32[]{:S(2)}) %collective-permute-start.25) | collective-permute-done | bytes 262176 | tf_op jit(solution)/shard_map/ppermute | solution.py:164
  112.8 3.4 %collective-permute-done.34 = bf16[64,2048]{1,0:T(8,128)(2,1)S(1)} collective-permute-done((bf16[64,2048]{1,0:T(8,128)(2,1)S(1)}, bf16[64,2048]{1,0:T(8,128)(2,1)S(1)}, u32[]{:S(2)}, u32[]{:S(2)}) %collective-permute-start.34) | collective-permute-done | bytes 262176 | tf_op jit(solution)/shard_map/ppermute | solution.py:164
  116.2 0.9 add_convert_fusion.8
  (88 shorter events, 12.0 us)
Async XLA Ops:
  0.9 6.5 %collective-permute-start = (bf16[64,1024]{1,0:T(8,128)(2,1)S(1)}, bf16[64,1024]{1,0:T(8,128)(2,1)S(1)}, u32[]{:S(2)}, u32[]{:S(2)}) collective-permute-start(bf16[64,1024]{1,0:T(8,128)(2,1)S(1)} %constant_dynamic-slice_fusion), channel_id=1, source_target_pairs={{0,1},{1,0},{2,3},{3,2},{4,5},{5,4},{6,7},{7,6},{8,9},{9,8},{10,11... | collective-permute-start | bytes 393224 | tf_op jit(solution)/shard_map/ppermute | solution.py:164
  5.4 38.5 %copy-start = (bf16[1,704,2048]{2,1,0:T(8,128)(2,1)S(1)}, bf16[1,704,2048]{2,1,0:T(8,128)(2,1)}, u32[]{:S(2)}) copy-start(bf16[1,704,2048]{2,1,0:T(8,128)(2,1)} %param.13) | copy-start | bytes 8650756
  10.3 9.0 %collective-permute-start.2 = (bf16[64,2176]{1,0:T(8,128)(2,1)}, bf16[64,2176]{1,0:T(8,128)(2,1)S(1)}, u32[]{:S(2)}, u32[]{:S(2)}) collective-permute-start(bf16[64,2176]{1,0:T(8,128)(2,1)} %get-tuple-element.56), channel_id=1, source_target_pairs={{0,8},{1,9},{2,10},{3,11},{4,12},{5,13},{6,14},{7,15},{8,24},{9,25... | collective-permute-start | bytes 835592 | tf_op jit(solution)/shard_map/ppermute | solution.py:164
  12.1 9.4 %collective-permute-start.1 = (bf16[64,2176]{1,0:T(8,128)(2,1)}, bf16[64,2176]{1,0:T(8,128)(2,1)S(1)}, u32[]{:S(2)}, u32[]{:S(2)}) collective-permute-start(bf16[64,2176]{1,0:T(8,128)(2,1)} %get-tuple-element.56), channel_id=1, source_target_pairs={{0,4},{1,5},{2,3},{3,2},{4,0},{5,1},{6,7},{7,6},{8,12},{9,13},{10,... | collective-permute-start | bytes 835592 | tf_op jit(solution)/shard_map/ppermute | solution.py:164
  19.3 10.9 %collective-permute-start.14 = (bf16[64,2176]{1,0:T(8,128)(2,1)S(1)}, bf16[64,2176]{1,0:T(8,128)(2,1)S(1)}, u32[]{:S(2)}, u32[]{:S(2)}) collective-permute-start(bf16[64,2176]{1,0:T(8,128)(2,1)S(1)} %collective-permute-done.2), channel_id=1, source_target_pairs={{0,4},{1,5},{2,3},{3,2},{4,0},{5,1},{6,7},{7,6},{8,12},{9,13},{10,... | collective-permute-start | bytes 835592 | tf_op jit(solution)/shard_map/ppermute | solution.py:164
  20.6 7.4 %collective-permute-start.5 = (bf16[64,2176]{1,0:T(8,128)(2,1)S(1)}, bf16[64,2176]{1,0:T(8,128)(2,1)S(1)}, u32[]{:S(2)}, u32[]{:S(2)}) collective-permute-start(bf16[64,2176]{1,0:T(8,128)(2,1)S(1)} %collective-permute-done.2), channel_id=1, source_target_pairs={{0,8},{1,9},{2,10},{3,11},{4,12},{5,13},{6,14},{7,15},{8,24},{9,25... | collective-permute-start | bytes 835592 | tf_op jit(solution)/shard_map/ppermute | solution.py:164
  22.5 7.7 %collective-permute-start.4 = (bf16[128,2176]{1,0:T(8,128)(2,1)S(1)}, bf16[128,2176]{1,0:T(8,128)(2,1)S(1)}, u32[]{:S(2)}, u32[]{:S(2)}) collective-permute-start(bf16[128,2176]{1,0:T(8,128)(2,1)S(1)} %pad_maximum_fusion.own_a), channel_id=1, source_target_pairs={{0,2},{1,3},{2,0},{3,1},{4,6},{5,7},{6,4},{7,5},{8,10},{9,11},{10,... | collective-permute-start | bytes 1671176 | tf_op jit(solution)/shard_map/ppermute | solution.py:164
  22.6 12.6 %collective-permute-start.3 = (bf16[128,2176]{1,0:T(8,128)(2,1)S(1)}, bf16[128,2176]{1,0:T(8,128)(2,1)S(1)}, u32[]{:S(2)}, u32[]{:S(2)}) collective-permute-start(bf16[128,2176]{1,0:T(8,128)(2,1)S(1)} %pad_maximum_fusion.own_a), channel_id=1, source_target_pairs={{0,1},{1,0},{2,6},{3,7},{4,5},{5,4},{6,2},{7,3},{8,9},{9,8},{10,14... | collective-permute-start | bytes 1671176 | tf_op jit(solution)/shard_map/ppermute | solution.py:164
  28.1 9.5 %collective-permute-start.11 = (bf16[64,2176]{1,0:T(8,128)(2,1)S(1)}, bf16[64,2176]{1,0:T(8,128)(2,1)S(1)}, u32[]{:S(2)}, u32[]{:S(2)}) collective-permute-start(bf16[64,2176]{1,0:T(8,128)(2,1)S(1)} %collective-permute-done.5), channel_id=1, source_target_pairs={{0,4},{1,5},{2,3},{3,2},{4,0},{5,1},{6,7},{7,6},{8,12},{9,13},{10,... | collective-permute-start | bytes 835592 | tf_op jit(solution)/shard_map/ppermute | solution.py:164
  29.4 7.4 %collective-permute-start.7 = (bf16[64,2176]{1,0:T(8,128)(2,1)S(1)}, bf16[64,2176]{1,0:T(8,128)(2,1)S(1)}, u32[]{:S(2)}, u32[]{:S(2)}) collective-permute-start(bf16[64,2176]{1,0:T(8,128)(2,1)S(1)} %collective-permute-done.5), channel_id=1, source_target_pairs={{0,8},{1,9},{2,10},{3,11},{4,12},{5,13},{6,14},{7,15},{8,24},{9,25... | collective-permute-start | bytes 835592 | tf_op jit(solution)/shard_map/ppermute | solution.py:164
  30.2 8.2 %collective-permute-start.16 = (bf16[128,2176]{1,0:T(8,128)(2,1)S(1)}, bf16[128,2176]{1,0:T(8,128)(2,1)S(1)}, u32[]{:S(2)}, u32[]{:S(2)}) collective-permute-start(bf16[128,2176]{1,0:T(8,128)(2,1)S(1)} %constant_dynamic-update-slice_fusion.2.own_a), channel_id=1, source_target_pairs={{0,2},{1,3},{2,0},{3,1},{4,6},{5,7},{6,4},{7,5},{8,10},{9,11},{10,... | collective-permute-start | bytes 1671176 | tf_op jit(solution)/shard_map/ppermute | solution.py:164
  31.1 10.2 %collective-permute-start.15 = (bf16[128,2176]{1,0:T(8,128)(2,1)S(1)}, bf16[128,2176]{1,0:T(8,128)(2,1)}, u32[]{:S(2)}, u32[]{:S(2)}) collective-permute-start(bf16[128,2176]{1,0:T(8,128)(2,1)S(1)} %constant_dynamic-update-slice_fusion.2.own_a), channel_id=1, source_target_pairs={{0,1},{1,0},{2,6},{3,7},{4,5},{5,4},{6,2},{7,3},{8,9},{9,8},{10,14... | collective-permute-start | bytes 1671176 | tf_op jit(solution)/shard_map/ppermute | solution.py:164
  31.9 0.8 copy-start.4
  35.2 0.8 copy-start.8
  38.4 0.8 copy-start.10
  41.3 2.6 %collective-permute-start.17 = (bf16[128,2176]{1,0:T(8,128)(2,1)}, bf16[128,2176]{1,0:T(8,128)(2,1)}, u32[]{:S(2)}, u32[]{:S(2)}) collective-permute-start(bf16[128,2176]{1,0:T(8,128)(2,1)} %collective-permute-done.15.own_b), channel_id=1, source_target_pairs={{0,2},{1,3},{2,0},{3,1},{4,6},{5,7},{6,4},{7,5},{8,10},{9,11},{10,... | collective-permute-start | bytes 1671176 | tf_op jit(solution)/shard_map/ppermute | solution.py:164
  41.3 13.8 %collective-permute-start.13 = (bf16[128,2176]{1,0:T(8,128)(2,1)}, bf16[128,2176]{1,0:T(8,128)(2,1)}, u32[]{:S(2)}, u32[]{:S(2)}) collective-permute-start(bf16[128,2176]{1,0:T(8,128)(2,1)} %pad_maximum_fusion.1.own_a), channel_id=1, source_target_pairs={{0,2},{1,3},{2,0},{3,1},{4,6},{5,7},{6,4},{7,5},{8,10},{9,11},{10,... | collective-permute-start | bytes 1671176 | tf_op jit(solution)/shard_map/ppermute | solution.py:164
  41.8 13.3 %collective-permute-start.12 = (bf16[128,2176]{1,0:T(8,128)(2,1)}, bf16[128,2176]{1,0:T(8,128)(2,1)}, u32[]{:S(2)}, u32[]{:S(2)}) collective-permute-start(bf16[128,2176]{1,0:T(8,128)(2,1)} %pad_maximum_fusion.1.own_a), channel_id=1, source_target_pairs={{0,1},{1,0},{2,6},{3,7},{4,5},{5,4},{6,2},{7,3},{8,9},{9,8},{10,14... | collective-permute-start | bytes 1671176 | tf_op jit(solution)/shard_map/ppermute | solution.py:164
  43.3 12.4 %collective-permute-start.8 = (bf16[64,2176]{1,0:T(8,128)(2,1)}, bf16[64,2176]{1,0:T(8,128)(2,1)S(1)}, u32[]{:S(2)}, u32[]{:S(2)}) collective-permute-start(bf16[64,2176]{1,0:T(8,128)(2,1)} %copy-done.12), channel_id=1, source_target_pairs={{0,4},{1,5},{2,3},{3,2},{4,0},{5,1},{6,7},{7,6},{8,12},{9,13},{10,... | collective-permute-start | bytes 835592 | tf_op jit(solution)/shard_map/ppermute | solution.py:164
  43.8 1.8 %copy-start.1 = (bf16[1,704,2048]{2,1,0:T(8,128)(2,1)S(1)}, bf16[1,704,2048]{2,1,0:T(8,128)(2,1)}, u32[]{:S(2)}) copy-start(bf16[1,704,2048]{2,1,0:T(8,128)(2,1)} %param.14) | copy-start | bytes 8650756
  45.7 1.8 %copy-start.3 = (bf16[1,704,2048]{2,1,0:T(8,128)(2,1)S(1)}, bf16[1,704,2048]{2,1,0:T(8,128)(2,1)}, u32[]{:S(2)}) copy-start(bf16[1,704,2048]{2,1,0:T(8,128)(2,1)} %param.15) | copy-start | bytes 8650756
  47.5 1.1 copy-start.5
  48.5 1.1 copy-start.11
  49.6 5.5 %copy-start.13 = (bf16[64,2176]{1,0:T(8,128)(2,1)S(1)}, bf16[64,2176]{1,0:T(8,128)(2,1)}, u32[]{:S(2)}) copy-start(bf16[64,2176]{1,0:T(8,128)(2,1)} %copy-done.12) | copy-start | bytes 835588
  49.6 7.6 %copy-start.9 = (bf16[128,2176]{1,0:T(8,128)(2,1)S(1)}, bf16[128,2176]{1,0:T(8,128)(2,1)}, u32[]{:S(2)}) copy-start(bf16[128,2176]{1,0:T(8,128)(2,1)} %copy-done.8) | copy-start | bytes 1671172
  55.0 10.4 %collective-permute-start.21 = (bf16[256,2048]{1,0:T(8,128)(2,1)S(1)}, bf16[256,2048]{1,0:T(8,128)(2,1)S(1)}, u32[]{:S(2)}, u32[]{:S(2)}) collective-permute-start(bf16[256,2048]{1,0:T(8,128)(2,1)S(1)} %get-tuple-element.73), channel_id=1, source_target_pairs={{0,2},{1,3},{2,0},{3,1},{4,6},{5,7},{6,4},{7,5},{8,10},{9,11},{10,... | collective-permute-start | bytes 3145736 | tf_op jit(solution)/shard_map/ppermute | solution.py:164
  55.1 4.3 %collective-permute-start.18 = (bf16[128,2176]{1,0:T(8,128)(2,1)}, bf16[128,2176]{1,0:T(8,128)(2,1)S(1)}, u32[]{:S(2)}, u32[]{:S(2)}) collective-permute-start(bf16[128,2176]{1,0:T(8,128)(2,1)} %collective-permute-done.12.own_b), channel_id=1, source_target_pairs={{0,2},{1,3},{2,0},{3,1},{4,6},{5,7},{6,4},{7,5},{8,10},{9,11},{10,... | collective-permute-start | bytes 1671176 | tf_op jit(solution)/shard_map/ppermute | solution.py:164
  55.7 9.3 %collective-permute-start.10 = (bf16[128,2176]{1,0:T(8,128)(2,1)S(1)}, bf16[128,2176]{1,0:T(8,128)(2,1)S(1)}, u32[]{:S(2)}, u32[]{:S(2)}) collective-permute-start(bf16[128,2176]{1,0:T(8,128)(2,1)S(1)} %constant_dynamic-update-slice_fusion.own_a), channel_id=1, source_target_pairs={{0,2},{1,3},{2,0},{3,1},{4,6},{5,7},{6,4},{7,5},{8,10},{9,11},{10,... | collective-permute-start | bytes 1671176 | tf_op jit(solution)/shard_map/ppermute | solution.py:164
  55.8 9.6 %collective-permute-start.9 = (bf16[128,2176]{1,0:T(8,128)(2,1)S(1)}, bf16[128,2176]{1,0:T(8,128)(2,1)S(1)}, u32[]{:S(2)}, u32[]{:S(2)}) collective-permute-start(bf16[128,2176]{1,0:T(8,128)(2,1)S(1)} %constant_dynamic-update-slice_fusion.own_a), channel_id=1, source_target_pairs={{0,1},{1,0},{2,6},{3,7},{4,5},{5,4},{6,2},{7,3},{8,9},{9,8},{10,14... | collective-permute-start | bytes 1671176 | tf_op jit(solution)/shard_map/ppermute | solution.py:164
  57.2 15.6 %collective-permute-start.6 = (bf16[128,2176]{1,0:T(8,128)(2,1)S(1)}, bf16[128,2176]{1,0:T(8,128)(2,1)S(1)}, u32[]{:S(2)}, u32[]{:S(2)}) collective-permute-start(bf16[128,2176]{1,0:T(8,128)(2,1)S(1)} %copy-done.9), channel_id=1, source_target_pairs={{0,2},{1,3},{2,0},{3,1},{4,6},{5,7},{6,4},{7,5},{8,10},{9,11},{10,... | collective-permute-start | bytes 1671176 | tf_op jit(solution)/shard_map/ppermute | solution.py:164
  64.7 3.5 %copy-start.2 = (bf16[1,704,2048]{2,1,0:T(8,128)(2,1)S(1)}, bf16[1,704,2048]{2,1,0:T(8,128)(2,1)}, u32[]{:S(2)}) copy-start(bf16[1,704,2048]{2,1,0:T(8,128)(2,1)} %param.14) | copy-start | bytes 8650756
  64.8 12.1 %collective-permute-start.27 = (bf16[256,2048]{1,0:T(8,128)(2,1)S(1)}, bf16[256,2048]{1,0:T(8,128)(2,1)S(1)}, u32[]{:S(2)}, u32[]{:S(2)}) collective-permute-start(bf16[256,2048]{1,0:T(8,128)(2,1)S(1)} %get-tuple-element.83), channel_id=1, source_target_pairs={{0,2},{1,3},{2,0},{3,1},{4,6},{5,7},{6,4},{7,5},{8,10},{9,11},{10,... | collective-permute-start | bytes 3145736 | tf_op jit(solution)/shard_map/ppermute | solution.py:164
  65.4 2.9 %collective-permute-start.19 = (bf16[128,2176]{1,0:T(8,128)(2,1)S(1)}, bf16[128,2176]{1,0:T(8,128)(2,1)S(1)}, u32[]{:S(2)}, u32[]{:S(2)}) collective-permute-start(bf16[128,2176]{1,0:T(8,128)(2,1)S(1)} %collective-permute-done.9.own_b), channel_id=1, source_target_pairs={{0,2},{1,3},{2,0},{3,1},{4,6},{5,7},{6,4},{7,5},{8,10},{9,11},{10,... | collective-permute-start | bytes 1671176 | tf_op jit(solution)/shard_map/ppermute | solution.py:164
  65.8 9.2 %collective-permute-start.22 = (bf16[128,2048]{1,0:T(8,128)(2,1)S(1)}, bf16[128,2048]{1,0:T(8,128)(2,1)S(1)}, u32[]{:S(2)}, u32[]{:S(2)}) collective-permute-start(bf16[128,2048]{1,0:T(8,128)(2,1)S(1)} %slice.65), channel_id=1, source_target_pairs={{0,1},{1,0},{2,6},{3,7},{4,5},{5,4},{6,2},{7,3},{8,9},{9,8},{10,14... | collective-permute-start | bytes 1572872 | tf_op jit(solution)/shard_map/ppermute | solution.py:164
  72.6 15.6 %collective-permute-start.31 = (bf16[256,2048]{1,0:T(8,128)(2,1)S(1)}, bf16[256,2048]{1,0:T(8,128)(2,1)S(1)}, u32[]{:S(2)}, u32[]{:S(2)}) collective-permute-start(bf16[256,2048]{1,0:T(8,128)(2,1)S(1)} %get-tuple-element.93), channel_id=1, source_target_pairs={{0,2},{1,3},{2,0},{3,1},{4,6},{5,7},{6,4},{7,5},{8,10},{9,11},{10,... | collective-permute-start | bytes 3145736 | tf_op jit(solution)/shard_map/ppermute | solution.py:164
  75.2 2.6 %copy-start.7 = (bf16[128,2176]{1,0:T(8,128)(2,1)S(1)}, bf16[128,2176]{1,0:T(8,128)(2,1)}, u32[]{:S(2)}) copy-start(bf16[128,2176]{1,0:T(8,128)(2,1)} %copy-done.6) | copy-start | bytes 1671172
  75.3 9.0 %collective-permute-start.23 = (bf16[64,2048]{1,0:T(8,128)(2,1)S(1)}, bf16[64,2048]{1,0:T(8,128)(2,1)S(1)}, u32[]{:S(2)}, u32[]{:S(2)}) collective-permute-start(bf16[64,2048]{1,0:T(8,128)(2,1)S(1)} %slice.67), channel_id=1, source_target_pairs={{0,4},{1,5},{2,3},{3,2},{4,0},{5,1},{6,7},{7,6},{8,12},{9,13},{10,... | collective-permute-start | bytes 786440 | tf_op jit(solution)/shard_map/ppermute | solution.py:164
  77.3 9.3 %collective-permute-start.28 = (bf16[128,2048]{1,0:T(8,128)(2,1)S(1)}, bf16[128,2048]{1,0:T(8,128)(2,1)S(1)}, u32[]{:S(2)}, u32[]{:S(2)}) collective-permute-start(bf16[128,2048]{1,0:T(8,128)(2,1)S(1)} %slice.69), channel_id=1, source_target_pairs={{0,1},{1,0},{2,6},{3,7},{4,5},{5,4},{6,2},{7,3},{8,9},{9,8},{10,14... | collective-permute-start | bytes 1572872 | tf_op jit(solution)/shard_map/ppermute | solution.py:164
  82.3 6.8 %collective-permute-start.20 = (bf16[256,2048]{1,0:T(8,128)(2,1)S(1)}, bf16[256,2048]{1,0:T(8,128)(2,1)S(1)}, u32[]{:S(2)}, u32[]{:S(2)}) collective-permute-start(bf16[256,2048]{1,0:T(8,128)(2,1)S(1)} %get-tuple-element.101), channel_id=1, source_target_pairs={{0,2},{1,3},{2,0},{3,1},{4,6},{5,7},{6,4},{7,5},{8,10},{9,11},{10,... | collective-permute-start | bytes 3145736 | tf_op jit(solution)/shard_map/ppermute | solution.py:164
  84.3 26.3 %collective-permute-start.26 = (bf16[64,2048]{1,0:T(8,128)(2,1)S(1)}, bf16[64,2048]{1,0:T(8,128)(2,1)S(1)}, u32[]{:S(2)}, u32[]{:S(2)}) collective-permute-start(bf16[64,2048]{1,0:T(8,128)(2,1)S(1)} %add_convert_fusion.11), channel_id=1, source_target_pairs={{0,16},{1,17},{2,18},{3,19},{4,20},{5,21},{6,22},{7,23},{8,0},{9,1... | collective-permute-start | bytes 786440 | tf_op jit(solution)/shard_map/ppermute | solution.py:164
  86.8 8.5 %collective-permute-start.29 = (bf16[64,2048]{1,0:T(8,128)(2,1)S(1)}, bf16[64,2048]{1,0:T(8,128)(2,1)S(1)}, u32[]{:S(2)}, u32[]{:S(2)}) collective-permute-start(bf16[64,2048]{1,0:T(8,128)(2,1)S(1)} %slice.71), channel_id=1, source_target_pairs={{0,4},{1,5},{2,3},{3,2},{4,0},{5,1},{6,7},{7,6},{8,12},{9,13},{10,... | collective-permute-start | bytes 786440 | tf_op jit(solution)/shard_map/ppermute | solution.py:164
  88.6 10.9 %collective-permute-start.32 = (bf16[128,2048]{1,0:T(8,128)(2,1)S(1)}, bf16[128,2048]{1,0:T(8,128)(2,1)S(1)}, u32[]{:S(2)}, u32[]{:S(2)}) collective-permute-start(bf16[128,2048]{1,0:T(8,128)(2,1)S(1)} %slice.73), channel_id=1, source_target_pairs={{0,1},{1,0},{2,6},{3,7},{4,5},{5,4},{6,2},{7,3},{8,9},{9,8},{10,14... | collective-permute-start | bytes 1572872 | tf_op jit(solution)/shard_map/ppermute | solution.py:164
  89.5 16.6 %collective-permute-start.24 = (bf16[128,2048]{1,0:T(8,128)(2,1)S(1)}, bf16[128,2048]{1,0:T(8,128)(2,1)S(1)}, u32[]{:S(2)}, u32[]{:S(2)}) collective-permute-start(bf16[128,2048]{1,0:T(8,128)(2,1)S(1)} %slice.53), channel_id=1, source_target_pairs={{0,1},{1,0},{2,6},{3,7},{4,5},{5,4},{6,2},{7,3},{8,9},{9,8},{10,14... | collective-permute-start | bytes 1572872 | tf_op jit(solution)/shard_map/ppermute | solution.py:164
  95.4 15.3 %collective-permute-start.30 = (bf16[64,2048]{1,0:T(8,128)(2,1)S(1)}, bf16[64,2048]{1,0:T(8,128)(2,1)S(1)}, u32[]{:S(2)}, u32[]{:S(2)}) collective-permute-start(bf16[64,2048]{1,0:T(8,128)(2,1)S(1)} %add_convert_fusion.10), channel_id=1, source_target_pairs={{0,24},{1,25},{2,26},{3,27},{4,28},{5,29},{6,30},{7,31},{8,16},{9,... | collective-permute-start | bytes 786440 | tf_op jit(solution)/shard_map/ppermute | solution.py:164
  99.7 16.5 %copy-start.14 = (bf16[64,2048]{1,0:T(8,128)(2,1)S(1)}, bf16[64,2048]{1,0:T(8,128)(2,1)}, u32[]{:S(2)}) copy-start(bf16[64,2048]{1,0:T(8,128)(2,1)} %get-tuple-element.55) | copy-start | bytes 786436
  99.7 7.5 %collective-permute-start.33 = (bf16[64,2048]{1,0:T(8,128)(2,1)S(1)}, bf16[64,2048]{1,0:T(8,128)(2,1)S(1)}, u32[]{:S(2)}, u32[]{:S(2)}) collective-permute-start(bf16[64,2048]{1,0:T(8,128)(2,1)S(1)} %slice.75), channel_id=1, source_target_pairs={{0,4},{1,5},{2,3},{3,2},{4,0},{5,1},{6,7},{7,6},{8,12},{9,13},{10,... | collective-permute-start | bytes 786440 | tf_op jit(solution)/shard_map/ppermute | solution.py:164
  106.3 6.4 %collective-permute-start.25 = (bf16[64,2048]{1,0:T(8,128)(2,1)S(1)}, bf16[64,2048]{1,0:T(8,128)(2,1)S(1)}, u32[]{:S(2)}, u32[]{:S(2)}) collective-permute-start(bf16[64,2048]{1,0:T(8,128)(2,1)S(1)} %slice.55), channel_id=1, source_target_pairs={{0,4},{1,5},{2,3},{3,2},{4,0},{5,1},{6,7},{7,6},{8,12},{9,13},{10,... | collective-permute-start | bytes 786440 | tf_op jit(solution)/shard_map/ppermute | solution.py:164
  107.3 8.8 %collective-permute-start.34 = (bf16[64,2048]{1,0:T(8,128)(2,1)S(1)}, bf16[64,2048]{1,0:T(8,128)(2,1)S(1)}, u32[]{:S(2)}, u32[]{:S(2)}) collective-permute-start(bf16[64,2048]{1,0:T(8,128)(2,1)S(1)} %add_convert_fusion.9), channel_id=1, source_target_pairs={{0,8},{1,9},{2,10},{3,11},{4,12},{5,13},{6,14},{7,15},{8,24},{9,25... | collective-permute-start | bytes 786440 | tf_op jit(solution)/shard_map/ppermute | solution.py:164
  (3 other events, 2.2 us)
